TPU v7x, 256 devices: a whole 4x4x8 slice. The times are simulated.
256 devices in a mesh: blk: 64 (over z, x, core), rep: 4 (over y).
Axes of the slice: x: 4, y: 4, z: 8, core: 2. Of those that a mesh axis runs over, the one named last changes fastest.
Arguments:
- samples: bfloat16 [512, 131072], P(None, 'blk'), may hold values from -6 to 6
- theta_tiles: bfloat16 [4096, 256, 256], P(('blk', 'rep')), may hold values from -6 to 6
- theta_diag: float32 [131072], P('blk'), may hold values from 0.5 to 2
- tile_row: int32 [4096], P(('blk', 'rep')), may hold values from 0 to 511, as said below
- tile_col: int32 [4096], P(('blk', 'rep')), may hold values from 0 to 7
- tile_count: int32 [256], P(('blk', 'rep')), may hold values from 4 to 16, as said below
Outputs:
- new_tiles: bfloat16 [4096, 256, 256], P(('blk', 'rep'))
- new_diag: float32 [131072], P('blk')
Inputs may be any that keep to these rules, and one draw needn't show every extreme that they name: tile_row[s] differs from the slot's block column j by 1 to 8, of either sign; pairs may repeat, and repeated tiles add. Each device's live slots are its first tile_count slots; in every blk index some device is full.
All inputs are finite; a program needn't handle non-finite values.
Results may differ from a plain program's by a relative error of at most 0.0035.
Values may be sent and summed in bfloat16 or wider, within the bound.
No kernel may reach another device: no remote copies, remote signals or barrier semaphores. Data moves between devices by JAX's collectives and lax.ppermute only.
A program may use at most 128 MiB of HBM per device.

v0:
```python
import jax
import jax.numpy as jnp
from jax import lax
from jax.sharding import PartitionSpec as P

B = 256


STEP = 0.25
PENALTY = 0.5


def extended(cells, sides, width):
    for axis, dim in sides:
        count = lax.axis_size(axis)
        ends = count - 1
        head = lax.slice_in_dim(cells, 0, width, axis=dim)
        tail = lax.slice_in_dim(cells, cells.shape[dim] - width, cells.shape[dim], axis=dim)
        cells = jnp.concatenate(
            [
                lax.ppermute(tail, axis, [(i, (i + 1) % count) for i in range(ends)]),
                cells,
                lax.ppermute(head, axis, [((i + 1) % count, i) for i in range(ends)]),
            ],
            axis=dim,
        )
    return cells


def shards(samples, theta_tiles, theta_diag, tile_row, tile_col, tile_count):
    count_ns, width = samples.shape
    blocks = width // B
    slots = theta_tiles.shape[0]
    group = lax.axis_index("blk")
    live = jnp.arange(slots, dtype=jnp.int32) < tile_count[0]
    tiles = jnp.where(live[:, None, None], theta_tiles, jnp.zeros_like(theta_tiles))
    rows = tile_row - (group - 1) * blocks
    onehot = (tile_col[:, None] == jnp.arange(blocks, dtype=jnp.int32)[None, :]).astype(jnp.float32)
    ext_x = extended(samples, (("blk", 1),), width)
    ext_x = ext_x.reshape(count_ns, 3 * blocks, B)
    x_row = jnp.take(ext_x, rows, axis=1)
    prod = jnp.einsum("sta,tab->stb", x_row, tiles, preferred_element_type=jnp.float32)
    partial_image = jnp.einsum(
        "stb,tk->skb", prod, onehot, precision=lax.Precision.HIGHEST
    ).reshape(count_ns, width)
    summed = lax.psum(partial_image, "rep")
    image = (summed + samples.astype(jnp.float32) * theta_diag[None, :]).astype(jnp.bfloat16)
    ext_w = extended(image, (("blk", 1),), width)
    own_image = ext_w[:, width : 2 * width]
    ext_w = ext_w.reshape(count_ns, 3 * blocks, B)
    w_row = jnp.take(ext_w, rows, axis=1)
    x_col = jnp.take(samples.reshape(count_ns, blocks, B), tile_col, axis=1)
    w_col = jnp.take(own_image.reshape(count_ns, blocks, B), tile_col, axis=1)
    first = jnp.einsum("sta,stb->tab", x_row, w_col, preferred_element_type=jnp.float32)
    second = jnp.einsum("sta,stb->tab", w_row, x_col, preferred_element_type=jnp.float32)
    grad = (first + second) / (2.0 * count_ns)
    moved = tiles.astype(jnp.float32) - STEP * grad
    soft_value = jnp.sign(moved) * jnp.maximum(jnp.abs(moved) - STEP * PENALTY, 0.0)
    new_tiles = jnp.where(live[:, None, None], soft_value, jnp.zeros_like(soft_value)).astype(
        jnp.bfloat16
    )
    dots = jnp.sum(samples.astype(jnp.float32) * own_image.astype(jnp.float32), axis=0) / count_ns
    new_diag = theta_diag - STEP * (dots - 1.0 / theta_diag)
    return (new_tiles, new_diag)


def solution(mesh):
    placed = (
        P(None, "blk"),
        P(("blk", "rep"), None, None),
        P("blk"),
        P(("blk", "rep")),
        P(("blk", "rep")),
        P(("blk", "rep")),
    )
    return jax.shard_map(
        shards,
        mesh=mesh,
        in_specs=placed,
        out_specs=(P(("blk", "rep"), None, None), P("blk")),
        check_vma=False,
    )
```

profile of v0, /device:TPU:103, one launch (start us, length us, event | category | flops | bytes accessed | tf_op | source)
XLA Modules:
  0.0 273.2 jit_solution(8585177451263751275)
XLA Ops:
  7.2 0.0 copy-start.5
  7.2 0.0 all-reduce.2.cloned.1.call-start
  7.2 2.9 %copy.10 = bf16[512,2048]{0,1:T(8,128)(2,1)S(1)} copy(bf16[512,2048]{1,0:T(8,128)(2,1)} %param.10) | data formatting | bytes 4194304 | tf_op args[0]
  10.1 5.2 %collective-permute-start = (bf16[512,2048]{0,1:T(8,128)(2,1)S(1)}, bf16[512,2048]{0,1:T(8,128)(2,1)}, u32[]{:S(2)}, u32[]{:S(2)}) collective-permute-start(bf16[512,2048]{0,1:T(8,128)(2,1)S(1)} %copy.10), channel_id=1, source_target_pairs={{0,4},{4,8},{8,12},{12,16},{16,20},{20,24},{24,28},{28,32},{32,36}... | collective-permute-start | bytes 6291464 | tf_op jit(solution)/shard_map/ppermute | solution.py:21
  15.3 1.9 collective-permute-start.1
  17.9 0.0 copy-done.5
  18.0 20.3 %collective-permute-done = bf16[512,2048]{0,1:T(8,128)(2,1)} collective-permute-done((bf16[512,2048]{0,1:T(8,128)(2,1)S(1)}, bf16[512,2048]{0,1:T(8,128)(2,1)}, u32[]{:S(2)}, u32[]{:S(2)}) %collective-permute-start) | collective-permute-done | bytes 2097184 | tf_op jit(solution)/shard_map/ppermute | solution.py:21
  38.3 7.8 %collective-permute-done.1 = bf16[512,2048]{0,1:T(8,128)(2,1)} collective-permute-done((bf16[512,2048]{0,1:T(8,128)(2,1)S(1)}, bf16[512,2048]{0,1:T(8,128)(2,1)}, u32[]{:S(2)}, u32[]{:S(2)}) %collective-permute-start.1) | collective-permute-done | bytes 2097184 | tf_op jit(solution)/shard_map/ppermute | solution.py:23
  46.1 5.5 %pad_maximum_fusion = bf16[512,6144]{0,1:T(8,128)(2,1)} fusion(bf16[512,2048]{0,1:T(8,128)(2,1)} %collective-permute-done.1, bf16[512,2048]{0,1:T(8,128)(2,1)S(1)} %copy.10, bf16[512,2048]{0,1:T(8,128)(2,1)} %collective-permute-done), kind=kLoop, calls=%fused_computation.4 | loop fusion | flops 18874368 | bytes 12582912 | tf_op jit(solution)/shard_map/concatenate | solution.py:19
  51.6 8.6 %copy.13 = bf16[512,24,256]{2,0,1:T(8,128)(2,1)} copy(bf16[512,24,256]{0,2,1:T(8,128)(2,1)} %bitcast.37) | data formatting | bytes 12582912 | tf_op jit(solution)/shard_map/reshape | solution.py:40
  60.2 5.5 %gather_fusion = bf16[16,512,256]{2,1,0:T(8,128)(2,1)} fusion(bf16[512,24,256]{2,0,1:T(8,128)(2,1)} %copy.13, s32[1024]{0:T(1024)S(1)} %pad_clamp_fusion.1), kind=kCustom, calls=%fused_computation.clone | custom fusion | bytes 8388672 | tf_op jit(solution)/shard_map/jit(_take)/gather | solution.py:41
  65.8 7.6 %fusion.17 = f32[512,16,256]{0,2,1:T(8,128)} fusion(bf16[16,512,256]{2,1,0:T(8,128)(2,1)} %gather_fusion, pred[16]{0:T(512)(128)(4,1)S(1)} %get-tuple-element.6, bf16[16,256,256]{2,1,0:T(8,128)(2,1)} %param.11, pred[16]{0:T(512)(128)(4,1)S(1)} %get-tuple-element.8), kind=kOutput, calls=%fused_computation.27 | convolution fusion | flops 1076887552 | bytes 14680096 | tf_op jit(solution)/shard_map/sta,tab->stb/dot_general | solution.py:42
  73.3 0.0 copy-start.4
  73.3 10.3 %copy.15 = f32[512,16,256]{2,1,0:T(8,128)} copy(f32[512,16,256]{0,2,1:T(8,128)} %fusion.17) | data formatting | bytes 16777216 | tf_op jit(solution)/shard_map/sta,tab->stb/transpose | solution.py:42
  83.6 0.0 copy-done.4
  83.6 8.4 %convolution_bitcast_fusion = f32[512,8,256]{2,1,0:T(8,128)} fusion(f32[512,16,256]{2,1,0:T(8,128)} %copy.15, s32[16]{0:T(128)S(1)} %copy-done.4), kind=kOutput, calls=%fused_computation.28 | convolution fusion | flops 201326720 | bytes 12582976 | tf_op jit(solution)/shard_map/stb,tk->skb/dot_general | solution.py:43
  92.0 5.3 %copy.27 = f32[512,8,256]{0,2,1:T(8,128)} copy(f32[512,8,256]{2,1,0:T(8,128)} %convolution_bitcast_fusion) | data formatting | bytes 8388608 | tf_op jit(solution)/shard_map/reshape | solution.py:45
  97.3 0.0 copy-start.3
  97.3 0.0 all-reduce.2.cloned.1.call-update
  97.4 96.6 %all-reduce.2.cloned.1.call-done = f32[512,2048]{0,1:T(8,128)} async-done(((f32[512,2048]{0,1:T(8,128)}), f32[512,2048]{0,1:T(8,128)}) %all-reduce.2.cloned.1.call-update) | async-done | bytes 4194320 | tf_op jit(solution)/shard_map/psum | solution.py:46
  193.9 0.0 copy-done.3
  193.9 4.7 %fusion.2 = (f32[2048]{0:T(1024)S(1)}, bf16[512,2048]{0,1:T(8,128)(2,1)}) fusion(bf16[512,2048]{0,1:T(8,128)(2,1)S(1)} %copy.10, f32[512,2048]{0,1:T(8,128)} %all-reduce.2.cloned.1.call-done, f32[2048]{0:T(1024)S(1)} %copy-done.3), kind=kLoop, calls=%fused_computation.10 | loop fusion | flops 7337984 | bytes 8404992 | tf_op jit(solution)/shard_map/reduce_sum | solution.py:62
  198.6 4.9 %collective-permute-start.2 = (bf16[512,2048]{0,1:T(8,128)(2,1)}, bf16[512,2048]{0,1:T(8,128)(2,1)}, u32[]{:S(2)}, u32[]{:S(2)}) collective-permute-start(bf16[512,2048]{0,1:T(8,128)(2,1)} %get-tuple-element.5), channel_id=1, source_target_pairs={{0,4},{4,8},{8,12},{12,16},{16,20},{20,24},{24,28},{28,32},{32,36}... | collective-permute-start | bytes 6291464 | tf_op jit(solution)/shard_map/ppermute | solution.py:21
  203.6 2.1 collective-permute-start.3
  205.7 2.4 copy.22
  208.1 4.4 %gather_fusion.3 = bf16[16,512,256]{2,1,0:T(8,128)(2,1)} fusion(bf16[512,8,256]{2,0,1:T(8,128)(2,1)} %copy.22, s32[1024]{0:T(1024)S(1)} %pad_clamp_fusion), kind=kCustom, calls=%fused_computation.3.clone | custom fusion | bytes 8388672 | tf_op jit(solution)/shard_map/jit(_take)/gather | solution.py:52
  212.5 2.8 %copy.18 = bf16[512,8,256]{2,0,1:T(8,128)(2,1)S(1)} copy(bf16[512,8,256]{0,2,1:T(8,128)(2,1)} %bitcast.7) | data formatting | bytes 4194304 | tf_op jit(solution)/shard_map/reshape | solution.py:53
  215.3 2.7 %gather_fusion.1 = bf16[16,512,256]{2,1,0:T(8,128)(2,1)} fusion(bf16[512,8,256]{2,0,1:T(8,128)(2,1)S(1)} %copy.18, s32[1024]{0:T(1024)S(1)} %pad_clamp_fusion), kind=kCustom, calls=%fused_computation.1.clone | custom fusion | bytes 8388672 | tf_op jit(solution)/shard_map/jit(_take)/gather | solution.py:53
  218.1 0.6 multiply_subtract_fusion
  218.7 8.2 %collective-permute-done.2 = bf16[512,2048]{0,1:T(8,128)(2,1)} collective-permute-done((bf16[512,2048]{0,1:T(8,128)(2,1)}, bf16[512,2048]{0,1:T(8,128)(2,1)}, u32[]{:S(2)}, u32[]{:S(2)}) %collective-permute-start.2) | collective-permute-done | bytes 2097184 | tf_op jit(solution)/shard_map/ppermute | solution.py:21
  226.8 7.7 %collective-permute-done.3 = bf16[512,2048]{0,1:T(8,128)(2,1)} collective-permute-done((bf16[512,2048]{0,1:T(8,128)(2,1)}, bf16[512,2048]{0,1:T(8,128)(2,1)}, u32[]{:S(2)}, u32[]{:S(2)}) %collective-permute-start.3) | collective-permute-done | bytes 2097184 | tf_op jit(solution)/shard_map/ppermute | solution.py:23
  234.6 5.9 %pad_maximum_fusion.1 = bf16[512,6144]{0,1:T(8,128)(2,1)} fusion(bf16[512,2048]{0,1:T(8,128)(2,1)} %collective-permute-done.3, bf16[512,2048]{0,1:T(8,128)(2,1)} %get-tuple-element.5, bf16[512,2048]{0,1:T(8,128)(2,1)} %collective-permute-done.2), kind=kLoop, calls=%fused_computation.5 | loop fusion | flops 18874368 | bytes 12582912 | tf_op jit(solution)/shard_map/concatenate | solution.py:19
  240.5 8.6 %copy.20 = bf16[512,24,256]{2,0,1:T(8,128)(2,1)} copy(bf16[512,24,256]{0,2,1:T(8,128)(2,1)} %bitcast.36) | data formatting | bytes 12582912 | tf_op jit(solution)/shard_map/reshape | solution.py:50
  249.1 5.5 %gather_fusion.2 = bf16[16,512,256]{2,1,0:T(8,128)(2,1)} fusion(bf16[512,24,256]{2,0,1:T(8,128)(2,1)} %copy.20, s32[1024]{0:T(1024)S(1)} %pad_clamp_fusion.1), kind=kCustom, calls=%fused_computation.2.clone | custom fusion | bytes 8388672 | tf_op jit(solution)/shard_map/jit(_take)/gather | solution.py:51
  254.6 0.0 copy-start
  254.6 0.0 copy-start.1
  254.6 0.0 copy-start.2
  254.6 5.2 %fusion.3 = f32[16,256,256]{2,1,0:T(8,128)S(1)} fusion(bf16[16,512,256]{2,1,0:T(8,128)(2,1)} %gather_fusion.3, bf16[16,512,256]{2,1,0:T(8,128)(2,1)} %gather_fusion.2, pred[16]{0:T(512)(128)(4,1)S(1)} %compare_and_fusion, pred[16]{0:T(512)(128)(4,1)S(1)} %get-tuple-element.6), kind=kOutput, calls=%fused_computation.11 | convolution fusion | flops 1077936128 | bytes 12582944 | tf_op jit(solution)/shard_map/sta,stb->tab/dot_general | solution.py:55
  259.9 0.0 copy-done
  259.9 0.7 copy-done.1
  260.6 0.6 copy-done.2
  261.2 5.2 %select_convert_fusion = bf16[16,256,256]{2,1,0:T(8,128)(2,1)} fusion(f32[16,256,256]{2,1,0:T(8,128)S(1)} %fusion.3, pred[16]{0:T(512)(128)(4,1)S(1)} %get-tuple-element.8, bf16[16,512,256]{2,1,0:T(8,128)(2,1)S(1)} %copy-done.1, pred[16]{0:T(512)(128)(4,1)S(1)} %compare_and_fusion, bf16[16,512,256]{2,1,0:T(8,128)(2,1)S(1)} %copy-done, ...), kind=kOutput, calls=%fused_computation.22 | convolution fusion | flops 1090519040 | bytes 16777264 | tf_op jit(solution)/shard_map/sta,stb->tab/dot_general | solution.py:54
  (5 shorter events, 0.0 us)
Async XLA Ops:
  7.2 10.8 %copy-start.5 = (s32[16]{0:T(128)S(1)}, s32[16]{0:T(128)}, u32[]{:S(2)}) copy-start(s32[16]{0:T(128)} %param.13) | copy-start | bytes 196
  7.2 186.8 %all-reduce.2.cloned.1.call-start = ((), (), s32[]{:S(2)}) async-start(), calls=%async_computation | async-start | bytes 8388608 | tf_op jit(solution)/shard_map/psum | solution.py:46
  10.1 28.2 %collective-permute-start = (bf16[512,2048]{0,1:T(8,128)(2,1)S(1)}, bf16[512,2048]{0,1:T(8,128)(2,1)}, u32[]{:S(2)}, u32[]{:S(2)}) collective-permute-start(bf16[512,2048]{0,1:T(8,128)(2,1)S(1)} %copy.10), channel_id=1, source_target_pairs={{0,4},{4,8},{8,12},{12,16},{16,20},{20,24},{24,28},{28,32},{32,36}... | collective-permute-start | bytes 6291464 | tf_op jit(solution)/shard_map/ppermute | solution.py:21
  15.3 30.8 %collective-permute-start.1 = (bf16[512,2048]{0,1:T(8,128)(2,1)S(1)}, bf16[512,2048]{0,1:T(8,128)(2,1)}, u32[]{:S(2)}, u32[]{:S(2)}) collective-permute-start(bf16[512,2048]{0,1:T(8,128)(2,1)S(1)} %copy.10), channel_id=1, source_target_pairs={{4,0},{8,4},{12,8},{16,12},{20,16},{24,20},{28,24},{32,28},{36,32}... | collective-permute-start | bytes 6291464 | tf_op jit(solution)/shard_map/ppermute | solution.py:23
  73.3 10.3 %copy-start.4 = (s32[16]{0:T(128)S(1)}, s32[16]{0:T(128)}, u32[]{:S(2)}) copy-start(s32[16]{0:T(128)} %param.14) | copy-start | bytes 196
  97.3 96.6 %copy-start.3 = (f32[2048]{0:T(1024)S(1)}, f32[2048]{0:T(1024)}, u32[]{:S(2)}) copy-start(f32[2048]{0:T(1024)} %param.12) | copy-start | bytes 24580
  198.6 28.2 %collective-permute-start.2 = (bf16[512,2048]{0,1:T(8,128)(2,1)}, bf16[512,2048]{0,1:T(8,128)(2,1)}, u32[]{:S(2)}, u32[]{:S(2)}) collective-permute-start(bf16[512,2048]{0,1:T(8,128)(2,1)} %get-tuple-element.5), channel_id=1, source_target_pairs={{0,4},{4,8},{8,12},{12,16},{16,20},{20,24},{24,28},{28,32},{32,36}... | collective-permute-start | bytes 6291464 | tf_op jit(solution)/shard_map/ppermute | solution.py:21
  203.6 31.0 %collective-permute-start.3 = (bf16[512,2048]{0,1:T(8,128)(2,1)}, bf16[512,2048]{0,1:T(8,128)(2,1)}, u32[]{:S(2)}, u32[]{:S(2)}) collective-permute-start(bf16[512,2048]{0,1:T(8,128)(2,1)} %get-tuple-element.5), channel_id=1, source_target_pairs={{4,0},{8,4},{12,8},{16,12},{20,16},{24,20},{28,24},{32,28},{36,32}... | collective-permute-start | bytes 6291464 | tf_op jit(solution)/shard_map/ppermute | solution.py:23
  254.6 5.2 %copy-start = (bf16[16,512,256]{2,1,0:T(8,128)(2,1)S(1)}, bf16[16,512,256]{2,1,0:T(8,128)(2,1)}, u32[]{:S(2)}) copy-start(bf16[16,512,256]{2,1,0:T(8,128)(2,1)} %gather_fusion) | copy-start | bytes 12582916
  254.6 5.9 %copy-start.1 = (bf16[16,512,256]{2,1,0:T(8,128)(2,1)S(1)}, bf16[16,512,256]{2,1,0:T(8,128)(2,1)}, u32[]{:S(2)}) copy-start(bf16[16,512,256]{2,1,0:T(8,128)(2,1)} %gather_fusion.1) | copy-start | bytes 12582916
  254.6 6.5 %copy-start.2 = (bf16[16,256,256]{2,1,0:T(8,128)(2,1)S(1)}, bf16[16,256,256]{2,1,0:T(8,128)(2,1)}, u32[]{:S(2)}) copy-start(bf16[16,256,256]{2,1,0:T(8,128)(2,1)} %param.11) | copy-start | bytes 6291460
Sparse Core Ops, SparseCore 0:
  97.5 96.4 all-reduce.1
where the time goes:
time: 275 us; the launch traced here: 273 us
  waiting for transfers between devices  141 us (51%)
  local copies, waits for them, and re-layouts  60.5 us (22%)
  matrix products  26.4 us (10%)
  other arithmetic  16.7 us (6%)
  between operations  14.8 us (5%)
  starting transfers between devices  14.2 us (5%)
    psum x1, waiting for transfers between devices, shards(): summed = lax.psum(partial_image, 'rep')  96.6 us
    ppermute x2, waiting for transfers between devices, extended(): lax.ppermute(tail, axis, [(i, (i + 1) % count) for i in range(ends)])  28.5 us
    ppermute x2, waiting for transfers between devices, extended(): lax.ppermute(head, axis, [((i + 1) % count, i) for i in range(ends)])  15.5 us
    concatenate x2, other arithmetic, extended(): jnp.concatenate([lax.ppermute(tail, axis, [(i, (i + 1) % count) for i in...  11.4 us
    transpose x1, local copies, waits for them, and re-layouts, shards(): jnp.einsum('sta,tab->stb', x_row, tiles, preferred_element_type=jnp.float32)  10.3 us
    ppermute x2, starting transfers between devices, extended(): lax.ppermute(tail, axis, [(i, (i + 1) % count) for i in range(ends)])  10.2 us
    reshape x1, local copies, waits for them, and re-layouts, shards(): ext_x = ext_x.reshape(count_ns, 3 * blocks, B)  8.63 us
    reshape x1, local copies, waits for them, and re-layouts, shards(): ext_w = ext_w.reshape(count_ns, 3 * blocks, B)  8.63 us
  transfers between devices with their start and end apart: 5, of which 5 were waited for; matrix products, arithmetic and copies ran while one was open for 5% of the time, Pallas kernels for 0%

commit v1 on v0

v1 whole, which is shorter than its diff:
```python
import functools

import jax
import jax.numpy as jnp
from jax import lax
from jax.experimental import pallas as pl
from jax.experimental.pallas import tpu as pltpu
from jax.sharding import PartitionSpec as P

B = 256
STEP = 0.25
PENALTY = 0.5
ANY = pl.BlockSpec(memory_space=pl.ANY)
VMEM = pl.BlockSpec(memory_space=pltpu.VMEM)
SMEM = pl.BlockSpec(memory_space=pltpu.SMEM)


def image_kernel(meta, src, blk, col, x_own, x_far, x_near, tiles, send_p, send_m, keep_p, keep_m, own,
                 rows_v, tiles_v, acc, row_sem, tile_sem):
    count = meta[0]
    r = meta[1]
    samples, width = acc.shape
    quarter = samples // 4
    half = quarter // 2

    def start(s, carry):
        at = pl.ds(pl.multiple_of(blk[s] * B, B), B)
        for k, ref in enumerate((x_own, x_far, x_near)):
            @pl.when(src[s] == k)
            def _():
                pltpu.make_async_copy(ref.at[:, at], rows_v.at[s], row_sem.at[s]).start()
        pltpu.make_async_copy(tiles.at[s], tiles_v.at[s], tile_sem.at[s]).start()
        return carry

    lax.fori_loop(0, count, start, 0)
    acc[...] = jnp.zeros_like(acc)

    def step(s, carry):
        pltpu.make_async_copy(x_own.at[:, pl.ds(0, B)], rows_v.at[s], row_sem.at[s]).wait()
        pltpu.make_async_copy(tiles.at[s], tiles_v.at[s], tile_sem.at[s]).wait()
        at = pl.ds(pl.multiple_of(col[s] * B, B), B)
        acc[:, at] += jnp.dot(rows_v[s], tiles_v[s], preferred_element_type=jnp.float32)
        return carry

    lax.fori_loop(0, count, step, 0)

    def part(chunk, off, rows):
        first = lax.rem(r + chunk, 4) * quarter + off
        return acc[pl.ds(pl.multiple_of(first, half), rows), :]

    send_p[:half] = part(2, half, half).astype(send_p.dtype)
    send_p[half:] = part(1, 0, half).astype(send_p.dtype)
    send_m[:half] = part(2, 0, half).astype(send_m.dtype)
    send_m[half:] = part(3, half, half).astype(send_m.dtype)
    keep_p[...] = part(1, half, half)
    keep_m[...] = part(3, 0, half)
    own[...] = part(0, 0, quarter)


def image_parts(meta, src, blk, col, x_own, x_far, x_near, tiles):
    samples, width = x_own.shape
    slots = tiles.shape[0]
    q = samples // 4
    f32, bf16 = jnp.float32, jnp.bfloat16
    return pl.pallas_call(
        image_kernel,
        out_shape=[
            jax.ShapeDtypeStruct((q, width), bf16),
            jax.ShapeDtypeStruct((q, width), bf16),
            jax.ShapeDtypeStruct((q // 2, width), f32),
            jax.ShapeDtypeStruct((q // 2, width), f32),
            jax.ShapeDtypeStruct((q, width), f32),
        ],
        in_specs=[SMEM] * 4 + [ANY] * 4,
        out_specs=[VMEM] * 5,
        scratch_shapes=[
            pltpu.VMEM((slots, samples, B), bf16),
            pltpu.VMEM((slots, B, B), bf16),
            pltpu.VMEM((samples, width), f32),
            pltpu.SemaphoreType.DMA((slots,)),
            pltpu.SemaphoreType.DMA((slots,)),
        ],
        compiler_params=pltpu.CompilerParams(vmem_limit_bytes=32 << 20),
        cost_estimate=pl.CostEstimate(flops=slots * 2 * samples * B * B, bytes_accessed=10 << 20, transcendentals=0),
        name="image_parts",
    )(meta, src, blk, col, x_own, x_far, x_near, tiles)


def grad_kernel(meta, src, blk, col, x_own, x_far, x_near, *rest):
    w_pieces = rest[:15]
    tiles, diag, out, new_diag, xv, wv, tiles_v, x_sem, w_sem, tile_sem = rest[15:]
    count = meta[0]
    r = meta[1]
    samples, width = x_own.shape
    quarter = samples // 4
    half = quarter // 2
    xs = [pltpu.make_async_copy(ref, xv.at[k], x_sem.at[k]) for k, ref in enumerate((x_own, x_far, x_near))]
    ws = []
    places = ((0, 0, quarter), (3, 0, quarter), (1, 0, quarter), (2, 0, half), (2, half, half))
    for k in range(3):
        for p, (chunk, off, rows) in enumerate(places):
            first = pl.multiple_of(lax.rem(r + chunk, 4) * quarter + off, half)
            ws.append(pltpu.make_async_copy(w_pieces[5 * k + p], wv.at[k, pl.ds(first, rows)], w_sem.at[5 * k + p]))
    tc = pltpu.make_async_copy(tiles, tiles_v, tile_sem)
    for c in xs + ws + [tc]:
        c.start()
    for c in xs + ws + [tc]:
        c.wait()

    dims = (((0,), (0,)), ((), ()))

    def step(s, carry):
        k = src[s]
        at_i = pl.ds(pl.multiple_of(blk[s] * B, B), B)
        at_j = pl.ds(pl.multiple_of(col[s] * B, B), B)
        grad = lax.dot_general(xv[k, :, at_i], wv[0, :, at_j], dims, preferred_element_type=jnp.float32)
        grad += lax.dot_general(wv[k, :, at_i], xv[0, :, at_j], dims, preferred_element_type=jnp.float32)
        moved = tiles_v[s].astype(jnp.float32) - grad * (STEP / (2.0 * samples))
        cut = STEP * PENALTY
        out[s] = (moved - jnp.clip(moved, -cut, cut)).astype(out.dtype)
        return carry

    lax.fori_loop(0, count, step, 0)

    def clear(s, carry):
        out[s] = jnp.zeros((B, B), out.dtype)
        return carry

    lax.fori_loop(count, out.shape[0], clear, 0)
    dots = jnp.sum(xv[0].astype(jnp.float32) * wv[0].astype(jnp.float32), axis=0, keepdims=True) / samples
    d = diag[...]
    new_diag[...] = d - STEP * (dots - 1.0 / d)


def updates(meta, src, blk, col, x_own, x_far, x_near, w_pieces, tiles, diag):
    samples, width = x_own.shape
    slots = tiles.shape[0]
    f32, bf16 = jnp.float32, jnp.bfloat16
    return pl.pallas_call(
        grad_kernel,
        out_shape=[
            jax.ShapeDtypeStruct(tiles.shape, bf16),
            jax.ShapeDtypeStruct((1, width), f32),
        ],
        in_specs=[SMEM] * 4 + [ANY] * 19 + [VMEM],
        out_specs=[VMEM, VMEM],
        scratch_shapes=[
            pltpu.VMEM((3, samples, width), bf16),
            pltpu.VMEM((3, samples, width), bf16),
            pltpu.VMEM(tiles.shape, bf16),
            pltpu.SemaphoreType.DMA((3,)),
            pltpu.SemaphoreType.DMA((15,)),
            pltpu.SemaphoreType.DMA,
        ],
        compiler_params=pltpu.CompilerParams(vmem_limit_bytes=40 << 20),
        cost_estimate=pl.CostEstimate(flops=slots * 4 * samples * B * B, bytes_accessed=18 << 20, transcendentals=0),
        name="updates",
    )(meta, src, blk, col, x_own, x_far, x_near, *w_pieces, tiles, diag)


def shards(samples, theta_tiles, theta_diag, tile_row, tile_col, tile_count):
    count_ns, width = samples.shape
    blocks = width // B
    groups = lax.axis_size("blk")
    reps = lax.axis_size("rep")
    group = lax.axis_index("blk")
    r = lax.axis_index("rep")
    f32, bf16 = jnp.float32, jnp.bfloat16
    half = count_ns // 8

    far = [p for g in range(1, groups - 1, 2) for p in ((g, g + 1), (g + 1, g))]
    near = [p for g in range(0, groups, 2) for p in ((g, g + 1), (g + 1, g))]
    swap_far = lambda v: lax.ppermute(v, "blk", far)
    swap_near = lambda v: lax.ppermute(v, "blk", near)
    up = lambda v: lax.ppermute(v, "rep", [(i, (i + 1) % reps) for i in range(reps)])
    down = lambda v: lax.ppermute(v, "rep", [((i + 1) % reps, i) for i in range(reps)])

    rel = tile_row // blocks - group
    even = group % 2 == 0
    src = jnp.where(rel == 0, 0, jnp.where((rel < 0) == even, 1, 2)).astype(jnp.int32)
    blk = (tile_row % blocks).astype(jnp.int32)
    col = tile_col.astype(jnp.int32)
    meta = jnp.stack([tile_count[0], r.astype(jnp.int32)])

    x_far = swap_far(samples)
    x_near = swap_near(samples)
    send_p, send_m, keep_p, keep_m, own = image_parts(meta, src, blk, col, samples, x_far, x_near, theta_tiles)
    got_p = up(send_p)
    got_m = down(send_m)
    second_p = up((keep_p + got_p[:half].astype(f32)).astype(bf16))
    second_m = down((keep_m + got_m[:half].astype(f32)).astype(bf16))
    x_mine = lax.dynamic_slice_in_dim(samples, r * (2 * half), 2 * half, 0)
    first = jnp.concatenate([got_p[half:].astype(f32) + second_m.astype(f32),
                             got_m[half:].astype(f32) + second_p.astype(f32)], axis=0)
    w_mine = (own + first + x_mine.astype(f32) * theta_diag[None, :]).astype(bf16)
    w_below = up(w_mine)
    w_above = down(w_mine)
    w_op_a = up(w_below[:half])
    w_op_b = down(w_above[half:])
    pieces = [w_mine, w_below, w_above, w_op_a, w_op_b]
    far_pieces = [swap_far(p) for p in pieces]
    near_pieces = [swap_near(p) for p in pieces]
    new_tiles, new_diag = updates(meta, src, blk, col, samples, x_far, x_near,
                                  pieces + far_pieces + near_pieces, theta_tiles, theta_diag[None, :])
    return new_tiles, new_diag.reshape(width)


def solution(mesh):
    placed = (
        P(None, "blk"),
        P(("blk", "rep"), None, None),
        P("blk"),
        P(("blk", "rep")),
        P(("blk", "rep")),
        P(("blk", "rep")),
    )
    return jax.shard_map(
        shards,
        mesh=mesh,
        in_specs=placed,
        out_specs=(P(("blk", "rep"), None, None), P("blk")),
        check_vma=False,
    )
```

time: 275 us -> 136 us (0.49)
  waiting for transfers between devices: 141 us -> 65.8 us
  local copies, waits for them, and re-layouts: 60.5 us -> 3.9 us
  starting transfers between devices: 14.2 us -> 41.1 us
  matrix products: 26.4 us -> 0 us
  Pallas kernels: 0 us -> 20 us
  between operations: 14.8 us -> 1.51 us
  other arithmetic: 16.7 us -> 4.29 us
    psum x1 -> x0, waiting for transfers between devices: 96.6 us -> none  [shards(): summed = lax.psum(partial_image, 'rep')]
    reshape x5 -> x0, local copies, waits for them, and re-layouts: 27.8 us -> none  [the longest x1 8.63 us: shards(): ext_x = ext_x.reshape(count_ns, 3 * blocks, B)]
    ppermute x4 -> x20, starting transfers between devices: 14.2 us -> 41.1 us  [the longest x6 24.7 us: shards(): swap_far = lambda v: lax.ppermute(v, 'blk', far)]
    dot_general x4 -> x0, matrix products: 26.4 us -> none  [the longest x1 8.41 us: shards(): jnp.einsum('stb,tk->skb', prod, onehot, precision=lax.Precision.HIGHEST)]
    ppermute x4 -> x20, waiting for transfers between devices: 44 us -> 65.8 us  [the longest x6 33.6 us: shards(): swap_far = lambda v: lax.ppermute(v, 'blk', far)]
    pallas_call x0 -> x2, Pallas kernels: none -> 20 us  [the longest x1 11.5 us: updates(): pl.pallas_call(grad_kernel, out_shape=[jax.ShapeDtypeStruct(tiles.shape,...]
    gather x4 -> x0, local copies, waits for them, and re-layouts: 18.2 us -> none  [the longest x1 5.54 us: shards(): w_row = jnp.take(ext_w, rows, axis=1)]
    concatenate x2 -> x0, other arithmetic: 11.4 us -> none  [extended(): jnp.concatenate([lax.ppermute(tail, axis, [(i, (i + 1) % count) for i in...]
  transfers between devices with their start and end apart: 5 -> 20, of which waited for: 5 -> 8; matrix products, arithmetic and copies ran while one was open for 5% -> 1% of each run, Pallas kernels for 0% -> 0%
where the time goes in v1:
time: 136 us; the launch traced here: 137 us
  waiting for transfers between devices  65.8 us (48%)
  starting transfers between devices  41.1 us (30%)
  Pallas kernels  20 us (15%)
  other arithmetic  4.29 us (3%)
  local copies, waits for them, and re-layouts  3.9 us (3%)
  between operations  1.51 us (1%)
    ppermute x6, waiting for transfers between devices, shards(): swap_far = lambda v: lax.ppermute(v, 'blk', far)  33.6 us
    ppermute x6, starting transfers between devices, shards(): swap_far = lambda v: lax.ppermute(v, 'blk', far)  24.7 us
    ppermute x4, waiting for transfers between devices, shards(): lax.ppermute(v, 'rep', [((i + 1) % reps, i) for i in range(reps)])  21.5 us
    pallas_call x1, Pallas kernels, updates(): pl.pallas_call(grad_kernel, out_shape=[jax.ShapeDtypeStruct(tiles.shape,...  11.5 us
    ppermute x4, waiting for transfers between devices, shards(): lax.ppermute(v, 'rep', [(i, (i + 1) % reps) for i in range(reps)])  10.7 us
    pallas_call x1, Pallas kernels, image_parts(): pl.pallas_call(image_kernel, out_shape=[jax.ShapeDtypeStruct((q, width),...  8.51 us
    ppermute x6, starting transfers between devices, shards(): swap_near = lambda v: lax.ppermute(v, 'blk', near)  8.08 us
    ppermute x4, starting transfers between devices, shards(): lax.ppermute(v, 'rep', [((i + 1) % reps, i) for i in range(reps)])  6.81 us
  transfers between devices with their start and end apart: 20, of which 8 were waited for; matrix products, arithmetic and copies ran while one was open for 1% of the time, Pallas kernels for 0%

profile of v1, /device:TPU:103, one launch (start us, length us, event | category | flops | bytes accessed | tf_op | source)
XLA Modules:
  0.0 136.5 jit_solution(1669656350351033349)
XLA Ops:
  0.6 0.8 collective-permute-start.1
  1.4 4.6 %collective-permute-start = (bf16[512,2048]{1,0:T(8,128)(2,1)}, bf16[512,2048]{1,0:T(8,128)(2,1)}, u32[]{:S(2)}, u32[]{:S(2)}) collective-permute-start(bf16[512,2048]{1,0:T(8,128)(2,1)} %x_own.3), channel_id=1, source_target_pairs={{4,8},{8,4},{12,16},{16,12},{20,24},{24,20},{28,32},{32,28},{36,40... | collective-permute-start | bytes 6291464 | tf_op jit(solution)/shard_map/ppermute | solution.py:173
  6.6 0.1 pad_add_fusion.meta
  6.7 0.7 and_select_fusion
  7.4 0.0 collective-permute-done.1.x_near
  7.4 0.0 copy-start.3
  7.4 25.0 %collective-permute-done.x_far = bf16[512,2048]{1,0:T(8,128)(2,1)} collective-permute-done((bf16[512,2048]{1,0:T(8,128)(2,1)}, bf16[512,2048]{1,0:T(8,128)(2,1)}, u32[]{:S(2)}, u32[]{:S(2)}) %collective-permute-start) | collective-permute-done | bytes 2097184 | tf_op jit(solution)/shard_map/ppermute | solution.py:173
  32.4 0.0 copy-start
  32.4 1.6 %copy-done = bf16[512,2048]{1,0:T(8,128)(2,1)S(1)} copy-done((bf16[512,2048]{1,0:T(8,128)(2,1)S(1)}, bf16[512,2048]{1,0:T(8,128)(2,1)}, u32[]{:S(2)}) %copy-start) | copy-done | bytes 2097176
  34.0 1.6 %copy-done.2 = bf16[16,256,256]{2,1,0:T(8,128)(2,1)S(1)} copy-done((bf16[16,256,256]{2,1,0:T(8,128)(2,1)S(1)}, bf16[16,256,256]{2,1,0:T(8,128)(2,1)}, u32[]{:S(2)}) %copy-start.2) | copy-done | bytes 2097176
  35.6 0.0 copy-start.6
  35.6 0.7 copy-done.6
  36.2 8.5 %image_parts.1 = (bf16[128,2048]{1,0:T(8,128)(2,1)S(1)}, bf16[128,2048]{1,0:T(8,128)(2,1)S(1)}, f32[64,2048]{1,0:T(8,128)S(1)}, f32[64,2048]{1,0:T(8,128)S(1)}, f32[128,2048]{1,0:T(8,128)S(1)}) custom-call(s32[2]{0:T(128)S(1)} %pad_add_fusion.meta, s32[16]{0:T(128)S(1)} %get-tuple-element.19.src, s32[16]{0:T(128)S(1)} %get-tuple-element.18.blk, ...), custom_call_target="tpu_custom_call" | custom-call | flops 1073741824 | bytes 10485760 | tf_op jit(solution)/shard_map/image_parts/pallas_call | solution.py:65
  44.7 0.0 copy-done.3
  44.7 0.1 collective-permute-start.3
  44.8 1.5 %collective-permute-start.2 = (bf16[128,2048]{1,0:T(8,128)(2,1)S(1)}, bf16[128,2048]{1,0:T(8,128)(2,1)S(1)}, u32[]{:S(2)}, u32[]{:S(2)}) collective-permute-start(bf16[128,2048]{1,0:T(8,128)(2,1)S(1)} %get-tuple-element.10), channel_id=1, source_target_pairs={{0,1},{1,2},{2,3},{3,0},{4,5},{5,6},{6,7},{7,4},{8,9},{9,10},{10,1... | collective-permute-start | bytes 1572872 | tf_op jit(solution)/shard_map/ppermute | solution.py:175
  46.3 10.2 %collective-permute-done.3 = bf16[128,2048]{1,0:T(8,128)(2,1)S(1)} collective-permute-done((bf16[128,2048]{1,0:T(8,128)(2,1)S(1)}, bf16[128,2048]{1,0:T(8,128)(2,1)S(1)}, u32[]{:S(2)}, u32[]{:S(2)}) %collective-permute-start.3) | collective-permute-done | bytes 524320 | tf_op jit(solution)/shard_map/ppermute | solution.py:176
  56.5 0.0 copy-start.8
  56.5 0.0 copy-start.1
  56.5 0.1 add_convert_fusion.1
  56.6 3.3 %collective-permute-start.4 = (bf16[64,2048]{1,0:T(8,128)(2,1)S(1)}, bf16[64,2048]{1,0:T(8,128)(2,1)S(1)}, u32[]{:S(2)}, u32[]{:S(2)}) collective-permute-start(bf16[64,2048]{1,0:T(8,128)(2,1)S(1)} %add_convert_fusion.1), channel_id=1, source_target_pairs={{1,0},{2,1},{3,2},{0,3},{5,4},{6,5},{7,6},{4,7},{9,8},{10,9},{11,1... | collective-permute-start | bytes 786440 | tf_op jit(solution)/shard_map/ppermute | solution.py:176
  59.9 0.0 collective-permute-done.2
  59.9 0.0 copy-done.8
  59.9 5.3 %collective-permute-done.4 = bf16[64,2048]{1,0:T(8,128)(2,1)S(1)} collective-permute-done((bf16[64,2048]{1,0:T(8,128)(2,1)S(1)}, bf16[64,2048]{1,0:T(8,128)(2,1)S(1)}, u32[]{:S(2)}, u32[]{:S(2)}) %collective-permute-start.4) | collective-permute-done | bytes 262176 | tf_op jit(solution)/shard_map/ppermute | solution.py:176
  65.2 1.0 convert_add_fusion.1
  66.2 0.0 collective-permute-start.5
  66.2 9.0 %collective-permute-done.5 = bf16[64,2048]{1,0:T(8,128)(2,1)S(1)} collective-permute-done((bf16[64,2048]{1,0:T(8,128)(2,1)}, bf16[64,2048]{1,0:T(8,128)(2,1)S(1)}, u32[]{:S(2)}, u32[]{:S(2)}) %collective-permute-start.5) | collective-permute-done | bytes 262176 | tf_op jit(solution)/shard_map/ppermute | solution.py:175
  75.2 1.0 convert_add_fusion
  76.2 0.0 copy-done.1
  76.2 0.0 copy-done.5
  76.2 0.0 copy-start.4
  76.2 0.0 copy-start.7
  76.3 1.5 %fusion.1.rest_0_ = bf16[128,2048]{1,0:T(8,128)(2,1)S(1)} fusion(f32[128,2048]{1,0:T(8,128)S(1)} %get-tuple-element.9, f32[64,2048]{1,0:T(8,128)S(1)} %convert_add_fusion, f32[64,2048]{1,0:T(8,128)} %get-tuple-element.16, f32[2048]{0:T(1024)S(1)} %copy-done.5, bf16[512,2048]{1,0:T(8,128)(2,1)S(1)} %copy-done.1, s32[]{:T(128)S(6)} %select_n.34), kind=kLoop, calls=%fused_computation.2 | loop fusion | flops 1572864 | bytes 3153924 | tf_op jit(solution)/shard_map/convert_element_type | solution.py:195
  77.7 1.2 collective-permute-start.7
  79.0 2.4 %collective-permute-start.15 = (bf16[128,2048]{1,0:T(8,128)(2,1)S(1)}, bf16[128,2048]{1,0:T(8,128)(2,1)S(1)}, u32[]{:S(2)}, u32[]{:S(2)}) collective-permute-start(bf16[128,2048]{1,0:T(8,128)(2,1)S(1)} %fusion.1.rest_0_), channel_id=1, source_target_pairs={{0,4},{4,0},{8,12},{12,8},{16,20},{20,16},{24,28},{28,24},{32,36},... | collective-permute-start | bytes 1572872 | tf_op jit(solution)/shard_map/ppermute | solution.py:174
  81.4 0.0 collective-permute-start.6
  81.4 1.9 %collective-permute-start.10 = (bf16[128,2048]{1,0:T(8,128)(2,1)S(1)}, bf16[128,2048]{1,0:T(8,128)(2,1)S(1)}, u32[]{:S(2)}, u32[]{:S(2)}) collective-permute-start(bf16[128,2048]{1,0:T(8,128)(2,1)S(1)} %fusion.1.rest_0_), channel_id=1, source_target_pairs={{4,8},{8,4},{12,16},{16,12},{20,24},{24,20},{28,32},{32,28},{36,40... | collective-permute-start | bytes 1572872 | tf_op jit(solution)/shard_map/ppermute | solution.py:173
  83.3 6.0 %collective-permute-done.7.rest_2_ = bf16[128,2048]{1,0:T(8,128)(2,1)S(1)} collective-permute-done((bf16[128,2048]{1,0:T(8,128)(2,1)S(1)}, bf16[128,2048]{1,0:T(8,128)(2,1)S(1)}, u32[]{:S(2)}, u32[]{:S(2)}) %collective-permute-start.7) | collective-permute-done | bytes 524320 | tf_op jit(solution)/shard_map/ppermute | solution.py:176
  89.4 2.2 %collective-permute-start.9 = (bf16[64,2048]{1,0:T(8,128)(2,1)S(1)}, bf16[64,2048]{1,0:T(8,128)(2,1)S(1)}, u32[]{:S(2)}, u32[]{:S(2)}) collective-permute-start(bf16[64,2048]{1,0:T(8,128)(2,1)S(1)} %slice.29), channel_id=1, source_target_pairs={{1,0},{2,1},{3,2},{0,3},{5,4},{6,5},{7,6},{4,7},{9,8},{10,9},{11,1... | collective-permute-start | bytes 786440 | tf_op jit(solution)/shard_map/ppermute | solution.py:176
  91.5 3.4 %collective-permute-start.17 = (bf16[128,2048]{1,0:T(8,128)(2,1)S(1)}, bf16[128,2048]{1,0:T(8,128)(2,1)S(1)}, u32[]{:S(2)}, u32[]{:S(2)}) collective-permute-start(bf16[128,2048]{1,0:T(8,128)(2,1)S(1)} %collective-permute-done.7.rest_2_), channel_id=1, source_target_pairs={{0,4},{4,0},{8,12},{12,8},{16,20},{20,16},{24,28},{28,24},{32,36},... | collective-permute-start | bytes 1572872 | tf_op jit(solution)/shard_map/ppermute | solution.py:174
  94.9 0.0 collective-permute-done.15.rest_10_
  94.9 1.9 %collective-permute-start.12 = (bf16[128,2048]{1,0:T(8,128)(2,1)S(1)}, bf16[128,2048]{1,0:T(8,128)(2,1)S(1)}, u32[]{:S(2)}, u32[]{:S(2)}) collective-permute-start(bf16[128,2048]{1,0:T(8,128)(2,1)S(1)} %collective-permute-done.7.rest_2_), channel_id=1, source_target_pairs={{4,8},{8,4},{12,16},{16,12},{20,24},{24,20},{28,32},{32,28},{36,40... | collective-permute-start | bytes 1572872 | tf_op jit(solution)/shard_map/ppermute | solution.py:173
  96.8 0.0 collective-permute-done.6.rest_1_
  96.8 0.1 collective-permute-start.16
  97.0 0.0 collective-permute-done.10.rest_5_
  97.0 0.1 collective-permute-start.8
  97.1 0.0 collective-permute-done.9.rest_4_
  97.1 6.9 %collective-permute-start.11 = (bf16[128,2048]{1,0:T(8,128)(2,1)S(1)}, bf16[128,2048]{1,0:T(8,128)(2,1)S(1)}, u32[]{:S(2)}, u32[]{:S(2)}) collective-permute-start(bf16[128,2048]{1,0:T(8,128)(2,1)S(1)} %collective-permute-done.6.rest_1_), channel_id=1, source_target_pairs={{4,8},{8,4},{12,16},{16,12},{20,24},{24,20},{28,32},{32,28},{36,40... | collective-permute-start | bytes 1572872 | tf_op jit(solution)/shard_map/ppermute | solution.py:173
  104.0 1.6 %collective-permute-done.8.rest_3_ = bf16[64,2048]{1,0:T(8,128)(2,1)S(1)} collective-permute-done((bf16[64,2048]{1,0:T(8,128)(2,1)S(1)}, bf16[64,2048]{1,0:T(8,128)(2,1)S(1)}, u32[]{:S(2)}, u32[]{:S(2)}) %collective-permute-start.8) | collective-permute-done | bytes 262176 | tf_op jit(solution)/shard_map/ppermute | solution.py:175
  105.7 1.3 collective-permute-start.19
  107.0 0.0 collective-permute-done.17.rest_12_
  107.0 6.9 %collective-permute-start.14 = (bf16[64,2048]{1,0:T(8,128)(2,1)S(1)}, bf16[64,2048]{1,0:T(8,128)(2,1)S(1)}, u32[]{:S(2)}, u32[]{:S(2)}) collective-permute-start(bf16[64,2048]{1,0:T(8,128)(2,1)S(1)} %collective-permute-done.9.rest_4_), channel_id=1, source_target_pairs={{4,8},{8,4},{12,16},{16,12},{20,24},{24,20},{28,32},{32,28},{36,40... | collective-permute-start | bytes 786440 | tf_op jit(solution)/shard_map/ppermute | solution.py:173
  113.9 0.0 collective-permute-done.12.rest_7_
  113.9 0.1 collective-permute-start.18
  114.0 0.0 collective-permute-done.16.rest_11_
  114.0 2.4 %collective-permute-start.13 = (bf16[64,2048]{1,0:T(8,128)(2,1)S(1)}, bf16[64,2048]{1,0:T(8,128)(2,1)S(1)}, u32[]{:S(2)}, u32[]{:S(2)}) collective-permute-start(bf16[64,2048]{1,0:T(8,128)(2,1)S(1)} %collective-permute-done.8.rest_3_), channel_id=1, source_target_pairs={{4,8},{8,4},{12,16},{16,12},{20,24},{24,20},{28,32},{32,28},{36,40... | collective-permute-start | bytes 786440 | tf_op jit(solution)/shard_map/ppermute | solution.py:173
  116.4 0.0 collective-permute-done.11.rest_6_
  116.5 0.0 collective-permute-done.19.rest_14_
  116.5 1.5 %collective-permute-done.14.rest_9_ = bf16[64,2048]{1,0:T(8,128)(2,1)S(1)} collective-permute-done((bf16[64,2048]{1,0:T(8,128)(2,1)S(1)}, bf16[64,2048]{1,0:T(8,128)(2,1)S(1)}, u32[]{:S(2)}, u32[]{:S(2)}) %collective-permute-start.14) | collective-permute-done | bytes 262176 | tf_op jit(solution)/shard_map/ppermute | solution.py:173
  118.0 0.0 collective-permute-done.18.rest_13_
  118.0 7.1 %collective-permute-done.13.rest_8_ = bf16[64,2048]{1,0:T(8,128)(2,1)S(1)} collective-permute-done((bf16[64,2048]{1,0:T(8,128)(2,1)S(1)}, bf16[64,2048]{1,0:T(8,128)(2,1)S(1)}, u32[]{:S(2)}, u32[]{:S(2)}) %collective-permute-start.13) | collective-permute-done | bytes 262176 | tf_op jit(solution)/shard_map/ppermute | solution.py:173
  125.1 0.0 copy-done.4
  125.1 0.0 copy-done.7
  125.1 11.5 %updates.1 = (bf16[16,256,256]{2,1,0:T(8,128)(2,1)}, f32[1,2048]{1,0:T(1,128)}) custom-call(s32[2]{0:T(128)S(1)} %pad_add_fusion.meta, s32[16]{0:T(128)S(1)} %get-tuple-element.19.src, s32[16]{0:T(128)S(1)} %get-tuple-element.18.blk, s32[16]{0:T(128)S(1)} %copy-done.7, bf16[512,2048]{1,0:T(8,128)(2,1)S(1)} %copy-done.1, ...), custom_call_target="tpu_custom_call" | custom-call | flops 2147483648 | bytes 18874368 | tf_op jit(solution)/shard_map/updates/pallas_call | solution.py:139
  (4 shorter events, 0.0 us)
Async XLA Ops:
  0.6 6.8 %collective-permute-start.1 = (bf16[512,2048]{1,0:T(8,128)(2,1)}, bf16[512,2048]{1,0:T(8,128)(2,1)S(1)}, u32[]{:S(2)}, u32[]{:S(2)}) collective-permute-start(bf16[512,2048]{1,0:T(8,128)(2,1)} %x_own.3), channel_id=1, source_target_pairs={{0,4},{4,0},{8,12},{12,8},{16,20},{20,16},{24,28},{28,24},{32,36},... | collective-permute-start | bytes 6291464 | tf_op jit(solution)/shard_map/ppermute | solution.py:174
  1.4 31.0 %collective-permute-start = (bf16[512,2048]{1,0:T(8,128)(2,1)}, bf16[512,2048]{1,0:T(8,128)(2,1)}, u32[]{:S(2)}, u32[]{:S(2)}) collective-permute-start(bf16[512,2048]{1,0:T(8,128)(2,1)} %x_own.3), channel_id=1, source_target_pairs={{4,8},{8,4},{12,16},{16,12},{20,24},{24,20},{28,32},{32,28},{36,40... | collective-permute-start | bytes 6291464 | tf_op jit(solution)/shard_map/ppermute | solution.py:173
  7.4 37.3 %copy-start.3 = (bf16[512,2048]{1,0:T(8,128)(2,1)}, bf16[512,2048]{1,0:T(8,128)(2,1)S(1)}, u32[]{:S(2)}) copy-start(bf16[512,2048]{1,0:T(8,128)(2,1)S(1)} %collective-permute-done.1.x_near) | copy-start | bytes 6291460
  32.4 1.6 %copy-start = (bf16[512,2048]{1,0:T(8,128)(2,1)S(1)}, bf16[512,2048]{1,0:T(8,128)(2,1)}, u32[]{:S(2)}) copy-start(bf16[512,2048]{1,0:T(8,128)(2,1)} %x_own.3) | copy-start | bytes 6291460
  34.0 1.6 %copy-start.2 = (bf16[16,256,256]{2,1,0:T(8,128)(2,1)S(1)}, bf16[16,256,256]{2,1,0:T(8,128)(2,1)}, u32[]{:S(2)}) copy-start(bf16[16,256,256]{2,1,0:T(8,128)(2,1)} %rest_15_.1) | copy-start | bytes 6291460
  35.6 0.7 copy-start.6
  44.7 11.8 %collective-permute-start.3 = (bf16[128,2048]{1,0:T(8,128)(2,1)S(1)}, bf16[128,2048]{1,0:T(8,128)(2,1)S(1)}, u32[]{:S(2)}, u32[]{:S(2)}) collective-permute-start(bf16[128,2048]{1,0:T(8,128)(2,1)S(1)} %get-tuple-element.12), channel_id=1, source_target_pairs={{1,0},{2,1},{3,2},{0,3},{5,4},{6,5},{7,6},{4,7},{9,8},{10,9},{11,1... | collective-permute-start | bytes 1572872 | tf_op jit(solution)/shard_map/ppermute | solution.py:176
  44.8 15.0 %collective-permute-start.2 = (bf16[128,2048]{1,0:T(8,128)(2,1)S(1)}, bf16[128,2048]{1,0:T(8,128)(2,1)S(1)}, u32[]{:S(2)}, u32[]{:S(2)}) collective-permute-start(bf16[128,2048]{1,0:T(8,128)(2,1)S(1)} %get-tuple-element.10), channel_id=1, source_target_pairs={{0,1},{1,2},{2,3},{3,0},{4,5},{5,6},{6,7},{7,4},{8,9},{9,10},{10,1... | collective-permute-start | bytes 1572872 | tf_op jit(solution)/shard_map/ppermute | solution.py:175
  56.5 3.4 %copy-start.8 = (bf16[128,2048]{1,0:T(8,128)(2,1)}, bf16[128,2048]{1,0:T(8,128)(2,1)S(1)}, u32[]{:S(2)}) copy-start(bf16[128,2048]{1,0:T(8,128)(2,1)S(1)} %collective-permute-done.3) | copy-start | bytes 1572868
  56.5 19.7 %copy-start.1 = (bf16[512,2048]{1,0:T(8,128)(2,1)S(1)}, bf16[512,2048]{1,0:T(8,128)(2,1)}, u32[]{:S(2)}) copy-start(bf16[512,2048]{1,0:T(8,128)(2,1)} %x_own.3) | copy-start | bytes 6291460
  56.5 19.7 %copy-start.5 = (f32[2048]{0:T(1024)S(1)}, f32[2048]{0:T(1024)}, u32[]{:S(2)}) copy-start(f32[2048]{0:T(1024)} %param.8) | copy-start | bytes 24580
  56.6 8.6 %collective-permute-start.4 = (bf16[64,2048]{1,0:T(8,128)(2,1)S(1)}, bf16[64,2048]{1,0:T(8,128)(2,1)S(1)}, u32[]{:S(2)}, u32[]{:S(2)}) collective-permute-start(bf16[64,2048]{1,0:T(8,128)(2,1)S(1)} %add_convert_fusion.1), channel_id=1, source_target_pairs={{1,0},{2,1},{3,2},{0,3},{5,4},{6,5},{7,6},{4,7},{9,8},{10,9},{11,1... | collective-permute-start | bytes 786440 | tf_op jit(solution)/shard_map/ppermute | solution.py:176
  66.2 9.0 %collective-permute-start.5 = (bf16[64,2048]{1,0:T(8,128)(2,1)}, bf16[64,2048]{1,0:T(8,128)(2,1)S(1)}, u32[]{:S(2)}, u32[]{:S(2)}) collective-permute-start(bf16[64,2048]{1,0:T(8,128)(2,1)} %get-tuple-element.17), channel_id=1, source_target_pairs={{0,1},{1,2},{2,3},{3,0},{4,5},{5,6},{6,7},{7,4},{8,9},{9,10},{10,1... | collective-permute-start | bytes 786440 | tf_op jit(solution)/shard_map/ppermute | solution.py:175
  76.2 48.8 %copy-start.4 = (bf16[512,2048]{1,0:T(8,128)(2,1)S(1)}, bf16[512,2048]{1,0:T(8,128)(2,1)}, u32[]{:S(2)}) copy-start(bf16[512,2048]{1,0:T(8,128)(2,1)} %copy-done.3) | copy-start | bytes 6291460
  76.2 48.8 %copy-start.7 = (s32[16]{0:T(128)S(1)}, s32[16]{0:T(128)}, u32[]{:S(2)}) copy-start(s32[16]{0:T(128)} %col.3) | copy-start | bytes 196
  77.7 11.6 %collective-permute-start.7 = (bf16[128,2048]{1,0:T(8,128)(2,1)S(1)}, bf16[128,2048]{1,0:T(8,128)(2,1)S(1)}, u32[]{:S(2)}, u32[]{:S(2)}) collective-permute-start(bf16[128,2048]{1,0:T(8,128)(2,1)S(1)} %fusion.1.rest_0_), channel_id=1, source_target_pairs={{1,0},{2,1},{3,2},{0,3},{5,4},{6,5},{7,6},{4,7},{9,8},{10,9},{11,1... | collective-permute-start | bytes 1572872 | tf_op jit(solution)/shard_map/ppermute | solution.py:176
  79.0 15.9 %collective-permute-start.15 = (bf16[128,2048]{1,0:T(8,128)(2,1)S(1)}, bf16[128,2048]{1,0:T(8,128)(2,1)S(1)}, u32[]{:S(2)}, u32[]{:S(2)}) collective-permute-start(bf16[128,2048]{1,0:T(8,128)(2,1)S(1)} %fusion.1.rest_0_), channel_id=1, source_target_pairs={{0,4},{4,0},{8,12},{12,8},{16,20},{20,16},{24,28},{28,24},{32,36},... | collective-permute-start | bytes 1572872 | tf_op jit(solution)/shard_map/ppermute | solution.py:174
  81.4 15.4 %collective-permute-start.6 = (bf16[128,2048]{1,0:T(8,128)(2,1)S(1)}, bf16[128,2048]{1,0:T(8,128)(2,1)S(1)}, u32[]{:S(2)}, u32[]{:S(2)}) collective-permute-start(bf16[128,2048]{1,0:T(8,128)(2,1)S(1)} %fusion.1.rest_0_), channel_id=1, source_target_pairs={{0,1},{1,2},{2,3},{3,0},{4,5},{5,6},{6,7},{7,4},{8,9},{9,10},{10,1... | collective-permute-start | bytes 1572872 | tf_op jit(solution)/shard_map/ppermute | solution.py:175
  81.4 15.6 %collective-permute-start.10 = (bf16[128,2048]{1,0:T(8,128)(2,1)S(1)}, bf16[128,2048]{1,0:T(8,128)(2,1)S(1)}, u32[]{:S(2)}, u32[]{:S(2)}) collective-permute-start(bf16[128,2048]{1,0:T(8,128)(2,1)S(1)} %fusion.1.rest_0_), channel_id=1, source_target_pairs={{4,8},{8,4},{12,16},{16,12},{20,24},{24,20},{28,32},{32,28},{36,40... | collective-permute-start | bytes 1572872 | tf_op jit(solution)/shard_map/ppermute | solution.py:173
  89.4 7.7 %collective-permute-start.9 = (bf16[64,2048]{1,0:T(8,128)(2,1)S(1)}, bf16[64,2048]{1,0:T(8,128)(2,1)S(1)}, u32[]{:S(2)}, u32[]{:S(2)}) collective-permute-start(bf16[64,2048]{1,0:T(8,128)(2,1)S(1)} %slice.29), channel_id=1, source_target_pairs={{1,0},{2,1},{3,2},{0,3},{5,4},{6,5},{7,6},{4,7},{9,8},{10,9},{11,1... | collective-permute-start | bytes 786440 | tf_op jit(solution)/shard_map/ppermute | solution.py:176
  91.5 15.4 %collective-permute-start.17 = (bf16[128,2048]{1,0:T(8,128)(2,1)S(1)}, bf16[128,2048]{1,0:T(8,128)(2,1)S(1)}, u32[]{:S(2)}, u32[]{:S(2)}) collective-permute-start(bf16[128,2048]{1,0:T(8,128)(2,1)S(1)} %collective-permute-done.7.rest_2_), channel_id=1, source_target_pairs={{0,4},{4,0},{8,12},{12,8},{16,20},{20,16},{24,28},{28,24},{32,36},... | collective-permute-start | bytes 1572872 | tf_op jit(solution)/shard_map/ppermute | solution.py:174
  94.9 19.0 %collective-permute-start.12 = (bf16[128,2048]{1,0:T(8,128)(2,1)S(1)}, bf16[128,2048]{1,0:T(8,128)(2,1)S(1)}, u32[]{:S(2)}, u32[]{:S(2)}) collective-permute-start(bf16[128,2048]{1,0:T(8,128)(2,1)S(1)} %collective-permute-done.7.rest_2_), channel_id=1, source_target_pairs={{4,8},{8,4},{12,16},{16,12},{20,24},{24,20},{28,32},{32,28},{36,40... | collective-permute-start | bytes 1572872 | tf_op jit(solution)/shard_map/ppermute | solution.py:173
  96.8 17.2 %collective-permute-start.16 = (bf16[128,2048]{1,0:T(8,128)(2,1)S(1)}, bf16[128,2048]{1,0:T(8,128)(2,1)S(1)}, u32[]{:S(2)}, u32[]{:S(2)}) collective-permute-start(bf16[128,2048]{1,0:T(8,128)(2,1)S(1)} %collective-permute-done.6.rest_1_), channel_id=1, source_target_pairs={{0,4},{4,0},{8,12},{12,8},{16,20},{20,16},{24,28},{28,24},{32,36},... | collective-permute-start | bytes 1572872 | tf_op jit(solution)/shard_map/ppermute | solution.py:174
  97.0 8.7 %collective-permute-start.8 = (bf16[64,2048]{1,0:T(8,128)(2,1)S(1)}, bf16[64,2048]{1,0:T(8,128)(2,1)S(1)}, u32[]{:S(2)}, u32[]{:S(2)}) collective-permute-start(bf16[64,2048]{1,0:T(8,128)(2,1)S(1)} %slice.28), channel_id=1, source_target_pairs={{0,1},{1,2},{2,3},{3,0},{4,5},{5,6},{6,7},{7,4},{8,9},{9,10},{10,1... | collective-permute-start | bytes 786440 | tf_op jit(solution)/shard_map/ppermute | solution.py:175
  97.1 19.4 %collective-permute-start.11 = (bf16[128,2048]{1,0:T(8,128)(2,1)S(1)}, bf16[128,2048]{1,0:T(8,128)(2,1)S(1)}, u32[]{:S(2)}, u32[]{:S(2)}) collective-permute-start(bf16[128,2048]{1,0:T(8,128)(2,1)S(1)} %collective-permute-done.6.rest_1_), channel_id=1, source_target_pairs={{4,8},{8,4},{12,16},{16,12},{20,24},{24,20},{28,32},{32,28},{36,40... | collective-permute-start | bytes 1572872 | tf_op jit(solution)/shard_map/ppermute | solution.py:173
  105.7 10.8 %collective-permute-start.19 = (bf16[64,2048]{1,0:T(8,128)(2,1)S(1)}, bf16[64,2048]{1,0:T(8,128)(2,1)S(1)}, u32[]{:S(2)}, u32[]{:S(2)}) collective-permute-start(bf16[64,2048]{1,0:T(8,128)(2,1)S(1)} %collective-permute-done.9.rest_4_), channel_id=1, source_target_pairs={{0,4},{4,0},{8,12},{12,8},{16,20},{20,16},{24,28},{28,24},{32,36},... | collective-permute-start | bytes 786440 | tf_op jit(solution)/shard_map/ppermute | solution.py:174
  107.0 11.0 %collective-permute-start.14 = (bf16[64,2048]{1,0:T(8,128)(2,1)S(1)}, bf16[64,2048]{1,0:T(8,128)(2,1)S(1)}, u32[]{:S(2)}, u32[]{:S(2)}) collective-permute-start(bf16[64,2048]{1,0:T(8,128)(2,1)S(1)} %collective-permute-done.9.rest_4_), channel_id=1, source_target_pairs={{4,8},{8,4},{12,16},{16,12},{20,24},{24,20},{28,32},{32,28},{36,40... | collective-permute-start | bytes 786440 | tf_op jit(solution)/shard_map/ppermute | solution.py:173
  113.9 4.1 %collective-permute-start.18 = (bf16[64,2048]{1,0:T(8,128)(2,1)S(1)}, bf16[64,2048]{1,0:T(8,128)(2,1)S(1)}, u32[]{:S(2)}, u32[]{:S(2)}) collective-permute-start(bf16[64,2048]{1,0:T(8,128)(2,1)S(1)} %collective-permute-done.8.rest_3_), channel_id=1, source_target_pairs={{0,4},{4,0},{8,12},{12,8},{16,20},{20,16},{24,28},{28,24},{32,36},... | collective-permute-start | bytes 786440 | tf_op jit(solution)/shard_map/ppermute | solution.py:174
  114.0 11.0 %collective-permute-start.13 = (bf16[64,2048]{1,0:T(8,128)(2,1)S(1)}, bf16[64,2048]{1,0:T(8,128)(2,1)S(1)}, u32[]{:S(2)}, u32[]{:S(2)}) collective-permute-start(bf16[64,2048]{1,0:T(8,128)(2,1)S(1)} %collective-permute-done.8.rest_3_), channel_id=1, source_target_pairs={{4,8},{8,4},{12,16},{16,12},{20,24},{24,20},{28,32},{32,28},{36,40... | collective-permute-start | bytes 786440 | tf_op jit(solution)/shard_map/ppermute | solution.py:173

commit v2 on v0

v2 whole, which is shorter than its diff:
```python
import functools

import jax
import jax.numpy as jnp
from jax import lax
from jax.experimental import pallas as pl
from jax.experimental.pallas import tpu as pltpu
from jax.sharding import PartitionSpec as P

B = 256
STEP = 0.25
PENALTY = 0.5
OWN, FAR, NEAR = 0, 1, 2
HBM = pl.BlockSpec(memory_space=pltpu.HBM)
VMEM = pl.BlockSpec(memory_space=pltpu.VMEM)
SMEM = pl.BlockSpec(memory_space=pltpu.SMEM)
ANY = pl.BlockSpec(memory_space=pl.ANY)
F32, BF16 = jnp.float32, jnp.bfloat16
DMA = pltpu.SemaphoreType.DMA
OVER_ROWS = (((0,), (0,)), ((), ()))
ROW_ORDER = (
    (0, 0, None), (1, 0, None), (0, 3, None), (0, 1, None), (1, 3, None), (1, 1, None),
    (0, 2, 0), (1, 2, 0), (0, 2, 1), (1, 2, 1),
)


def call(kernel, name, outs, ins, out_specs, flops, moved, scratch=(), aliases=None):
    return pl.pallas_call(
        kernel,
        out_shape=outs,
        in_specs=ins,
        out_specs=out_specs,
        scratch_shapes=scratch,
        input_output_aliases=aliases or {},
        compiler_params=pltpu.CompilerParams(vmem_limit_bytes=10 << 20),
        cost_estimate=pl.CostEstimate(flops=flops, bytes_accessed=moved, transcendentals=0),
        name=name,
    )


def like(shape, dtype):
    return jax.ShapeDtypeStruct(shape, dtype)


def block(index):
    return pl.ds(pl.multiple_of(index * B, B), B)


def each_live(count, body):
    def step(s, carry):
        body(s)
        return carry

    lax.fori_loop(0, count, step, 0)


def each_of(source, src, count, body):
    def one(s):
        @pl.when(src[s] == source)
        def _():
            body(s)

    each_live(count, one)


def over_rows(a, b):
    return lax.dot_general(a, b, OVER_ROWS, preferred_element_type=F32)


def soft(moved):
    cut = STEP * PENALTY
    return (moved - jnp.clip(moved, -cut, cut)).astype(BF16)


def load_kernel(firsts, src, *refs):
    n = len(firsts)
    copies = [
        pltpu.make_async_copy(src.at[pl.ds(first, dst.shape[0])], dst, refs[n].at[k])
        for k, (first, dst) in enumerate(zip(firsts, refs[:n], strict=True))
    ]
    for c in copies:
        c.start()
    for c in copies:
        c.wait()


def load(src, ranges):
    return call(
        functools.partial(load_kernel, [first for first, _ in ranges]), "load",
        [like((rows, src.shape[1]), src.dtype) for _, rows in ranges], [HBM], [VMEM] * len(ranges), 2 << 30, 1 << 20,
        [DMA((len(ranges),))],
    )(src)


def own_image_kernel(meta, src, blk, col, x_own, x_near, tiles, acc):
    acc[...] = jnp.zeros_like(acc)
    for source, x in ((OWN, x_own), (NEAR, x_near)):

        def add(s):
            acc[:, block(col[s])] += jnp.dot(x[:, block(blk[s])], tiles[s], preferred_element_type=F32)

        each_of(source, src, meta[0], add)


def far_image_kernel(first, meta, src, blk, col, acc, x_far, tiles, own, send_1, send_2, send_3, total):
    rows = total.shape[0]
    part = rows // 4
    total[...] = acc[first : first + rows, :]

    def add(s):
        total[:, block(col[s])] += jnp.dot(x_far[:, block(blk[s])], tiles[s], preferred_element_type=F32)

    each_of(FAR, src, meta[0], add)
    for k, out in enumerate((own, send_1, send_2, send_3)):
        at = pl.ds(pl.multiple_of(lax.rem(meta[1] + k, 4) * part, part), part)
        out[...] = total[at, :].astype(out.dtype)


def combined(first, meta, own, got, samples, diag):
    part = own.shape[0]
    at = pl.ds(pl.multiple_of(first + meta[1] * part, part), part)
    total = own[...]
    for other in got:
        total += other[:part, :].astype(F32)
    return (total + samples[at, :].astype(F32) * diag[...]).astype(BF16)


def first_combine_kernel(meta, own, got_1, got_2, got_3, samples, diag, mine):
    mine[...] = combined(0, meta, own, (got_1, got_2, got_3), samples, diag)


def second_combine_kernel(first, meta, own, got_1, got_2, got_3, samples, diag, below, above, _, __, mine, second):
    part = own.shape[0]
    mine[...] = combined(first, meta, own, (got_1, got_2, got_3), samples, diag)
    second[:part, :] = mine[...]
    second[part : 2 * part, :] = below[...]
    second[2 * part :, :] = above[...]


def stack_kernel(second, below, above, _, go_up, go_down):
    part = below.shape[0]
    half = part // 2
    go_up[:half, :] = second[part : part + half, :]
    go_up[half:, :] = below[:half, :]
    go_down[:half, :] = second[2 * part + half :, :]
    go_down[half:, :] = above[half:, :]


def join_kernel(mine, second, below, above, op_a, op_b, _, out, last):
    at = 0
    for piece in (mine, second, below, above, op_a, op_b):
        out[at : at + piece.shape[0], :] = piece[...]
        at += piece.shape[0]
    last[...] = out[at // 2 :, :]


def reorder_kernel(meta, x_own, x_far0, x_far1, x_near, out):
    rows = x_far0.shape[0]
    part = rows // 4
    to = 0
    for c, rep, half in ROW_ORDER:
        size = part if half is None else part // 2
        at = pl.multiple_of(lax.rem(meta[1] + rep, 4) * part + (half or 0) * size, size)
        out[OWN, to : to + size, :] = x_own[pl.ds(c * rows + at, size), :]
        out[FAR, to : to + size, :] = (x_far0, x_far1)[c][pl.ds(at, size), :]
        out[NEAR, to : to + size, :] = x_near[pl.ds(c * rows + at, size), :]
        to += size


def pairs(count, body):
    def step(t, carry):
        body(2 * t)
        body(2 * t + 1)
        return carry

    lax.fori_loop(0, (count + 1) // 2, step, 0)


def gradient(s, rows, src, blk, col, x, w):
    at_i, at_j = block(blk[s]), block(col[s])
    one = over_rows(x[src[s], rows, at_i], w[:, at_j])
    two = over_rows(w[:, at_i], x[OWN, rows, at_j])
    return one + jnp.where(src[s] == OWN, two, 0.0)


def column_dots(x, w):
    return jnp.sum(x.astype(F32) * w.astype(F32), axis=0, keepdims=True)


def first_update_kernel(meta, src, blk, col, x, w_mine, w_most, acc, dots, w):
    rows, cut = w.shape[0], w_mine.shape[0]
    w[:cut, :] = w_mine[...]
    w[cut:, :] = w_most[...]

    def add(s):
        acc[s] = gradient(s, slice(0, rows), src, blk, col, x, w)

    pairs(meta[0], add)
    dots[...] = column_dots(x[OWN, :rows], w[...])


def own_update_kernel(meta, src, blk, col, x, w_all, acc, tiles, diag, dots, out, moved, new_diag, out_v, sem):
    samples = x.shape[1]
    slots = tiles.shape[0]
    rows = slice(samples // 2, samples)
    w = w_all.at[samples // 2 :]
    scale = STEP / (2.0 * samples)
    save = lambda s: pltpu.make_async_copy(out_v.at[s], out.at[s], sem.at[s])

    def finish(s):
        value = tiles[s].astype(F32) - (acc[s] + gradient(s, rows, src, blk, col, x, w)) * scale
        moved[s] = value
        out_v[s] = jnp.where(s < meta[0], soft(value), jnp.zeros((B, B), BF16))

    pairs(meta[0], finish)

    def clear(s, carry):
        out_v[s] = jnp.zeros((B, B), out.dtype)
        return carry

    lax.fori_loop(meta[0], slots, clear, 0)

    def each_done(body):
        def one(s, carry):
            @pl.when(jnp.logical_or(s >= meta[0], src[s] == OWN))
            def _():
                body(s)

            return carry

        lax.fori_loop(0, slots, one, 0)

    each_done(lambda s: save(s).start())
    total = dots[...] + column_dots(x[OWN, rows], w[...])
    d = diag[...]
    new_diag[...] = d - STEP * (total / samples - 1.0 / d)
    each_done(lambda s: save(s).wait())


def other_update_kernel(source, meta, src, blk, col, x, moved, *rest):
    *pieces, _, out, w, out_v, sem = rest
    scale = STEP / (2.0 * x.shape[1])
    if len(pieces) == 1:
        w = pieces[0]
    else:
        at = 0
        for piece in pieces:
            w[at : at + piece.shape[0], :] = piece[...]
            at += piece.shape[0]
    save = lambda s: pltpu.make_async_copy(out_v.at[s], out.at[s], sem.at[s])

    def finish(s):
        grad = over_rows(w[:, block(blk[s])], x[OWN, :, block(col[s])])
        out_v[s] = soft(moved[s] - grad * scale)
        save(s).start()

    each_of(source, src, meta[0], finish)
    each_of(source, src, meta[0], lambda s: save(s).wait())


def shards(samples, theta_tiles, theta_diag, tile_row, tile_col, tile_count):
    count_ns, width = samples.shape
    blocks = width // B
    slots = theta_tiles.shape[0]
    groups = lax.axis_size("blk")
    reps = lax.axis_size("rep")
    group = lax.axis_index("blk")
    r = lax.axis_index("rep")
    rows = count_ns // 2
    part = rows // 4
    dot = 2 * count_ns * B * B

    far = [p for g in range(1, groups - 1, 2) for p in ((g, g + 1), (g + 1, g))]
    near = [p for g in range(0, groups, 2) for p in ((g, g + 1), (g + 1, g))]
    swap_far = lambda v: lax.ppermute(v, "blk", far)
    swap_near = lambda v: lax.ppermute(v, "blk", near)
    up = lambda v, n: lax.ppermute(v, "rep", [(i, (i + n) % reps) for i in range(reps)])

    rel = tile_row // blocks - group
    even = group % 2 == 0
    src = jnp.where(rel == 0, OWN, jnp.where((rel < 0) == even, FAR, NEAR)).astype(jnp.int32)
    blk = (tile_row % blocks).astype(jnp.int32)
    col = tile_col.astype(jnp.int32)
    meta = jnp.stack([tile_count[0], r.astype(jnp.int32)])
    index = (meta, src, blk, col)
    diag = theta_diag[None, :]

    x_near = swap_near(samples)
    (x_half,) = load(samples, [(0, rows)])
    x_own, x_half1 = load(samples, [(0, count_ns), (rows, rows)])
    x_far = [swap_far(x_half), swap_far(x_half1)]

    acc = call(
        own_image_kernel, "own_image", like((count_ns, width), F32), [SMEM] * 4 + [VMEM] * 3, VMEM,
        slots * dot, 4 << 20,
    )(*index, x_own, x_near, theta_tiles)

    parts = [
        call(
            functools.partial(far_image_kernel, c * rows), "far_image",
            [like((part, width), F32)] + [like((part, width), BF16)] * 3,
            [SMEM] * 4 + [VMEM] * 3, [VMEM] * 4, slots * dot // 4, 1 << 20,
            [pltpu.VMEM((rows, width), F32)],
        )(*index, acc, x_far[c], theta_tiles)
        for c in range(2)
    ]
    x_all = call(
        reorder_kernel, "reorder", like((3, count_ns, width), BF16), [SMEM] + [VMEM] * 4, VMEM, 0, 2 << 20,
    )(meta, x_own, *x_far, x_near)
    (own_0, *sends_0), (own_1, *sends_1) = parts
    got_0 = [up(send, k + 1) for k, send in enumerate(sends_0)]
    got_1 = [up(send, k + 1) for k, send in enumerate(sends_1)]
    mine_0 = call(
        first_combine_kernel, "combine", like((part, width), BF16), [SMEM] + [VMEM] * 6, VMEM, 0, 1 << 20,
    )(meta, own_0, *got_0, x_own, diag)
    far_first = swap_far(mine_0)
    mine_1, second = call(
        functools.partial(second_combine_kernel, rows), "combine",
        [like((part, width), BF16), like((3 * part, width), BF16)],
        [SMEM] + [VMEM] * 8 + [ANY] * 2, [VMEM] * 2, 0, 1 << 20,
    )(meta, own_1, *got_1, x_own, diag, up(mine_0, 1), up(mine_0, 3), far_first, x_all)
    far_second = swap_far(second)
    below, above = up(mine_1, 1), up(mine_1, 3)

    acc, dots = call(
        first_update_kernel, "first_update",
        [like(theta_tiles.shape, F32), like((1, width), F32)],
        [SMEM] * 4 + [VMEM] * 3, [VMEM] * 2, slots * dot, 4 << 20,
        [pltpu.VMEM((rows, width), BF16)],
    )(*index, x_all, mine_0, second)

    go_up, go_down = call(
        stack_kernel, "stack", [like((part, width), BF16)] * 2, [VMEM] * 3 + [ANY], [VMEM] * 2, 0, 1 << 20,
    )(second, below, above, acc)
    op_a, op_b = up(go_up, 1), up(go_down, 3)
    w_all, last = call(
        join_kernel, "join", [like((count_ns, width), BF16), like((rows, width), BF16)],
        [VMEM] * 6 + [ANY], [VMEM] * 2, 0, 1 << 20,
    )(mine_0, second, below, above, op_a, op_b, far_second)
    far_last = swap_far(last)
    w_near = swap_near(w_all)

    new_tiles, moved, new_diag = call(
        own_update_kernel, "own_update",
        [like(theta_tiles.shape, BF16), like(theta_tiles.shape, F32), like((1, width), F32)],
        [SMEM] * 4 + [VMEM] * 6, [HBM, VMEM, VMEM], slots * dot, 4 << 20,
        [pltpu.VMEM(theta_tiles.shape, BF16), DMA((slots,))],
    )(*index, x_all, w_all, acc, theta_tiles, diag, dots)

    far_pieces = [far_first, far_second, far_last]
    for source, pieces in ((NEAR, [w_near]), (FAR, far_pieces)):
        new_tiles = call(
            functools.partial(other_update_kernel, source), "other_update", like(theta_tiles.shape, BF16),
            [SMEM] * 4 + [VMEM] * (2 + len(pieces)) + [HBM], HBM, slots * dot // 4, 2 << 20,
            [pltpu.VMEM((count_ns, width), BF16), pltpu.VMEM(theta_tiles.shape, BF16), DMA((slots,))],
            {6 + len(pieces): 0},
        )(*index, x_all, moved, *pieces, new_tiles)
    return new_tiles, new_diag.reshape(width)


def solution(mesh):
    placed = (
        P(None, "blk"),
        P(("blk", "rep"), None, None),
        P("blk"),
        P(("blk", "rep")),
        P(("blk", "rep")),
        P(("blk", "rep")),
    )
    return jax.shard_map(
        shards,
        mesh=mesh,
        in_specs=placed,
        out_specs=(P(("blk", "rep"), None, None), P("blk")),
        check_vma=False,
    )
```

time: 275 us -> 106 us (0.39)
  waiting for transfers between devices: 141 us -> 28.7 us
  local copies, waits for them, and re-layouts: 60.5 us -> 3.2 us
  Pallas kernels: 0 us -> 31.4 us
  matrix products: 26.4 us -> 0 us
  starting transfers between devices: 14.2 us -> 40 us
  other arithmetic: 16.7 us -> 0.09 us
  between operations: 14.8 us -> 1.67 us
    psum x1 -> x0, waiting for transfers between devices: 96.6 us -> none  [shards(): summed = lax.psum(partial_image, 'rep')]
    pallas_call x0 -> x14, Pallas kernels: none -> 31.4 us  [the longest x2 6.07 us: shards(): call(functools.partial(other_update_kernel, source), 'other_update', like...]
    reshape x5 -> x0, local copies, waits for them, and re-layouts: 27.8 us -> none  [the longest x1 8.63 us: shards(): ext_x = ext_x.reshape(count_ns, 3 * blocks, B)]
    dot_general x4 -> x0, matrix products: 26.4 us -> none  [the longest x1 8.41 us: shards(): jnp.einsum('stb,tk->skb', prod, onehot, precision=lax.Precision.HIGHEST)]
    ppermute x4 -> x19, starting transfers between devices: 14.2 us -> 40 us  [the longest x5 23.6 us: shards(): swap_far = lambda v: lax.ppermute(v, 'blk', far)]
    gather x4 -> x0, local copies, waits for them, and re-layouts: 18.2 us -> none  [the longest x1 5.54 us: shards(): w_row = jnp.take(ext_w, rows, axis=1)]
    ppermute x4 -> x19, waiting for transfers between devices: 44 us -> 28.7 us  [the longest x5 14.6 us: shards(): swap_far = lambda v: lax.ppermute(v, 'blk', far)]
    concatenate x2 -> x0, other arithmetic: 11.4 us -> none  [extended(): jnp.concatenate([lax.ppermute(tail, axis, [(i, (i + 1) % count) for i in...]
  transfers between devices with their start and end apart: 5 -> 19, of which waited for: 5 -> 11; matrix products, arithmetic and copies ran while one was open for 5% -> 0% of each run, Pallas kernels for 0% -> 25%
where the time goes in v2:
time: 106 us; the launch traced here: 105 us
  starting transfers between devices  40 us (38%)
  Pallas kernels  31.4 us (30%)
  waiting for transfers between devices  28.7 us (27%)
  local copies, waits for them, and re-layouts  3.2 us (3%)
  between operations  1.67 us (2%)
    ppermute x5, starting transfers between devices, shards(): swap_far = lambda v: lax.ppermute(v, 'blk', far)  23.6 us
    ppermute x12, starting transfers between devices, shards(): lax.ppermute(v, 'rep', [(i, (i + n) % reps) for i in range(reps)])  15.2 us
    ppermute x5, waiting for transfers between devices, shards(): swap_far = lambda v: lax.ppermute(v, 'blk', far)  14.6 us
    ppermute x12, waiting for transfers between devices, shards(): lax.ppermute(v, 'rep', [(i, (i + n) % reps) for i in range(reps)])  14.2 us
    pallas_call x2, Pallas kernels, shards(): call(functools.partial(other_update_kernel, source), 'other_update', like...  6.07 us
    pallas_call x1, Pallas kernels, shards(): call(own_update_kernel, 'own_update', [like(theta_tiles.shape, BF16), lik...  5.53 us
    pallas_call x2, Pallas kernels, shards(): call(functools.partial(far_image_kernel, c * rows), 'far_image', [like((p...  4.92 us
    pallas_call x1, Pallas kernels, shards(): call(own_image_kernel, 'own_image', like((count_ns, width), F32), [SMEM]...  4.64 us
  transfers between devices with their start and end apart: 19, of which 11 were waited for; matrix products, arithmetic and copies ran while one was open for 0% of the time, Pallas kernels for 25%

profile of v2, /device:TPU:103, one launch (start us, length us, event | category | flops | bytes accessed | tf_op | source)
XLA Modules:
  0.0 105.1 jit_solution(5415127347846249246)
XLA Ops:
  0.6 0.8 collective-permute-start.2
  1.4 0.0 copy-start.4
  1.4 1.6 %copy-done.4 = bf16[512,2048]{1,0:T(8,128)(2,1)S(1)} copy-done((bf16[512,2048]{1,0:T(8,128)(2,1)S(1)}, bf16[512,2048]{1,0:T(8,128)(2,1)}, u32[]{:S(2)}) %copy-start.4) | copy-done | bytes 2097176
  3.0 1.0 load.3
  4.0 0.0 copy-start.5
  4.1 0.0 copy-start.3
  4.1 4.6 %collective-permute-start = (bf16[256,2048]{1,0:T(8,128)(2,1)}, bf16[256,2048]{1,0:T(8,128)(2,1)S(1)}, u32[]{:S(2)}, u32[]{:S(2)}) collective-permute-start(bf16[256,2048]{1,0:T(8,128)(2,1)} %load.3), channel_id=1, source_target_pairs={{4,8},{8,4},{12,16},{16,12},{20,24},{24,20},{28,32},{32,28},{36,40... | collective-permute-start | bytes 3145736 | tf_op jit(solution)/shard_map/ppermute | solution.py:275
  8.6 1.2 %load.2 = (bf16[512,2048]{1,0:T(8,128)(2,1)S(1)}, bf16[256,2048]{1,0:T(8,128)(2,1)}) custom-call(bf16[512,2048]{1,0:T(8,128)(2,1)S(1)} %copy-done.4), custom_call_target="tpu_custom_call" | custom-call | flops 2147483648 | bytes 1048576 | tf_op jit(solution)/shard_map/load/pallas_call | solution.py:88
  9.9 4.3 %collective-permute-start.1 = (bf16[256,2048]{1,0:T(8,128)(2,1)}, bf16[256,2048]{1,0:T(8,128)(2,1)}, u32[]{:S(2)}, u32[]{:S(2)}) collective-permute-start(bf16[256,2048]{1,0:T(8,128)(2,1)} %get-tuple-element.24), channel_id=1, source_target_pairs={{4,8},{8,4},{12,16},{16,12},{20,24},{24,20},{28,32},{32,28},{36,40... | collective-permute-start | bytes 3145736 | tf_op jit(solution)/shard_map/ppermute | solution.py:275
  14.8 0.1 pad_add_fusion.meta
  14.9 0.0 copy-done.5
  14.9 0.0 collective-permute-done.2.x_near
  14.9 0.0 copy-done.3
  14.9 0.0 copy-start
  15.0 1.6 %copy-done = bf16[16,256,256]{2,1,0:T(8,128)(2,1)S(1)} copy-done((bf16[16,256,256]{2,1,0:T(8,128)(2,1)S(1)}, bf16[16,256,256]{2,1,0:T(8,128)(2,1)}, u32[]{:S(2)}) %copy-start) | copy-done | bytes 2097176
  16.5 0.0 copy-start.1
  16.5 4.6 %own_image.1.acc = f32[512,2048]{1,0:T(8,128)S(1)} custom-call(s32[2]{0:T(128)S(1)} %pad_add_fusion.meta, s32[16]{0:T(128)S(1)} %get-tuple-element.45.src, s32[16]{0:T(128)S(1)} %get-tuple-element.44.blk, s32[16]{0:T(128)S(1)} %copy-done.3, bf16[512,2048]{1,0:T(8,128)(2,1)S(1)} %get-tuple-element.23.x_own.samples, ...), custom_call_target="tpu_custom_call" | custom-call | flops 1073741824 | bytes 4194304 | tf_op jit(solution)/shard_map/own_image/pallas_call | solution.py:293
  21.2 2.5 %collective-permute-done.x_far0.x_far = bf16[256,2048]{1,0:T(8,128)(2,1)S(1)} collective-permute-done((bf16[256,2048]{1,0:T(8,128)(2,1)}, bf16[256,2048]{1,0:T(8,128)(2,1)S(1)}, u32[]{:S(2)}, u32[]{:S(2)}) %collective-permute-start) | collective-permute-done | bytes 1048608 | tf_op jit(solution)/shard_map/ppermute | solution.py:275
  23.7 0.0 copy-done.1
  23.7 2.1 %far_image.2 = (f32[64,2048]{1,0:T(8,128)S(1)}, bf16[64,2048]{1,0:T(8,128)(2,1)S(1)}, bf16[64,2048]{1,0:T(8,128)(2,1)S(1)}, bf16[64,2048]{1,0:T(8,128)(2,1)S(1)}) custom-call(s32[2]{0:T(128)S(1)} %pad_add_fusion.meta, s32[16]{0:T(128)S(1)} %get-tuple-element.45.src, s32[16]{0:T(128)S(1)} %get-tuple-element.44.blk, s32[16]{0:T(128)S(1)} %copy-done.3, ...), custom_call_target="tpu_custom_call" | custom-call | flops 268435456 | bytes 1048576 | tf_op jit(solution)/shard_map/far_image/pallas_call | solution.py:299
  25.8 1.0 collective-permute-start.3
  26.8 2.4 %collective-permute-start.4 = (bf16[64,2048]{1,0:T(8,128)(2,1)S(1)}, bf16[64,2048]{1,0:T(8,128)(2,1)S(1)}, u32[]{:S(2)}, u32[]{:S(2)}) collective-permute-start(bf16[64,2048]{1,0:T(8,128)(2,1)S(1)} %get-tuple-element.27), channel_id=1, source_target_pairs={{0,2},{1,3},{2,0},{3,1},{4,6},{5,7},{6,4},{7,5},{8,10},{9,11},{10,... | collective-permute-start | bytes 786440 | tf_op jit(solution)/shard_map/ppermute | solution.py:277
  29.3 0.0 copy-start.2
  29.3 1.3 %collective-permute-start.5 = (bf16[64,2048]{1,0:T(8,128)(2,1)S(1)}, bf16[64,2048]{1,0:T(8,128)(2,1)S(1)}, u32[]{:S(2)}, u32[]{:S(2)}) collective-permute-start(bf16[64,2048]{1,0:T(8,128)(2,1)S(1)} %get-tuple-element.28), channel_id=1, source_target_pairs={{0,3},{1,0},{2,1},{3,2},{4,7},{5,4},{6,5},{7,6},{8,11},{9,8},{10,9... | collective-permute-start | bytes 786440 | tf_op jit(solution)/shard_map/ppermute | solution.py:277
  30.5 4.5 %collective-permute-done.1.x_far1.x_far = bf16[256,2048]{1,0:T(8,128)(2,1)} collective-permute-done((bf16[256,2048]{1,0:T(8,128)(2,1)}, bf16[256,2048]{1,0:T(8,128)(2,1)}, u32[]{:S(2)}, u32[]{:S(2)}) %collective-permute-start.1) | collective-permute-done | bytes 1048608 | tf_op jit(solution)/shard_map/ppermute | solution.py:275
  35.1 2.8 %far_image.3 = (f32[64,2048]{1,0:T(8,128)S(1)}, bf16[64,2048]{1,0:T(8,128)(2,1)S(1)}, bf16[64,2048]{1,0:T(8,128)(2,1)S(1)}, bf16[64,2048]{1,0:T(8,128)(2,1)S(1)}) custom-call(s32[2]{0:T(128)S(1)} %pad_add_fusion.meta, s32[16]{0:T(128)S(1)} %get-tuple-element.45.src, s32[16]{0:T(128)S(1)} %get-tuple-element.44.blk, s32[16]{0:T(128)S(1)} %copy-done.3, ...), custom_call_target="tpu_custom_call" | custom-call | flops 268435456 | bytes 1048576 | tf_op jit(solution)/shard_map/far_image/pallas_call | solution.py:299
  37.9 1.0 collective-permute-start.6
  38.8 2.5 %collective-permute-start.7 = (bf16[64,2048]{1,0:T(8,128)(2,1)S(1)}, bf16[64,2048]{1,0:T(8,128)(2,1)S(1)}, u32[]{:S(2)}, u32[]{:S(2)}) collective-permute-start(bf16[64,2048]{1,0:T(8,128)(2,1)S(1)} %get-tuple-element.31), channel_id=1, source_target_pairs={{0,2},{1,3},{2,0},{3,1},{4,6},{5,7},{6,4},{7,5},{8,10},{9,11},{10,... | collective-permute-start | bytes 786440 | tf_op jit(solution)/shard_map/ppermute | solution.py:277
  41.3 0.0 collective-permute-done.3.got_1
  41.3 1.2 %collective-permute-start.8 = (bf16[64,2048]{1,0:T(8,128)(2,1)S(1)}, bf16[64,2048]{1,0:T(8,128)(2,1)S(1)}, u32[]{:S(2)}, u32[]{:S(2)}) collective-permute-start(bf16[64,2048]{1,0:T(8,128)(2,1)S(1)} %get-tuple-element.32), channel_id=1, source_target_pairs={{0,3},{1,0},{2,1},{3,2},{4,7},{5,4},{6,5},{7,6},{8,11},{9,8},{10,9... | collective-permute-start | bytes 786440 | tf_op jit(solution)/shard_map/ppermute | solution.py:277
  42.5 0.0 collective-permute-done.4.got_2
  42.5 0.0 collective-permute-done.5.got_3
  42.5 0.0 copy-done.2
  42.5 0.7 combine.2.w_mine.mine
  43.3 5.6 %collective-permute-start.11 = (bf16[64,2048]{1,0:T(8,128)(2,1)S(1)}, bf16[64,2048]{1,0:T(8,128)(2,1)S(1)}, u32[]{:S(2)}, u32[]{:S(2)}) collective-permute-start(bf16[64,2048]{1,0:T(8,128)(2,1)S(1)} %combine.2.w_mine.mine), channel_id=1, source_target_pairs={{4,8},{8,4},{12,16},{16,12},{20,24},{24,20},{28,32},{32,28},{36,40... | collective-permute-start | bytes 786440 | tf_op jit(solution)/shard_map/ppermute | solution.py:275
  48.9 0.1 collective-permute-start.10
  49.0 0.0 collective-permute-done.6.got_1
  49.0 1.4 %collective-permute-start.9 = (bf16[64,2048]{1,0:T(8,128)(2,1)S(1)}, bf16[64,2048]{1,0:T(8,128)(2,1)S(1)}, u32[]{:S(2)}, u32[]{:S(2)}) collective-permute-start(bf16[64,2048]{1,0:T(8,128)(2,1)S(1)} %combine.2.w_mine.mine), channel_id=1, source_target_pairs={{0,1},{1,2},{2,3},{3,0},{4,5},{5,6},{6,7},{7,4},{8,9},{9,10},{10,1... | collective-permute-start | bytes 786440 | tf_op jit(solution)/shard_map/ppermute | solution.py:277
  50.4 2.3 %reorder.1.__.x = bf16[3,512,2048]{2,1,0:T(8,128)(2,1)S(1)} custom-call(s32[2]{0:T(128)S(1)} %pad_add_fusion.meta, bf16[512,2048]{1,0:T(8,128)(2,1)S(1)} %get-tuple-element.23.x_own.samples, bf16[256,2048]{1,0:T(8,128)(2,1)S(1)} %collective-permute-done.x_far0.x_far, bf16[256,2048]{1,0:T(8,128)(2,1)} %collective-permute-done.1.x_far1.x_far, ...), custom_call_target="tpu_custom_call" | custom-call | bytes 2097152 | tf_op jit(solution)/shard_map/reorder/pallas_call | solution.py:307
  52.8 0.7 collective-permute-done.7.got_2
  53.5 0.1 collective-permute-done.8.got_3
  53.6 0.7 collective-permute-done.11._.rest_0_
  54.3 1.9 %collective-permute-done.10.above = bf16[64,2048]{1,0:T(8,128)(2,1)S(1)} collective-permute-done((bf16[64,2048]{1,0:T(8,128)(2,1)S(1)}, bf16[64,2048]{1,0:T(8,128)(2,1)S(1)}, u32[]{:S(2)}, u32[]{:S(2)}) %collective-permute-start.10) | collective-permute-done | bytes 262176 | tf_op jit(solution)/shard_map/ppermute | solution.py:277
  56.1 0.6 collective-permute-done.9.below
  56.8 0.9 combine.3
  57.6 4.6 %collective-permute-start.16 = (bf16[192,2048]{1,0:T(8,128)(2,1)S(1)}, bf16[192,2048]{1,0:T(8,128)(2,1)S(1)}, u32[]{:S(2)}, u32[]{:S(2)}) collective-permute-start(bf16[192,2048]{1,0:T(8,128)(2,1)S(1)} %get-tuple-element.33.w_most.second), channel_id=1, source_target_pairs={{4,8},{8,4},{12,16},{16,12},{20,24},{24,20},{28,32},{32,28},{36,40... | collective-permute-start | bytes 2359304 | tf_op jit(solution)/shard_map/ppermute | solution.py:275
  62.2 1.5 %collective-permute-start.13 = (bf16[64,2048]{1,0:T(8,128)(2,1)S(1)}, bf16[64,2048]{1,0:T(8,128)(2,1)S(1)}, u32[]{:S(2)}, u32[]{:S(2)}) collective-permute-start(bf16[64,2048]{1,0:T(8,128)(2,1)S(1)} %get-tuple-element.34), channel_id=1, source_target_pairs={{0,3},{1,0},{2,1},{3,2},{4,7},{5,4},{6,5},{7,6},{8,11},{9,8},{10,9... | collective-permute-start | bytes 786440 | tf_op jit(solution)/shard_map/ppermute | solution.py:277
  63.8 0.0 collective-permute-start.12
  63.8 3.8 %first_update.1 = (f32[16,256,256]{2,1,0:T(8,128)S(1)}, f32[1,2048]{1,0:T(1,128)S(1)}) custom-call(s32[2]{0:T(128)S(1)} %pad_add_fusion.meta, s32[16]{0:T(128)S(1)} %get-tuple-element.45.src, s32[16]{0:T(128)S(1)} %get-tuple-element.44.blk, s32[16]{0:T(128)S(1)} %copy-done.3, bf16[3,512,2048]{2,1,0:T(8,128)(2,1)S(1)} %reorder.1.__.x, ...), custom_call_target="tpu_custom_call" | custom-call | flops 1073741824 | bytes 4194304 | tf_op jit(solution)/shard_map/first_update/pallas_call | solution.py:325
  67.6 0.8 collective-permute-done.13.above
  68.4 3.4 %collective-permute-done.12.below = bf16[64,2048]{1,0:T(8,128)(2,1)S(1)} collective-permute-done((bf16[64,2048]{1,0:T(8,128)(2,1)S(1)}, bf16[64,2048]{1,0:T(8,128)(2,1)S(1)}, u32[]{:S(2)}, u32[]{:S(2)}) %collective-permute-start.12) | collective-permute-done | bytes 262176 | tf_op jit(solution)/shard_map/ppermute | solution.py:277
  71.8 0.1 collective-permute-start.14
  71.9 2.7 %collective-permute-start.15 = (bf16[64,2048]{1,0:T(8,128)(2,1)S(1)}, bf16[64,2048]{1,0:T(8,128)(2,1)S(1)}, u32[]{:S(2)}, u32[]{:S(2)}) collective-permute-start(bf16[64,2048]{1,0:T(8,128)(2,1)S(1)} %get-tuple-element.37), channel_id=1, source_target_pairs={{0,3},{1,0},{2,1},{3,2},{4,7},{5,4},{6,5},{7,6},{8,11},{9,8},{10,9... | collective-permute-start | bytes 786440 | tf_op jit(solution)/shard_map/ppermute | solution.py:277
  74.6 6.7 %collective-permute-done.14.op_a = bf16[64,2048]{1,0:T(8,128)(2,1)S(1)} collective-permute-done((bf16[64,2048]{1,0:T(8,128)(2,1)S(1)}, bf16[64,2048]{1,0:T(8,128)(2,1)S(1)}, u32[]{:S(2)}, u32[]{:S(2)}) %collective-permute-start.14) | collective-permute-done | bytes 262176 | tf_op jit(solution)/shard_map/ppermute | solution.py:277
  81.2 0.0 collective-permute-done.15.op_b
  81.2 0.0 collective-permute-done.16._.rest_1_
  81.2 0.2 join.1
  81.5 0.5 collective-permute-start.18
  81.9 4.6 %collective-permute-start.17 = (bf16[256,2048]{1,0:T(8,128)(2,1)S(1)}, bf16[256,2048]{1,0:T(8,128)(2,1)S(1)}, u32[]{:S(2)}, u32[]{:S(2)}) collective-permute-start(bf16[256,2048]{1,0:T(8,128)(2,1)S(1)} %get-tuple-element.41), channel_id=1, source_target_pairs={{4,8},{8,4},{12,16},{16,12},{20,24},{24,20},{28,32},{32,28},{36,40... | collective-permute-start | bytes 3145736 | tf_op jit(solution)/shard_map/ppermute | solution.py:275
  86.5 5.5 %own_update.1 = (bf16[16,256,256]{2,1,0:T(8,128)(2,1)}, f32[16,256,256]{2,1,0:T(8,128)S(1)}, f32[1,2048]{1,0:T(1,128)}) custom-call(s32[2]{0:T(128)S(1)} %pad_add_fusion.meta, s32[16]{0:T(128)S(1)} %get-tuple-element.45.src, s32[16]{0:T(128)S(1)} %get-tuple-element.44.blk, s32[16]{0:T(128)S(1)} %copy-done.3, bf16[3,512,2048]{2,1,0:T(8,128)(2,1)S(1)} %reorder.1.__.x, ...), custom_call_target="tpu_custom_call" | custom-call | flops 1073741824 | bytes 4194304 | tf_op jit(solution)/shard_map/own_update/pallas_call | solution.py:343
  92.0 0.0 collective-permute-done.18.rest_0_
  92.0 2.5 %other_update.2.rest_3_ = bf16[16,256,256]{2,1,0:T(8,128)(2,1)} custom-call(s32[2]{0:T(128)S(1)} %pad_add_fusion.meta, s32[16]{0:T(128)S(1)} %get-tuple-element.45.src, s32[16]{0:T(128)S(1)} %get-tuple-element.44.blk, s32[16]{0:T(128)S(1)} %copy-done.3, bf16[3,512,2048]{2,1,0:T(8,128)(2,1)S(1)} %reorder.1.__.x, ...), custom_call_target="tpu_custom_call", output_to_operand_aliasing={{}: (7, {})} | custom-call | flops 268435456 | bytes 2097152 | tf_op jit(solution)/shard_map/other_update/pallas_call | solution.py:352
  94.5 6.9 %collective-permute-done.17.rest_2_ = bf16[256,2048]{1,0:T(8,128)(2,1)S(1)} collective-permute-done((bf16[256,2048]{1,0:T(8,128)(2,1)S(1)}, bf16[256,2048]{1,0:T(8,128)(2,1)S(1)}, u32[]{:S(2)}, u32[]{:S(2)}) %collective-permute-start.17) | collective-permute-done | bytes 1048608 | tf_op jit(solution)/shard_map/ppermute | solution.py:275
  101.4 3.6 %other_update.3 = bf16[16,256,256]{2,1,0:T(8,128)(2,1)} custom-call(s32[2]{0:T(128)S(1)} %pad_add_fusion.meta, s32[16]{0:T(128)S(1)} %get-tuple-element.45.src, s32[16]{0:T(128)S(1)} %get-tuple-element.44.blk, s32[16]{0:T(128)S(1)} %copy-done.3, bf16[3,512,2048]{2,1,0:T(8,128)(2,1)S(1)} %reorder.1.__.x, ...), custom_call_target="tpu_custom_call", output_to_operand_aliasing={{}: (9, {})} | custom-call | flops 268435456 | bytes 2097152 | tf_op jit(solution)/shard_map/other_update/pallas_call | solution.py:352
  (2 shorter events, 0.0 us)
Async XLA Ops:
  0.6 14.3 %collective-permute-start.2 = (bf16[512,2048]{1,0:T(8,128)(2,1)}, bf16[512,2048]{1,0:T(8,128)(2,1)}, u32[]{:S(2)}, u32[]{:S(2)}) collective-permute-start(bf16[512,2048]{1,0:T(8,128)(2,1)} %src.3), channel_id=1, source_target_pairs={{0,4},{4,0},{8,12},{12,8},{16,20},{20,16},{24,28},{28,24},{32,36},... | collective-permute-start | bytes 6291464 | tf_op jit(solution)/shard_map/ppermute | solution.py:276
  1.4 1.6 %copy-start.4 = (bf16[512,2048]{1,0:T(8,128)(2,1)S(1)}, bf16[512,2048]{1,0:T(8,128)(2,1)}, u32[]{:S(2)}) copy-start(bf16[512,2048]{1,0:T(8,128)(2,1)} %src.3) | copy-start | bytes 6291460
  4.0 10.9 %copy-start.5 = (s32[16]{0:T(128)S(1)}, s32[16]{0:T(128)}, u32[]{:S(2)}) copy-start(s32[16]{0:T(128)} %param.9) | copy-start | bytes 196
  4.1 10.9 %copy-start.3 = (s32[16]{0:T(128)S(1)}, s32[16]{0:T(128)}, u32[]{:S(2)}) copy-start(s32[16]{0:T(128)} %col.13) | copy-start | bytes 196
  4.1 19.6 %collective-permute-start = (bf16[256,2048]{1,0:T(8,128)(2,1)}, bf16[256,2048]{1,0:T(8,128)(2,1)S(1)}, u32[]{:S(2)}, u32[]{:S(2)}) collective-permute-start(bf16[256,2048]{1,0:T(8,128)(2,1)} %load.3), channel_id=1, source_target_pairs={{4,8},{8,4},{12,16},{16,12},{20,24},{24,20},{28,32},{32,28},{36,40... | collective-permute-start | bytes 3145736 | tf_op jit(solution)/shard_map/ppermute | solution.py:275
  9.9 25.2 %collective-permute-start.1 = (bf16[256,2048]{1,0:T(8,128)(2,1)}, bf16[256,2048]{1,0:T(8,128)(2,1)}, u32[]{:S(2)}, u32[]{:S(2)}) collective-permute-start(bf16[256,2048]{1,0:T(8,128)(2,1)} %get-tuple-element.24), channel_id=1, source_target_pairs={{4,8},{8,4},{12,16},{16,12},{20,24},{24,20},{28,32},{32,28},{36,40... | collective-permute-start | bytes 3145736 | tf_op jit(solution)/shard_map/ppermute | solution.py:275
  14.9 1.6 %copy-start = (bf16[16,256,256]{2,1,0:T(8,128)(2,1)S(1)}, bf16[16,256,256]{2,1,0:T(8,128)(2,1)}, u32[]{:S(2)}) copy-start(bf16[16,256,256]{2,1,0:T(8,128)(2,1)} %tiles.7) | copy-start | bytes 6291460
  16.5 7.2 %copy-start.1 = (bf16[16,256,256]{2,1,0:T(8,128)(2,1)S(1)}, bf16[16,256,256]{2,1,0:T(8,128)(2,1)}, u32[]{:S(2)}) copy-start(bf16[16,256,256]{2,1,0:T(8,128)(2,1)} %tiles.7) | copy-start | bytes 6291460
  25.8 15.4 %collective-permute-start.3 = (bf16[64,2048]{1,0:T(8,128)(2,1)S(1)}, bf16[64,2048]{1,0:T(8,128)(2,1)S(1)}, u32[]{:S(2)}, u32[]{:S(2)}) collective-permute-start(bf16[64,2048]{1,0:T(8,128)(2,1)S(1)} %get-tuple-element.26), channel_id=1, source_target_pairs={{0,1},{1,2},{2,3},{3,0},{4,5},{5,6},{6,7},{7,4},{8,9},{9,10},{10,1... | collective-permute-start | bytes 786440 | tf_op jit(solution)/shard_map/ppermute | solution.py:277
  26.8 15.7 %collective-permute-start.4 = (bf16[64,2048]{1,0:T(8,128)(2,1)S(1)}, bf16[64,2048]{1,0:T(8,128)(2,1)S(1)}, u32[]{:S(2)}, u32[]{:S(2)}) collective-permute-start(bf16[64,2048]{1,0:T(8,128)(2,1)S(1)} %get-tuple-element.27), channel_id=1, source_target_pairs={{0,2},{1,3},{2,0},{3,1},{4,6},{5,7},{6,4},{7,5},{8,10},{9,11},{10,... | collective-permute-start | bytes 786440 | tf_op jit(solution)/shard_map/ppermute | solution.py:277
  29.3 13.3 %copy-start.2 = (f32[2048]{0:T(1024)S(1)}, f32[2048]{0:T(1024)}, u32[]{:S(2)}) copy-start(f32[2048]{0:T(1024)} %param.8) | copy-start | bytes 24580
  29.3 13.3 %collective-permute-start.5 = (bf16[64,2048]{1,0:T(8,128)(2,1)S(1)}, bf16[64,2048]{1,0:T(8,128)(2,1)S(1)}, u32[]{:S(2)}, u32[]{:S(2)}) collective-permute-start(bf16[64,2048]{1,0:T(8,128)(2,1)S(1)} %get-tuple-element.28), channel_id=1, source_target_pairs={{0,3},{1,0},{2,1},{3,2},{4,7},{5,4},{6,5},{7,6},{8,11},{9,8},{10,9... | collective-permute-start | bytes 786440 | tf_op jit(solution)/shard_map/ppermute | solution.py:277
  37.9 11.1 %collective-permute-start.6 = (bf16[64,2048]{1,0:T(8,128)(2,1)S(1)}, bf16[64,2048]{1,0:T(8,128)(2,1)S(1)}, u32[]{:S(2)}, u32[]{:S(2)}) collective-permute-start(bf16[64,2048]{1,0:T(8,128)(2,1)S(1)} %get-tuple-element.30), channel_id=1, source_target_pairs={{0,1},{1,2},{2,3},{3,0},{4,5},{5,6},{6,7},{7,4},{8,9},{9,10},{10,1... | collective-permute-start | bytes 786440 | tf_op jit(solution)/shard_map/ppermute | solution.py:277
  38.8 14.7 %collective-permute-start.7 = (bf16[64,2048]{1,0:T(8,128)(2,1)S(1)}, bf16[64,2048]{1,0:T(8,128)(2,1)S(1)}, u32[]{:S(2)}, u32[]{:S(2)}) collective-permute-start(bf16[64,2048]{1,0:T(8,128)(2,1)S(1)} %get-tuple-element.31), channel_id=1, source_target_pairs={{0,2},{1,3},{2,0},{3,1},{4,6},{5,7},{6,4},{7,5},{8,10},{9,11},{10,... | collective-permute-start | bytes 786440 | tf_op jit(solution)/shard_map/ppermute | solution.py:277
  41.3 12.3 %collective-permute-start.8 = (bf16[64,2048]{1,0:T(8,128)(2,1)S(1)}, bf16[64,2048]{1,0:T(8,128)(2,1)S(1)}, u32[]{:S(2)}, u32[]{:S(2)}) collective-permute-start(bf16[64,2048]{1,0:T(8,128)(2,1)S(1)} %get-tuple-element.32), channel_id=1, source_target_pairs={{0,3},{1,0},{2,1},{3,2},{4,7},{5,4},{6,5},{7,6},{8,11},{9,8},{10,9... | collective-permute-start | bytes 786440 | tf_op jit(solution)/shard_map/ppermute | solution.py:277
  43.3 11.0 %collective-permute-start.11 = (bf16[64,2048]{1,0:T(8,128)(2,1)S(1)}, bf16[64,2048]{1,0:T(8,128)(2,1)S(1)}, u32[]{:S(2)}, u32[]{:S(2)}) collective-permute-start(bf16[64,2048]{1,0:T(8,128)(2,1)S(1)} %combine.2.w_mine.mine), channel_id=1, source_target_pairs={{4,8},{8,4},{12,16},{16,12},{20,24},{24,20},{28,32},{32,28},{36,40... | collective-permute-start | bytes 786440 | tf_op jit(solution)/shard_map/ppermute | solution.py:275
  48.9 7.2 %collective-permute-start.10 = (bf16[64,2048]{1,0:T(8,128)(2,1)S(1)}, bf16[64,2048]{1,0:T(8,128)(2,1)S(1)}, u32[]{:S(2)}, u32[]{:S(2)}) collective-permute-start(bf16[64,2048]{1,0:T(8,128)(2,1)S(1)} %combine.2.w_mine.mine), channel_id=1, source_target_pairs={{0,3},{1,0},{2,1},{3,2},{4,7},{5,4},{6,5},{7,6},{8,11},{9,8},{10,9... | collective-permute-start | bytes 786440 | tf_op jit(solution)/shard_map/ppermute | solution.py:277
  49.0 7.8 %collective-permute-start.9 = (bf16[64,2048]{1,0:T(8,128)(2,1)S(1)}, bf16[64,2048]{1,0:T(8,128)(2,1)S(1)}, u32[]{:S(2)}, u32[]{:S(2)}) collective-permute-start(bf16[64,2048]{1,0:T(8,128)(2,1)S(1)} %combine.2.w_mine.mine), channel_id=1, source_target_pairs={{0,1},{1,2},{2,3},{3,0},{4,5},{5,6},{6,7},{7,4},{8,9},{9,10},{10,1... | collective-permute-start | bytes 786440 | tf_op jit(solution)/shard_map/ppermute | solution.py:277
  57.6 23.6 %collective-permute-start.16 = (bf16[192,2048]{1,0:T(8,128)(2,1)S(1)}, bf16[192,2048]{1,0:T(8,128)(2,1)S(1)}, u32[]{:S(2)}, u32[]{:S(2)}) collective-permute-start(bf16[192,2048]{1,0:T(8,128)(2,1)S(1)} %get-tuple-element.33.w_most.second), channel_id=1, source_target_pairs={{4,8},{8,4},{12,16},{16,12},{20,24},{24,20},{28,32},{32,28},{36,40... | collective-permute-start | bytes 2359304 | tf_op jit(solution)/shard_map/ppermute | solution.py:275
  62.2 6.2 %collective-permute-start.13 = (bf16[64,2048]{1,0:T(8,128)(2,1)S(1)}, bf16[64,2048]{1,0:T(8,128)(2,1)S(1)}, u32[]{:S(2)}, u32[]{:S(2)}) collective-permute-start(bf16[64,2048]{1,0:T(8,128)(2,1)S(1)} %get-tuple-element.34), channel_id=1, source_target_pairs={{0,3},{1,0},{2,1},{3,2},{4,7},{5,4},{6,5},{7,6},{8,11},{9,8},{10,9... | collective-permute-start | bytes 786440 | tf_op jit(solution)/shard_map/ppermute | solution.py:277
  63.8 8.0 %collective-permute-start.12 = (bf16[64,2048]{1,0:T(8,128)(2,1)S(1)}, bf16[64,2048]{1,0:T(8,128)(2,1)S(1)}, u32[]{:S(2)}, u32[]{:S(2)}) collective-permute-start(bf16[64,2048]{1,0:T(8,128)(2,1)S(1)} %get-tuple-element.34), channel_id=1, source_target_pairs={{0,1},{1,2},{2,3},{3,0},{4,5},{5,6},{6,7},{7,4},{8,9},{9,10},{10,1... | collective-permute-start | bytes 786440 | tf_op jit(solution)/shard_map/ppermute | solution.py:277
  71.8 9.4 %collective-permute-start.14 = (bf16[64,2048]{1,0:T(8,128)(2,1)S(1)}, bf16[64,2048]{1,0:T(8,128)(2,1)S(1)}, u32[]{:S(2)}, u32[]{:S(2)}) collective-permute-start(bf16[64,2048]{1,0:T(8,128)(2,1)S(1)} %get-tuple-element.36), channel_id=1, source_target_pairs={{0,1},{1,2},{2,3},{3,0},{4,5},{5,6},{6,7},{7,4},{8,9},{9,10},{10,1... | collective-permute-start | bytes 786440 | tf_op jit(solution)/shard_map/ppermute | solution.py:277
  71.9 9.3 %collective-permute-start.15 = (bf16[64,2048]{1,0:T(8,128)(2,1)S(1)}, bf16[64,2048]{1,0:T(8,128)(2,1)S(1)}, u32[]{:S(2)}, u32[]{:S(2)}) collective-permute-start(bf16[64,2048]{1,0:T(8,128)(2,1)S(1)} %get-tuple-element.37), channel_id=1, source_target_pairs={{0,3},{1,0},{2,1},{3,2},{4,7},{5,4},{6,5},{7,6},{8,11},{9,8},{10,9... | collective-permute-start | bytes 786440 | tf_op jit(solution)/shard_map/ppermute | solution.py:277
  81.5 10.6 %collective-permute-start.18 = (bf16[512,2048]{1,0:T(8,128)(2,1)S(1)}, bf16[512,2048]{1,0:T(8,128)(2,1)S(1)}, u32[]{:S(2)}, u32[]{:S(2)}) collective-permute-start(bf16[512,2048]{1,0:T(8,128)(2,1)S(1)} %get-tuple-element.38.w_all), channel_id=1, source_target_pairs={{0,4},{4,0},{8,12},{12,8},{16,20},{20,16},{24,28},{28,24},{32,36},... | collective-permute-start | bytes 6291464 | tf_op jit(solution)/shard_map/ppermute | solution.py:276
  81.9 19.4 %collective-permute-start.17 = (bf16[256,2048]{1,0:T(8,128)(2,1)S(1)}, bf16[256,2048]{1,0:T(8,128)(2,1)S(1)}, u32[]{:S(2)}, u32[]{:S(2)}) collective-permute-start(bf16[256,2048]{1,0:T(8,128)(2,1)S(1)} %get-tuple-element.41), channel_id=1, source_target_pairs={{4,8},{8,4},{12,16},{16,12},{20,24},{24,20},{28,32},{32,28},{36,40... | collective-permute-start | bytes 3145736 | tf_op jit(solution)/shard_map/ppermute | solution.py:275

commit v3 on v2

v3 whole, which is shorter than its diff:
```python
import functools

import jax
import jax.numpy as jnp
from jax import lax
from jax.experimental import pallas as pl
from jax.experimental.pallas import tpu as pltpu
from jax.sharding import PartitionSpec as P

B = 256
STEP = 0.25
PENALTY = 0.5
OWN, FAR, NEAR = 0, 1, 2
HBM = pl.BlockSpec(memory_space=pltpu.HBM)
VMEM = pl.BlockSpec(memory_space=pltpu.VMEM)
SMEM = pl.BlockSpec(memory_space=pltpu.SMEM)
ANY = pl.BlockSpec(memory_space=pl.ANY)
F32, BF16 = jnp.float32, jnp.bfloat16
DMA = pltpu.SemaphoreType.DMA
OVER_ROWS = (((0,), (0,)), ((), ()))
REPS = (0, 3, 1, 2)
CHUNKS = (256, 256)


def call(kernel, name, outs, ins, out_specs, flops, moved, scratch=(), aliases=None, vmem=10):
    return pl.pallas_call(
        kernel,
        out_shape=outs,
        in_specs=ins,
        out_specs=out_specs,
        scratch_shapes=scratch,
        input_output_aliases=aliases or {},
        compiler_params=pltpu.CompilerParams(vmem_limit_bytes=vmem << 20),
        cost_estimate=pl.CostEstimate(flops=flops, bytes_accessed=moved, transcendentals=0),
        name=name,
    )


def like(shape, dtype):
    return jax.ShapeDtypeStruct(shape, dtype)


def block(index):
    return pl.ds(pl.multiple_of(index * B, B), B)


def each_live(count, body):
    def step(s, carry):
        body(s)
        return carry

    lax.fori_loop(0, count, step, 0)


def each_of(source, src, count, body):
    def one(s):
        @pl.when(src[s] == source)
        def _():
            body(s)

    each_live(count, one)


def over_rows(a, b):
    return lax.dot_general(a, b, OVER_ROWS, preferred_element_type=F32)


def soft(moved):
    cut = STEP * PENALTY
    return (moved - jnp.clip(moved, -cut, cut)).astype(BF16)


def load_kernel(firsts, src, *refs):
    n = len(firsts)
    copies = [
        pltpu.make_async_copy(src.at[pl.ds(first, dst.shape[0])], dst, refs[n].at[k])
        for k, (first, dst) in enumerate(zip(firsts, refs[:n], strict=True))
    ]
    for c in copies:
        c.start()
    for c in copies:
        c.wait()


def load(src, ranges, vmem):
    return call(
        functools.partial(load_kernel, [first for first, _ in ranges]), "load",
        [like((rows, src.shape[1]), src.dtype) for _, rows in ranges], [HBM], [VMEM] * len(ranges), 2 << 30, 1 << 20,
        [DMA((len(ranges),))], vmem=vmem,
    )(src)


def own_image_kernel(first, meta, src, blk, col, x_own, x_near, tiles, acc):
    rows = pl.ds(first, acc.shape[0])
    acc[...] = jnp.zeros_like(acc)
    for source, x in ((OWN, x_own), (NEAR, x_near)):

        def add(s):
            acc[:, block(col[s])] += jnp.dot(x[rows, block(blk[s])], tiles[s], preferred_element_type=F32)

        each_of(source, src, meta[0], add)


def far_image_kernel(meta, src, blk, col, acc, x_far, tiles, own, send_1, send_2, send_3, total):
    rows = total.shape[0]
    part = rows // 4
    total[...] = acc[...]

    def add(s):
        total[:, block(col[s])] += jnp.dot(x_far[:, block(blk[s])], tiles[s], preferred_element_type=F32)

    each_of(FAR, src, meta[0], add)
    for k, out in enumerate((own, send_1, send_2, send_3)):
        at = pl.ds(pl.multiple_of(lax.rem(meta[1] + k, 4) * part, part), part)
        out[...] = total[at, :].astype(out.dtype)


def combined(first, meta, own, got, samples, diag):
    part = own.shape[0]
    at = pl.ds(pl.multiple_of(first + meta[1] * part, part), part)
    total = own[...]
    for other in got:
        total += other[:part, :].astype(F32)
    return (total + samples[at, :].astype(F32) * diag[...]).astype(BF16)


def combine_kernel(first, joined, meta, own, got_1, got_2, got_3, samples, diag, *refs):
    out = refs[-1]
    if joined:
        out[:joined, :] = refs[0][...]
    out[joined:, :] = combined(first, meta, own, (got_1, got_2, got_3), samples, diag)


def stack_kernel(mine, below, above, most, rest, go_up, go_down):
    part = below.shape[0]
    half = part // 2
    for n, piece in enumerate((mine, below, above)):
        most[n * part : (n + 1) * part, :] = piece[...]
    rest[...] = most[most.shape[0] - rest.shape[0] :, :]
    go_up[...] = below[:half, :]
    go_down[...] = above[half:, :]


def join_kernel(op_a, op_b, _, out):
    half = op_a.shape[0]
    out[:half, :] = op_a[...]
    out[half:, :] = op_b[...]


def reorder_kernel(meta, x_own, x_near, *refs):
    *x_far, out = refs
    to = 0
    for rep in REPS:
        first = 0
        for far in x_far:
            rows = far.shape[0]
            part = rows // 4
            at = pl.multiple_of(lax.rem(meta[1] + rep, 4) * part, part)
            out[OWN, to : to + part, :] = x_own[pl.ds(first + at, part), :]
            out[FAR, to : to + part, :] = far[pl.ds(at, part), :]
            out[NEAR, to : to + part, :] = x_near[pl.ds(first + at, part), :]
            to += part
            first += rows


def pairs(count, body):
    def step(t, carry):
        body(2 * t)
        body(2 * t + 1)
        return carry

    lax.fori_loop(0, (count + 1) // 2, step, 0)


def gradient(s, rows, src, blk, col, x, w_own, w_near):
    k = src[s]
    at_i, at_j = block(blk[s]), block(col[s])
    one = over_rows(x[k, rows, at_i], w_own[:, at_j])
    two = over_rows(jnp.where(k == NEAR, w_near[:, at_i], w_own[:, at_i]), x[OWN, rows, at_j])
    return one + jnp.where(k == FAR, 0.0, two)


def column_dots(x, w):
    return jnp.sum(x.astype(F32) * w.astype(F32), axis=0, keepdims=True)


def first_update_kernel(meta, src, blk, col, x, w_own, w_near, acc, dots):
    rows = slice(0, w_own.shape[0])

    def add(s):
        acc[s] = gradient(s, rows, src, blk, col, x, w_own, w_near)

    pairs(meta[0], add)
    dots[...] = column_dots(x[OWN, rows], w_own[...])


def own_update_kernel(meta, src, blk, col, x, w_op, near_op, acc, tiles, diag, dots, out, moved, new_diag, out_v, sem):
    samples = x.shape[1]
    slots = tiles.shape[0]
    rows = slice(samples - w_op.shape[0], samples)
    scale = STEP / (2.0 * samples)
    count = meta[0]
    even = (count + 1) // 2 * 2
    save = lambda s: pltpu.make_async_copy(out_v.at[s], out.at[s], sem.at[s])

    def clear(s, carry):
        out_v[s] = jnp.zeros((B, B), out.dtype)
        save(s).start()
        return carry

    lax.fori_loop(even, slots, clear, 0)

    def done_here(s):
        return jnp.logical_or(s >= count, src[s] != FAR)

    def finish(s):
        value = tiles[s].astype(F32) - (acc[s] + gradient(s, rows, src, blk, col, x, w_op, near_op)) * scale
        moved[s] = value
        out_v[s] = jnp.where(s < count, soft(value), jnp.zeros((B, B), BF16))

    def step(t, carry):
        finish(2 * t)
        finish(2 * t + 1)
        for s in (2 * t, 2 * t + 1):

            @pl.when(done_here(s))
            def _():
                save(s).start()

        return carry

    lax.fori_loop(0, even // 2, step, 0)
    total = dots[...] + column_dots(x[OWN, rows], w_op[...])
    d = diag[...]
    new_diag[...] = d - STEP * (total / samples - 1.0 / d)

    def end(s, carry):
        @pl.when(done_here(s))
        def _():
            save(s).wait()

        return carry

    lax.fori_loop(0, slots, end, 0)


def far_update_kernel(meta, src, blk, col, x, moved, *rest):
    *pieces, _, out, w, out_v, sem = rest
    scale = STEP / (2.0 * x.shape[1])
    at = 0
    for piece in pieces:
        w[at : at + piece.shape[0], :] = piece[...]
        at += piece.shape[0]
    save = lambda s: pltpu.make_async_copy(out_v.at[s], out.at[s], sem.at[s])

    def finish(s):
        grad = over_rows(w[:, block(blk[s])], x[OWN, :, block(col[s])])
        out_v[s] = soft(moved[s] - grad * scale)
        save(s).start()

    each_of(FAR, src, meta[0], finish)
    each_of(FAR, src, meta[0], lambda s: save(s).wait())


def shards(samples, theta_tiles, theta_diag, tile_row, tile_col, tile_count):
    count_ns, width = samples.shape
    blocks = width // B
    slots = theta_tiles.shape[0]
    groups = lax.axis_size("blk")
    reps = lax.axis_size("rep")
    group = lax.axis_index("blk")
    r = lax.axis_index("rep")
    quarter = count_ns // 4
    firsts = [sum(CHUNKS[:c]) for c in range(len(CHUNKS))]
    dot = 2 * count_ns * B * B

    far = [p for g in range(1, groups - 1, 2) for p in ((g, g + 1), (g + 1, g))]
    near = [p for g in range(0, groups, 2) for p in ((g, g + 1), (g + 1, g))]
    swap_far = lambda v: lax.ppermute(v, "blk", far)
    swap_near = lambda v: lax.ppermute(v, "blk", near)
    up = lambda v, n: lax.ppermute(v, "rep", [(i, (i + n) % reps) for i in range(reps)])

    rel = tile_row // blocks - group
    even = group % 2 == 0
    src = jnp.where(rel == 0, OWN, jnp.where((rel < 0) == even, FAR, NEAR)).astype(jnp.int32)
    blk = (tile_row % blocks).astype(jnp.int32)
    col = tile_col.astype(jnp.int32)
    meta = jnp.stack([tile_count[0], r.astype(jnp.int32)])
    index = (meta, src, blk, col)
    diag = theta_diag[None, :]

    x_near = swap_near(samples)
    (x_first,) = load(samples, [(0, CHUNKS[0])], 62)
    x_own, *x_rest = load(samples, [(0, count_ns), *zip(firsts[1:], CHUNKS[1:], strict=True)], 10)
    x_far = [swap_far(x) for x in (x_first, *x_rest)]

    accs = [
        call(
            functools.partial(own_image_kernel, first), "own_image", like((rows, width), F32),
            [SMEM] * 4 + [VMEM] * 3, VMEM, slots * dot, 4 << 20,
        )(*index, x_own, x_near, theta_tiles)
        for first, rows in zip(firsts, CHUNKS, strict=True)
    ]
    x_all = call(
        reorder_kernel, "reorder", like((3, count_ns, width), BF16), [SMEM] + [VMEM] * (2 + len(CHUNKS)), VMEM,
        0, 2 << 20,
    )(meta, x_own, x_near, *x_far)

    joined, done, before = [], 0, []
    for c, (first, rows) in enumerate(zip(firsts, CHUNKS, strict=True)):
        part = rows // 4
        own, *sends = call(
            far_image_kernel, "far_image",
            [like((part, width), F32)] + [like((part, width), BF16)] * 3,
            [SMEM] * 4 + [VMEM] * 3, [VMEM] * 4, slots * dot // 4, 1 << 20,
            [pltpu.VMEM((rows, width), F32)],
        )(*index, accs[c], x_far[c], theta_tiles)
        got = [up(send, k + 1) for k, send in enumerate(sends)]
        if c + 1 == len(CHUNKS):
            far_first = swap_far(joined[0])
            before = [far_first, x_all]
        joined = [
            call(
                functools.partial(combine_kernel, first, done), "combine", like((done + part, width), BF16),
                [SMEM] + [VMEM] * (6 + len(joined)) + [ANY] * len(before), VMEM, 0, 1 << 20,
            )(meta, own, *got, x_own, diag, *joined, *before)
        ]
        done += part
    w_mine = joined[0]
    w_most, w_rest, go_up, go_down = call(
        stack_kernel, "stack",
        [like((3 * quarter, width), BF16), like((2 * quarter + part, width), BF16)]
        + [like((quarter // 2, width), BF16)] * 2,
        [VMEM] * 3, [VMEM] * 4, 0, 1 << 20,
    )(w_mine, up(w_mine, 1), up(w_mine, 3))
    far_rest, near_most = swap_far(w_rest), swap_near(w_most)
    op_a, op_b = up(go_up, 1), up(go_down, 3)

    acc, dots = call(
        first_update_kernel, "first_update",
        [like(theta_tiles.shape, F32), like((1, width), F32)],
        [SMEM] * 4 + [VMEM] * 3, [VMEM] * 2, slots * dot, 4 << 20,
    )(*index, x_all, w_most, near_most)

    w_op = call(
        join_kernel, "join", like((quarter, width), BF16), [VMEM] * 2 + [ANY], VMEM, 0, 1 << 20,
    )(op_a, op_b, acc)
    far_op = swap_far(w_op)

    new_tiles, moved, new_diag = call(
        own_update_kernel, "own_update",
        [like(theta_tiles.shape, BF16), like(theta_tiles.shape, F32), like((1, width), F32)],
        [SMEM] * 4 + [VMEM] * 7, [HBM, VMEM, VMEM], slots * dot, 4 << 20,
        [pltpu.VMEM(theta_tiles.shape, BF16), DMA((slots,))],
    )(*index, x_all, w_op, swap_near(w_op), acc, theta_tiles, diag, dots)

    far_pieces = [far_first, far_rest, far_op]
    new_tiles = call(
        far_update_kernel, "far_update", like(theta_tiles.shape, BF16),
        [SMEM] * 4 + [VMEM] * (2 + len(far_pieces)) + [HBM], HBM, slots * dot // 4, 2 << 20,
        [pltpu.VMEM((count_ns, width), BF16), pltpu.VMEM(theta_tiles.shape, BF16), DMA((slots,))],
        {6 + len(far_pieces): 0},
    )(*index, x_all, moved, *far_pieces, new_tiles)
    return new_tiles, new_diag.reshape(width)


def solution(mesh):
    placed = (
        P(None, "blk"),
        P(("blk", "rep"), None, None),
        P("blk"),
        P(("blk", "rep")),
        P(("blk", "rep")),
        P(("blk", "rep")),
    )
    return jax.shard_map(
        shards,
        mesh=mesh,
        in_specs=placed,
        out_specs=(P(("blk", "rep"), None, None), P("blk")),
        check_vma=False,
    )
```

time: 106 us -> 99.2 us (0.936)
  waiting for transfers between devices: 28.7 us -> 23.1 us
  starting transfers between devices: 40 us -> 36.5 us
  Pallas kernels: 31.4 us -> 32.9 us
  local copies, waits for them, and re-layouts: 3.2 us -> 4.52 us
    ppermute x5, waiting for transfers between devices: 14.6 us -> 8.85 us  [shards(): swap_far = lambda v: lax.ppermute(v, 'blk', far)]
    ppermute x5, starting transfers between devices: 23.6 us -> 21.2 us  [shards(): swap_far = lambda v: lax.ppermute(v, 'blk', far)]
    unnamed x12 -> x16, local copies, waits for them, and re-layouts: 3.2 us -> 4.52 us
    ppermute x12 -> x10, starting transfers between devices: 15.2 us -> 13.9 us  [shards(): lax.ppermute(v, 'rep', [(i, (i + n) % reps) for i in range(reps)])]
    pallas_call x2, Pallas kernels: 2.25 us -> 3.45 us  [load(): call(functools.partial(load_kernel, [first for first, _ in ranges]), 'loa...]
    pallas_call x1, Pallas kernels: 3.8 us -> 4.87 us  [shards(): call(first_update_kernel, 'first_update', [like(theta_tiles.shape, F32),...]
    ppermute x12 -> x10, waiting for transfers between devices: 14.2 us -> 14.3 us  [shards(): lax.ppermute(v, 'rep', [(i, (i + n) % reps) for i in range(reps)])]
  transfers between devices with their start and end apart: 19 -> 18, of which waited for: 11 -> 9; matrix products, arithmetic and copies ran while one was open for 0% -> 0% of each run, Pallas kernels for 25% -> 30%
where the time goes in v3:
time: 99.2 us; the launch traced here: 98.7 us
  starting transfers between devices  36.5 us (37%)
  Pallas kernels  32.9 us (33%)
  waiting for transfers between devices  23.1 us (23%)
  local copies, waits for them, and re-layouts  4.52 us (5%)
  between operations  1.53 us (2%)
    ppermute x5, starting transfers between devices, shards(): swap_far = lambda v: lax.ppermute(v, 'blk', far)  21.2 us
    ppermute x10, waiting for transfers between devices, shards(): lax.ppermute(v, 'rep', [(i, (i + n) % reps) for i in range(reps)])  14.3 us
    ppermute x10, starting transfers between devices, shards(): lax.ppermute(v, 'rep', [(i, (i + n) % reps) for i in range(reps)])  13.9 us
    pallas_call x2, Pallas kernels, shards(): call(functools.partial(own_image_kernel, first), 'own_image', like((rows,...  9.07 us
    ppermute x5, waiting for transfers between devices, shards(): swap_far = lambda v: lax.ppermute(v, 'blk', far)  8.85 us
    pallas_call x1, Pallas kernels, shards(): call(own_update_kernel, 'own_update', [like(theta_tiles.shape, BF16), lik...  5.13 us
    pallas_call x1, Pallas kernels, shards(): call(first_update_kernel, 'first_update', [like(theta_tiles.shape, F32),...  4.87 us
    unnamed x16, local copies, waits for them, and re-layouts  4.52 us
  transfers between devices with their start and end apart: 18, of which 9 were waited for; matrix products, arithmetic and copies ran while one was open for 0% of the time, Pallas kernels for 30%

profile of v3, /device:TPU:103, one launch (start us, length us, event | category | flops | bytes accessed | tf_op | source)
XLA Modules:
  0.0 98.7 jit_solution(9408036222199006371)
XLA Ops:
  0.6 0.8 collective-permute-start
  1.4 2.2 %load.3 = bf16[256,2048]{1,0:T(8,128)(2,1)} custom-call(bf16[512,2048]{1,0:T(8,128)(2,1)} %src.3), custom_call_target="tpu_custom_call" | custom-call | flops 2147483648 | bytes 1048576 | tf_op jit(solution)/shard_map/load/pallas_call | solution.py:86
  3.6 0.0 copy-start
  3.7 0.0 copy-start.5
  3.7 4.7 %collective-permute-start.1 = (bf16[256,2048]{1,0:T(8,128)(2,1)}, bf16[256,2048]{1,0:T(8,128)(2,1)S(1)}, u32[]{:S(2)}, u32[]{:S(2)}) collective-permute-start(bf16[256,2048]{1,0:T(8,128)(2,1)} %load.3), channel_id=1, source_target_pairs={{4,8},{8,4},{12,16},{16,12},{20,24},{24,20},{28,32},{32,28},{36,40... | collective-permute-start | bytes 3145736 | tf_op jit(solution)/shard_map/ppermute | solution.py:279
  8.4 0.0 copy-start.6
  8.4 1.6 %copy-done.6 = bf16[512,2048]{1,0:T(8,128)(2,1)S(1)} copy-done((bf16[512,2048]{1,0:T(8,128)(2,1)S(1)}, bf16[512,2048]{1,0:T(8,128)(2,1)}, u32[]{:S(2)}) %copy-start.6) | copy-done | bytes 2097176
  10.0 1.2 %load.2 = (bf16[512,2048]{1,0:T(8,128)(2,1)S(1)}, bf16[256,2048]{1,0:T(8,128)(2,1)}) custom-call(bf16[512,2048]{1,0:T(8,128)(2,1)S(1)} %copy-done.6), custom_call_target="tpu_custom_call" | custom-call | flops 2147483648 | bytes 1048576 | tf_op jit(solution)/shard_map/load/pallas_call | solution.py:86
  11.2 0.0 copy-start.1
  11.2 1.3 %copy-done.1 = bf16[512,2048]{1,0:T(8,128)(2,1)} copy-done((bf16[512,2048]{1,0:T(8,128)(2,1)}, bf16[512,2048]{1,0:T(8,128)(2,1)S(1)}, u32[]{:S(2)}) %copy-start.1) | copy-done | bytes 2097176
  12.5 4.3 %collective-permute-start.2 = (bf16[256,2048]{1,0:T(8,128)(2,1)}, bf16[256,2048]{1,0:T(8,128)(2,1)}, u32[]{:S(2)}, u32[]{:S(2)}) collective-permute-start(bf16[256,2048]{1,0:T(8,128)(2,1)} %get-tuple-element.22), channel_id=1, source_target_pairs={{4,8},{8,4},{12,16},{16,12},{20,24},{24,20},{28,32},{32,28},{36,40... | collective-permute-start | bytes 3145736 | tf_op jit(solution)/shard_map/ppermute | solution.py:279
  17.5 0.1 pad_add_fusion.meta
  17.6 0.0 copy-done.7
  17.6 0.0 collective-permute-done.x_near
  17.6 0.0 copy-done
  17.6 0.0 copy-done.5
  17.6 0.0 copy-start.2
  17.6 1.6 %copy-done.2 = bf16[512,2048]{1,0:T(8,128)(2,1)S(1)} copy-done((bf16[512,2048]{1,0:T(8,128)(2,1)S(1)}, bf16[512,2048]{1,0:T(8,128)(2,1)}, u32[]{:S(2)}) %copy-start.2) | copy-done | bytes 2097176
  19.2 4.5 %own_image.3.acc = f32[256,2048]{1,0:T(8,128)S(1)} custom-call(s32[2]{0:T(128)S(1)} %pad_add_fusion.meta, s32[16]{0:T(128)S(1)} %get-tuple-element.41.src, s32[16]{0:T(128)S(1)} %get-tuple-element.40.blk, s32[16]{0:T(128)S(1)} %copy-done.5, bf16[512,2048]{1,0:T(8,128)(2,1)S(1)} %copy-done.2, bf16[512,2048]{1,0:T(8,128)(2,1)} %collective-permute-done.x_near, ...), custom_call_target="tpu_custom_call" | custom-call | flops 1073741824 | bytes 4194304 | tf_op jit(solution)/shard_map/own_image/pallas_call | solution.py:298
  23.7 0.0 copy-start.3
  23.7 0.0 collective-permute-done.1.refs_0_.x_far
  23.8 1.6 %far_image.3 = (f32[64,2048]{1,0:T(8,128)S(1)}, bf16[64,2048]{1,0:T(8,128)(2,1)S(1)}, bf16[64,2048]{1,0:T(8,128)(2,1)S(1)}, bf16[64,2048]{1,0:T(8,128)(2,1)S(1)}) custom-call(s32[2]{0:T(128)S(1)} %pad_add_fusion.meta, s32[16]{0:T(128)S(1)} %get-tuple-element.41.src, s32[16]{0:T(128)S(1)} %get-tuple-element.40.blk, s32[16]{0:T(128)S(1)} %copy-done.5, ...), custom_call_target="tpu_custom_call" | custom-call | flops 268435456 | bytes 1048576 | tf_op jit(solution)/shard_map/far_image/pallas_call | solution.py:312
  25.3 1.4 %collective-permute-start.6 = (bf16[64,2048]{1,0:T(8,128)(2,1)S(1)}, bf16[64,2048]{1,0:T(8,128)(2,1)S(1)}, u32[]{:S(2)}, u32[]{:S(2)}) collective-permute-start(bf16[64,2048]{1,0:T(8,128)(2,1)S(1)} %get-tuple-element.28), channel_id=1, source_target_pairs={{0,1},{1,2},{2,3},{3,0},{4,5},{5,6},{6,7},{7,4},{8,9},{9,10},{10,1... | collective-permute-start | bytes 786440 | tf_op jit(solution)/shard_map/ppermute | solution.py:281
  26.8 2.1 %collective-permute-start.7 = (bf16[64,2048]{1,0:T(8,128)(2,1)S(1)}, bf16[64,2048]{1,0:T(8,128)(2,1)S(1)}, u32[]{:S(2)}, u32[]{:S(2)}) collective-permute-start(bf16[64,2048]{1,0:T(8,128)(2,1)S(1)} %get-tuple-element.29), channel_id=1, source_target_pairs={{0,2},{1,3},{2,0},{3,1},{4,6},{5,7},{6,4},{7,5},{8,10},{9,11},{10,... | collective-permute-start | bytes 786440 | tf_op jit(solution)/shard_map/ppermute | solution.py:281
  28.9 0.5 collective-permute-start.8
  29.4 0.0 copy-done.3
  29.4 4.5 %own_image.2.acc = f32[256,2048]{1,0:T(8,128)S(1)} custom-call(s32[2]{0:T(128)S(1)} %pad_add_fusion.meta, s32[16]{0:T(128)S(1)} %get-tuple-element.41.src, s32[16]{0:T(128)S(1)} %get-tuple-element.40.blk, s32[16]{0:T(128)S(1)} %copy-done.5, bf16[512,2048]{1,0:T(8,128)(2,1)S(1)} %copy-done.3, bf16[512,2048]{1,0:T(8,128)(2,1)} %collective-permute-done.x_near, ...), custom_call_target="tpu_custom_call" | custom-call | flops 1073741824 | bytes 4194304 | tf_op jit(solution)/shard_map/own_image/pallas_call | solution.py:298
  33.9 0.0 copy-start.4
  33.9 0.8 collective-permute-done.2.refs_1_.x_far
  34.8 2.3 %far_image.2 = (f32[64,2048]{1,0:T(8,128)S(1)}, bf16[64,2048]{1,0:T(8,128)(2,1)S(1)}, bf16[64,2048]{1,0:T(8,128)(2,1)S(1)}, bf16[64,2048]{1,0:T(8,128)(2,1)S(1)}) custom-call(s32[2]{0:T(128)S(1)} %pad_add_fusion.meta, s32[16]{0:T(128)S(1)} %get-tuple-element.41.src, s32[16]{0:T(128)S(1)} %get-tuple-element.40.blk, s32[16]{0:T(128)S(1)} %copy-done.5, ...), custom_call_target="tpu_custom_call" | custom-call | flops 268435456 | bytes 1048576 | tf_op jit(solution)/shard_map/far_image/pallas_call | solution.py:312
  37.0 1.7 %collective-permute-start.3 = (bf16[64,2048]{1,0:T(8,128)(2,1)S(1)}, bf16[64,2048]{1,0:T(8,128)(2,1)S(1)}, u32[]{:S(2)}, u32[]{:S(2)}) collective-permute-start(bf16[64,2048]{1,0:T(8,128)(2,1)S(1)} %get-tuple-element.24), channel_id=1, source_target_pairs={{0,1},{1,2},{2,3},{3,0},{4,5},{5,6},{6,7},{7,4},{8,9},{9,10},{10,1... | collective-permute-start | bytes 786440 | tf_op jit(solution)/shard_map/ppermute | solution.py:281
  38.8 2.1 %collective-permute-start.4 = (bf16[64,2048]{1,0:T(8,128)(2,1)S(1)}, bf16[64,2048]{1,0:T(8,128)(2,1)S(1)}, u32[]{:S(2)}, u32[]{:S(2)}) collective-permute-start(bf16[64,2048]{1,0:T(8,128)(2,1)S(1)} %get-tuple-element.25), channel_id=1, source_target_pairs={{0,2},{1,3},{2,0},{3,1},{4,6},{5,7},{6,4},{7,5},{8,10},{9,11},{10,... | collective-permute-start | bytes 786440 | tf_op jit(solution)/shard_map/ppermute | solution.py:281
  40.9 0.0 collective-permute-done.6.got_1
  40.9 0.5 collective-permute-start.5
  41.4 0.0 collective-permute-done.7.got_2
  41.4 0.0 collective-permute-done.8.got_3
  41.4 0.7 combine.2.refs_0_
  42.1 5.6 %collective-permute-start.9 = (bf16[64,2048]{1,0:T(8,128)(2,1)S(1)}, bf16[64,2048]{1,0:T(8,128)(2,1)S(1)}, u32[]{:S(2)}, u32[]{:S(2)}) collective-permute-start(bf16[64,2048]{1,0:T(8,128)(2,1)S(1)} %combine.2.refs_0_), channel_id=1, source_target_pairs={{4,8},{8,4},{12,16},{16,12},{20,24},{24,20},{28,32},{32,28},{36,40... | collective-permute-start | bytes 786440 | tf_op jit(solution)/shard_map/ppermute | solution.py:279
  47.8 2.3 %reorder.1.refs_2_.x = bf16[3,512,2048]{2,1,0:T(8,128)(2,1)S(1)} custom-call(s32[2]{0:T(128)S(1)} %pad_add_fusion.meta, bf16[512,2048]{1,0:T(8,128)(2,1)S(1)} %copy-done.3, bf16[512,2048]{1,0:T(8,128)(2,1)} %collective-permute-done.x_near, bf16[256,2048]{1,0:T(8,128)(2,1)S(1)} %collective-permute-done.1.refs_0_.x_far, ...), custom_call_target="tpu_custom_call" | custom-call | bytes 2097152 | tf_op jit(solution)/shard_map/reorder/pallas_call | solution.py:304
  50.1 0.0 collective-permute-done.3.got_1
  50.1 0.1 collective-permute-done.4.got_2
  50.2 0.9 collective-permute-done.5.got_3
  51.1 2.1 %collective-permute-done.9.refs_1_.rest_0_ = bf16[64,2048]{1,0:T(8,128)(2,1)S(1)} collective-permute-done((bf16[64,2048]{1,0:T(8,128)(2,1)S(1)}, bf16[64,2048]{1,0:T(8,128)(2,1)S(1)}, u32[]{:S(2)}, u32[]{:S(2)}) %collective-permute-start.9) | collective-permute-done | bytes 262176 | tf_op jit(solution)/shard_map/ppermute | solution.py:279
  53.2 0.7 combine.3.mine
  53.9 1.1 %collective-permute-start.10 = (bf16[128,2048]{1,0:T(8,128)(2,1)S(1)}, bf16[128,2048]{1,0:T(8,128)(2,1)S(1)}, u32[]{:S(2)}, u32[]{:S(2)}) collective-permute-start(bf16[128,2048]{1,0:T(8,128)(2,1)S(1)} %combine.3.mine), channel_id=1, source_target_pairs={{0,1},{1,2},{2,3},{3,0},{4,5},{5,6},{6,7},{7,4},{8,9},{9,10},{10,1... | collective-permute-start | bytes 1572872 | tf_op jit(solution)/shard_map/ppermute | solution.py:281
  55.0 1.7 %collective-permute-start.11 = (bf16[128,2048]{1,0:T(8,128)(2,1)S(1)}, bf16[128,2048]{1,0:T(8,128)(2,1)S(1)}, u32[]{:S(2)}, u32[]{:S(2)}) collective-permute-start(bf16[128,2048]{1,0:T(8,128)(2,1)S(1)} %combine.3.mine), channel_id=1, source_target_pairs={{0,3},{1,0},{2,1},{3,2},{4,7},{5,4},{6,5},{7,6},{8,11},{9,8},{10,9... | collective-permute-start | bytes 1572872 | tf_op jit(solution)/shard_map/ppermute | solution.py:281
  56.7 10.6 %collective-permute-done.10.below = bf16[128,2048]{1,0:T(8,128)(2,1)S(1)} collective-permute-done((bf16[128,2048]{1,0:T(8,128)(2,1)S(1)}, bf16[128,2048]{1,0:T(8,128)(2,1)S(1)}, u32[]{:S(2)}, u32[]{:S(2)}) %collective-permute-start.10) | collective-permute-done | bytes 524320 | tf_op jit(solution)/shard_map/ppermute | solution.py:281
  67.2 0.7 collective-permute-done.11.above
  67.9 0.2 stack.9
  68.2 0.1 collective-permute-start.14
  68.3 2.8 %collective-permute-start.16 = (bf16[320,2048]{1,0:T(8,128)(2,1)S(1)}, bf16[320,2048]{1,0:T(8,128)(2,1)S(1)}, u32[]{:S(2)}, u32[]{:S(2)}) collective-permute-start(bf16[320,2048]{1,0:T(8,128)(2,1)S(1)} %get-tuple-element.37), channel_id=1, source_target_pairs={{4,8},{8,4},{12,16},{16,12},{20,24},{24,20},{28,32},{32,28},{36,40... | collective-permute-start | bytes 3932168 | tf_op jit(solution)/shard_map/ppermute | solution.py:279
  71.1 0.2 collective-permute-start.12
  71.3 2.6 %collective-permute-start.13 = (bf16[64,2048]{1,0:T(8,128)(2,1)S(1)}, bf16[64,2048]{1,0:T(8,128)(2,1)S(1)}, u32[]{:S(2)}, u32[]{:S(2)}) collective-permute-start(bf16[64,2048]{1,0:T(8,128)(2,1)S(1)} %get-tuple-element.32), channel_id=1, source_target_pairs={{0,3},{1,0},{2,1},{3,2},{4,7},{5,4},{6,5},{7,6},{8,11},{9,8},{10,9... | collective-permute-start | bytes 786440 | tf_op jit(solution)/shard_map/ppermute | solution.py:281
  73.9 0.0 collective-permute-done.14.w_near
  73.9 4.9 %first_update.1 = (f32[16,256,256]{2,1,0:T(8,128)S(1)}, f32[1,2048]{1,0:T(1,128)S(1)}) custom-call(s32[2]{0:T(128)S(1)} %pad_add_fusion.meta, s32[16]{0:T(128)S(1)} %get-tuple-element.41.src, s32[16]{0:T(128)S(1)} %get-tuple-element.40.blk, s32[16]{0:T(128)S(1)} %copy-done.5, bf16[3,512,2048]{2,1,0:T(8,128)(2,1)S(1)} %reorder.1.refs_2_.x, ...), custom_call_target="tpu_custom_call" | custom-call | flops 1073741824 | bytes 4194304 | tf_op jit(solution)/shard_map/first_update/pallas_call | solution.py:339
  78.7 2.0 %collective-permute-done.12.op_a = bf16[64,2048]{1,0:T(8,128)(2,1)S(1)} collective-permute-done((bf16[64,2048]{1,0:T(8,128)(2,1)S(1)}, bf16[64,2048]{1,0:T(8,128)(2,1)S(1)}, u32[]{:S(2)}, u32[]{:S(2)}) %collective-permute-start.12) | collective-permute-done | bytes 262176 | tf_op jit(solution)/shard_map/ppermute | solution.py:281
  80.7 0.0 collective-permute-done.13.op_b
  80.7 0.5 collective-permute-start.15
  81.2 3.8 %collective-permute-start.17 = (bf16[128,2048]{1,0:T(8,128)(2,1)S(1)}, bf16[128,2048]{1,0:T(8,128)(2,1)S(1)}, u32[]{:S(2)}, u32[]{:S(2)}) collective-permute-start(bf16[128,2048]{1,0:T(8,128)(2,1)S(1)} %join.1.w_op), channel_id=1, source_target_pairs={{4,8},{8,4},{12,16},{16,12},{20,24},{24,20},{28,32},{32,28},{36,40... | collective-permute-start | bytes 1572872 | tf_op jit(solution)/shard_map/ppermute | solution.py:279
  85.1 0.0 collective-permute-done.15.near_op
  85.1 5.1 %own_update.1 = (bf16[16,256,256]{2,1,0:T(8,128)(2,1)}, f32[16,256,256]{2,1,0:T(8,128)S(1)}, f32[1,2048]{1,0:T(1,128)}) custom-call(s32[2]{0:T(128)S(1)} %pad_add_fusion.meta, s32[16]{0:T(128)S(1)} %get-tuple-element.41.src, s32[16]{0:T(128)S(1)} %get-tuple-element.40.blk, s32[16]{0:T(128)S(1)} %copy-done.5, bf16[3,512,2048]{2,1,0:T(8,128)(2,1)S(1)} %reorder.1.refs_2_.x, ...), custom_call_target="tpu_custom_call" | custom-call | flops 1073741824 | bytes 4194304 | tf_op jit(solution)/shard_map/own_update/pallas_call | solution.py:350
  90.2 0.3 collective-permute-done.16.rest_1_
  90.5 5.6 %collective-permute-done.17.rest_2_ = bf16[128,2048]{1,0:T(8,128)(2,1)S(1)} collective-permute-done((bf16[128,2048]{1,0:T(8,128)(2,1)S(1)}, bf16[128,2048]{1,0:T(8,128)(2,1)S(1)}, u32[]{:S(2)}, u32[]{:S(2)}) %collective-permute-start.17) | collective-permute-done | bytes 524320 | tf_op jit(solution)/shard_map/ppermute | solution.py:279
  96.2 2.6 %far_update.1 = bf16[16,256,256]{2,1,0:T(8,128)(2,1)} custom-call(s32[2]{0:T(128)S(1)} %pad_add_fusion.meta, s32[16]{0:T(128)S(1)} %get-tuple-element.41.src, s32[16]{0:T(128)S(1)} %get-tuple-element.40.blk, s32[16]{0:T(128)S(1)} %copy-done.5, bf16[3,512,2048]{2,1,0:T(8,128)(2,1)S(1)} %reorder.1.refs_2_.x, ...), custom_call_target="tpu_custom_call", output_to_operand_aliasing={{}: (9, {})} | custom-call | flops 268435456 | bytes 2097152 | tf_op jit(solution)/shard_map/far_update/pallas_call | solution.py:358
  (4 shorter events, 0.1 us)
Async XLA Ops:
  0.6 16.9 %collective-permute-start = (bf16[512,2048]{1,0:T(8,128)(2,1)}, bf16[512,2048]{1,0:T(8,128)(2,1)}, u32[]{:S(2)}, u32[]{:S(2)}) collective-permute-start(bf16[512,2048]{1,0:T(8,128)(2,1)} %src.3), channel_id=1, source_target_pairs={{0,4},{4,0},{8,12},{12,8},{16,20},{20,16},{24,28},{28,24},{32,36},... | collective-permute-start | bytes 6291464 | tf_op jit(solution)/shard_map/ppermute | solution.py:280
  3.6 13.9 %copy-start = (bf16[16,256,256]{2,1,0:T(8,128)(2,1)S(1)}, bf16[16,256,256]{2,1,0:T(8,128)(2,1)}, u32[]{:S(2)}) copy-start(bf16[16,256,256]{2,1,0:T(8,128)(2,1)} %tiles.9) | copy-start | bytes 6291460
  3.7 13.9 %copy-start.5 = (s32[16]{0:T(128)S(1)}, s32[16]{0:T(128)}, u32[]{:S(2)}) copy-start(s32[16]{0:T(128)} %col.13) | copy-start | bytes 196
  3.7 20.1 %collective-permute-start.1 = (bf16[256,2048]{1,0:T(8,128)(2,1)}, bf16[256,2048]{1,0:T(8,128)(2,1)S(1)}, u32[]{:S(2)}, u32[]{:S(2)}) collective-permute-start(bf16[256,2048]{1,0:T(8,128)(2,1)} %load.3), channel_id=1, source_target_pairs={{4,8},{8,4},{12,16},{16,12},{20,24},{24,20},{28,32},{32,28},{36,40... | collective-permute-start | bytes 3145736 | tf_op jit(solution)/shard_map/ppermute | solution.py:279
  8.4 1.6 %copy-start.6 = (bf16[512,2048]{1,0:T(8,128)(2,1)S(1)}, bf16[512,2048]{1,0:T(8,128)(2,1)}, u32[]{:S(2)}) copy-start(bf16[512,2048]{1,0:T(8,128)(2,1)} %src.3) | copy-start | bytes 6291460
  10.0 7.6 %copy-start.7 = (s32[16]{0:T(128)S(1)}, s32[16]{0:T(128)}, u32[]{:S(2)}) copy-start(s32[16]{0:T(128)} %param.9) | copy-start | bytes 196
  11.2 1.3 %copy-start.1 = (bf16[512,2048]{1,0:T(8,128)(2,1)}, bf16[512,2048]{1,0:T(8,128)(2,1)S(1)}, u32[]{:S(2)}) copy-start(bf16[512,2048]{1,0:T(8,128)(2,1)S(1)} %get-tuple-element.21.x_own.samples) | copy-start | bytes 6291460
  12.5 22.3 %collective-permute-start.2 = (bf16[256,2048]{1,0:T(8,128)(2,1)}, bf16[256,2048]{1,0:T(8,128)(2,1)}, u32[]{:S(2)}, u32[]{:S(2)}) collective-permute-start(bf16[256,2048]{1,0:T(8,128)(2,1)} %get-tuple-element.22), channel_id=1, source_target_pairs={{4,8},{8,4},{12,16},{16,12},{20,24},{24,20},{28,32},{32,28},{36,40... | collective-permute-start | bytes 3145736 | tf_op jit(solution)/shard_map/ppermute | solution.py:279
  17.6 1.6 %copy-start.2 = (bf16[512,2048]{1,0:T(8,128)(2,1)S(1)}, bf16[512,2048]{1,0:T(8,128)(2,1)}, u32[]{:S(2)}) copy-start(bf16[512,2048]{1,0:T(8,128)(2,1)} %copy-done.1) | copy-start | bytes 6291460
  23.7 5.7 %copy-start.3 = (bf16[512,2048]{1,0:T(8,128)(2,1)S(1)}, bf16[512,2048]{1,0:T(8,128)(2,1)}, u32[]{:S(2)}) copy-start(bf16[512,2048]{1,0:T(8,128)(2,1)} %copy-done.1) | copy-start | bytes 6291460
  25.3 15.6 %collective-permute-start.6 = (bf16[64,2048]{1,0:T(8,128)(2,1)S(1)}, bf16[64,2048]{1,0:T(8,128)(2,1)S(1)}, u32[]{:S(2)}, u32[]{:S(2)}) collective-permute-start(bf16[64,2048]{1,0:T(8,128)(2,1)S(1)} %get-tuple-element.28), channel_id=1, source_target_pairs={{0,1},{1,2},{2,3},{3,0},{4,5},{5,6},{6,7},{7,4},{8,9},{9,10},{10,1... | collective-permute-start | bytes 786440 | tf_op jit(solution)/shard_map/ppermute | solution.py:281
  26.8 14.6 %collective-permute-start.7 = (bf16[64,2048]{1,0:T(8,128)(2,1)S(1)}, bf16[64,2048]{1,0:T(8,128)(2,1)S(1)}, u32[]{:S(2)}, u32[]{:S(2)}) collective-permute-start(bf16[64,2048]{1,0:T(8,128)(2,1)S(1)} %get-tuple-element.29), channel_id=1, source_target_pairs={{0,2},{1,3},{2,0},{3,1},{4,6},{5,7},{6,4},{7,5},{8,10},{9,11},{10,... | collective-permute-start | bytes 786440 | tf_op jit(solution)/shard_map/ppermute | solution.py:281
  28.9 12.5 %collective-permute-start.8 = (bf16[64,2048]{1,0:T(8,128)(2,1)S(1)}, bf16[64,2048]{1,0:T(8,128)(2,1)S(1)}, u32[]{:S(2)}, u32[]{:S(2)}) collective-permute-start(bf16[64,2048]{1,0:T(8,128)(2,1)S(1)} %get-tuple-element.30), channel_id=1, source_target_pairs={{0,3},{1,0},{2,1},{3,2},{4,7},{5,4},{6,5},{7,6},{8,11},{9,8},{10,9... | collective-permute-start | bytes 786440 | tf_op jit(solution)/shard_map/ppermute | solution.py:281
  33.9 7.5 %copy-start.4 = (f32[2048]{0:T(1024)S(1)}, f32[2048]{0:T(1024)}, u32[]{:S(2)}) copy-start(f32[2048]{0:T(1024)} %param.8) | copy-start | bytes 24580
  37.0 13.0 %collective-permute-start.3 = (bf16[64,2048]{1,0:T(8,128)(2,1)S(1)}, bf16[64,2048]{1,0:T(8,128)(2,1)S(1)}, u32[]{:S(2)}, u32[]{:S(2)}) collective-permute-start(bf16[64,2048]{1,0:T(8,128)(2,1)S(1)} %get-tuple-element.24), channel_id=1, source_target_pairs={{0,1},{1,2},{2,3},{3,0},{4,5},{5,6},{6,7},{7,4},{8,9},{9,10},{10,1... | collective-permute-start | bytes 786440 | tf_op jit(solution)/shard_map/ppermute | solution.py:281
  38.8 11.4 %collective-permute-start.4 = (bf16[64,2048]{1,0:T(8,128)(2,1)S(1)}, bf16[64,2048]{1,0:T(8,128)(2,1)S(1)}, u32[]{:S(2)}, u32[]{:S(2)}) collective-permute-start(bf16[64,2048]{1,0:T(8,128)(2,1)S(1)} %get-tuple-element.25), channel_id=1, source_target_pairs={{0,2},{1,3},{2,0},{3,1},{4,6},{5,7},{6,4},{7,5},{8,10},{9,11},{10,... | collective-permute-start | bytes 786440 | tf_op jit(solution)/shard_map/ppermute | solution.py:281
  40.9 10.2 %collective-permute-start.5 = (bf16[64,2048]{1,0:T(8,128)(2,1)S(1)}, bf16[64,2048]{1,0:T(8,128)(2,1)S(1)}, u32[]{:S(2)}, u32[]{:S(2)}) collective-permute-start(bf16[64,2048]{1,0:T(8,128)(2,1)S(1)} %get-tuple-element.26), channel_id=1, source_target_pairs={{0,3},{1,0},{2,1},{3,2},{4,7},{5,4},{6,5},{7,6},{8,11},{9,8},{10,9... | collective-permute-start | bytes 786440 | tf_op jit(solution)/shard_map/ppermute | solution.py:281
  42.1 11.0 %collective-permute-start.9 = (bf16[64,2048]{1,0:T(8,128)(2,1)S(1)}, bf16[64,2048]{1,0:T(8,128)(2,1)S(1)}, u32[]{:S(2)}, u32[]{:S(2)}) collective-permute-start(bf16[64,2048]{1,0:T(8,128)(2,1)S(1)} %combine.2.refs_0_), channel_id=1, source_target_pairs={{4,8},{8,4},{12,16},{16,12},{20,24},{24,20},{28,32},{32,28},{36,40... | collective-permute-start | bytes 786440 | tf_op jit(solution)/shard_map/ppermute | solution.py:279
  53.9 13.3 %collective-permute-start.10 = (bf16[128,2048]{1,0:T(8,128)(2,1)S(1)}, bf16[128,2048]{1,0:T(8,128)(2,1)S(1)}, u32[]{:S(2)}, u32[]{:S(2)}) collective-permute-start(bf16[128,2048]{1,0:T(8,128)(2,1)S(1)} %combine.3.mine), channel_id=1, source_target_pairs={{0,1},{1,2},{2,3},{3,0},{4,5},{5,6},{6,7},{7,4},{8,9},{9,10},{10,1... | collective-permute-start | bytes 1572872 | tf_op jit(solution)/shard_map/ppermute | solution.py:281
  55.0 13.0 %collective-permute-start.11 = (bf16[128,2048]{1,0:T(8,128)(2,1)S(1)}, bf16[128,2048]{1,0:T(8,128)(2,1)S(1)}, u32[]{:S(2)}, u32[]{:S(2)}) collective-permute-start(bf16[128,2048]{1,0:T(8,128)(2,1)S(1)} %combine.3.mine), channel_id=1, source_target_pairs={{0,3},{1,0},{2,1},{3,2},{4,7},{5,4},{6,5},{7,6},{8,11},{9,8},{10,9... | collective-permute-start | bytes 1572872 | tf_op jit(solution)/shard_map/ppermute | solution.py:281
  68.2 5.7 %collective-permute-start.14 = (bf16[384,2048]{1,0:T(8,128)(2,1)S(1)}, bf16[384,2048]{1,0:T(8,128)(2,1)S(1)}, u32[]{:S(2)}, u32[]{:S(2)}) collective-permute-start(bf16[384,2048]{1,0:T(8,128)(2,1)S(1)} %get-tuple-element.33.w_own), channel_id=1, source_target_pairs={{0,4},{4,0},{8,12},{12,8},{16,20},{20,16},{24,28},{28,24},{32,36},... | collective-permute-start | bytes 4718600 | tf_op jit(solution)/shard_map/ppermute | solution.py:280
  68.3 22.2 %collective-permute-start.16 = (bf16[320,2048]{1,0:T(8,128)(2,1)S(1)}, bf16[320,2048]{1,0:T(8,128)(2,1)S(1)}, u32[]{:S(2)}, u32[]{:S(2)}) collective-permute-start(bf16[320,2048]{1,0:T(8,128)(2,1)S(1)} %get-tuple-element.37), channel_id=1, source_target_pairs={{4,8},{8,4},{12,16},{16,12},{20,24},{24,20},{28,32},{32,28},{36,40... | collective-permute-start | bytes 3932168 | tf_op jit(solution)/shard_map/ppermute | solution.py:279
  71.1 9.6 %collective-permute-start.12 = (bf16[64,2048]{1,0:T(8,128)(2,1)S(1)}, bf16[64,2048]{1,0:T(8,128)(2,1)S(1)}, u32[]{:S(2)}, u32[]{:S(2)}) collective-permute-start(bf16[64,2048]{1,0:T(8,128)(2,1)S(1)} %get-tuple-element.31), channel_id=1, source_target_pairs={{0,1},{1,2},{2,3},{3,0},{4,5},{5,6},{6,7},{7,4},{8,9},{9,10},{10,1... | collective-permute-start | bytes 786440 | tf_op jit(solution)/shard_map/ppermute | solution.py:281
  71.3 9.4 %collective-permute-start.13 = (bf16[64,2048]{1,0:T(8,128)(2,1)S(1)}, bf16[64,2048]{1,0:T(8,128)(2,1)S(1)}, u32[]{:S(2)}, u32[]{:S(2)}) collective-permute-start(bf16[64,2048]{1,0:T(8,128)(2,1)S(1)} %get-tuple-element.32), channel_id=1, source_target_pairs={{0,3},{1,0},{2,1},{3,2},{4,7},{5,4},{6,5},{7,6},{8,11},{9,8},{10,9... | collective-permute-start | bytes 786440 | tf_op jit(solution)/shard_map/ppermute | solution.py:281
  80.7 4.3 %collective-permute-start.15 = (bf16[128,2048]{1,0:T(8,128)(2,1)S(1)}, bf16[128,2048]{1,0:T(8,128)(2,1)S(1)}, u32[]{:S(2)}, u32[]{:S(2)}) collective-permute-start(bf16[128,2048]{1,0:T(8,128)(2,1)S(1)} %join.1.w_op), channel_id=1, source_target_pairs={{0,4},{4,0},{8,12},{12,8},{16,20},{20,16},{24,28},{28,24},{32,36},... | collective-permute-start | bytes 1572872 | tf_op jit(solution)/shard_map/ppermute | solution.py:280
  81.2 14.9 %collective-permute-start.17 = (bf16[128,2048]{1,0:T(8,128)(2,1)S(1)}, bf16[128,2048]{1,0:T(8,128)(2,1)S(1)}, u32[]{:S(2)}, u32[]{:S(2)}) collective-permute-start(bf16[128,2048]{1,0:T(8,128)(2,1)S(1)} %join.1.w_op), channel_id=1, source_target_pairs={{4,8},{8,4},{12,16},{16,12},{20,24},{24,20},{28,32},{32,28},{36,40... | collective-permute-start | bytes 1572872 | tf_op jit(solution)/shard_map/ppermute | solution.py:279

commit v4 on v3

--- a/solution.py
+++ b/solution.py
@@ -30,7 +30,7 @@
         out_specs=out_specs,
         scratch_shapes=scratch,
         input_output_aliases=aliases or {},
-        compiler_params=pltpu.CompilerParams(vmem_limit_bytes=vmem << 20),
+        compiler_params=pltpu.CompilerParams(vmem_limit_bytes=int(vmem * 2**20)),
         cost_estimate=pl.CostEstimate(flops=flops, bytes_accessed=moved, transcendentals=0),
         name=name,
     )
@@ -82,23 +82,33 @@
         c.wait()
 
 
+def load_first_kernel(src, dst, through, in_sem, out_sem):
+    pieces, rows, _ = through.shape
+    ins = [pltpu.make_async_copy(src.at[pl.ds(n * rows, rows)], through.at[n], in_sem.at[n]) for n in range(pieces)]
+    outs = [pltpu.make_async_copy(through.at[n], dst.at[pl.ds(n * rows, rows)], out_sem.at[n]) for n in range(pieces)]
+    for c in ins:
+        c.start()
+    for came, goes in zip(ins, outs, strict=True):
+        came.wait()
+        goes.start()
+    for c in outs:
+        c.wait()
+
+
+def load_first(src, rows):
+    pieces = 4
+    return call(
+        load_first_kernel, "load", like((rows, src.shape[1]), src.dtype), [HBM], HBM, 0, 1 << 20,
+        [pltpu.VMEM((pieces, rows // pieces, src.shape[1]), src.dtype), DMA((pieces,)), DMA((pieces,))], vmem=62.5,
+    )(src)
+
+
 def load(src, ranges, vmem):
     return call(
         functools.partial(load_kernel, [first for first, _ in ranges]), "load",
         [like((rows, src.shape[1]), src.dtype) for _, rows in ranges], [HBM], [VMEM] * len(ranges), 2 << 30, 1 << 20,
         [DMA((len(ranges),))], vmem=vmem,
     )(src)
-
-
-def own_image_kernel(first, meta, src, blk, col, x_own, x_near, tiles, acc):
-    rows = pl.ds(first, acc.shape[0])
-    acc[...] = jnp.zeros_like(acc)
-    for source, x in ((OWN, x_own), (NEAR, x_near)):
-
-        def add(s):
-            acc[:, block(col[s])] += jnp.dot(x[rows, block(blk[s])], tiles[s], preferred_element_type=F32)
-
-        each_of(source, src, meta[0], add)
 
 
 def far_image_kernel(meta, src, blk, col, acc, x_far, tiles, own, send_1, send_2, send_3, total):
@@ -163,13 +173,19 @@
             first += rows
 
 
-def pairs(count, body):
+UNROLL = 4
+
+
+def whole_steps(count):
+    return (count + UNROLL - 1) // UNROLL
+
+
+def in_steps(count, body):
     def step(t, carry):
-        body(2 * t)
-        body(2 * t + 1)
+        body([UNROLL * t + n for n in range(UNROLL)])
         return carry
 
-    lax.fori_loop(0, (count + 1) // 2, step, 0)
+    lax.fori_loop(0, whole_steps(count), step, 0)
 
 
 def gradient(s, rows, src, blk, col, x, w_own, w_near):
@@ -187,10 +203,11 @@
 def first_update_kernel(meta, src, blk, col, x, w_own, w_near, acc, dots):
     rows = slice(0, w_own.shape[0])
 
-    def add(s):
-        acc[s] = gradient(s, rows, src, blk, col, x, w_own, w_near)
-
-    pairs(meta[0], add)
+    def add(slots):
+        for s in slots:
+            acc[s] = gradient(s, rows, src, blk, col, x, w_own, w_near)
+
+    in_steps(meta[0], add)
     dots[...] = column_dots(x[OWN, rows], w_own[...])
 
 
@@ -200,7 +217,7 @@
     rows = slice(samples - w_op.shape[0], samples)
     scale = STEP / (2.0 * samples)
     count = meta[0]
-    even = (count + 1) // 2 * 2
+    whole = whole_steps(count) * UNROLL
     save = lambda s: pltpu.make_async_copy(out_v.at[s], out.at[s], sem.at[s])
 
     def clear(s, carry):
@@ -208,7 +225,7 @@
         save(s).start()
         return carry
 
-    lax.fori_loop(even, slots, clear, 0)
+    lax.fori_loop(whole, slots, clear, 0)
 
     def done_here(s):
         return jnp.logical_or(s >= count, src[s] != FAR)
@@ -218,18 +235,16 @@
         moved[s] = value
         out_v[s] = jnp.where(s < count, soft(value), jnp.zeros((B, B), BF16))
 
-    def step(t, carry):
-        finish(2 * t)
-        finish(2 * t + 1)
-        for s in (2 * t, 2 * t + 1):
+    def step(some):
+        for s in some:
+            finish(s)
+        for s in some:
 
             @pl.when(done_here(s))
             def _():
                 save(s).start()
 
-        return carry
-
-    lax.fori_loop(0, even // 2, step, 0)
+    in_steps(count, step)
     total = dots[...] + column_dots(x[OWN, rows], w_op[...])
     d = diag[...]
     new_diag[...] = d - STEP * (total / samples - 1.0 / d)
@@ -242,6 +257,23 @@
         return carry
 
     lax.fori_loop(0, slots, end, 0)
+
+
+def own_image_kernel(first, meta, src, blk, col, x_own, x_near, tiles, acc):
+    rows = pl.ds(first, acc.shape[0])
+    acc[...] = jnp.zeros_like(acc)
+
+    def add(slots):
+        products = []
+        for s in slots:
+            at = block(blk[s])
+            x = jnp.where(src[s] == NEAR, x_near[rows, at], x_own[rows, at])
+            used = jnp.logical_and(s < meta[0], src[s] != FAR)
+            products.append(jnp.where(used, jnp.dot(x, tiles[s], preferred_element_type=F32), 0.0))
+        for s, product in zip(slots, products, strict=True):
+            acc[:, block(col[s])] += product
+
+    in_steps(meta[0], add)
 
 
 def far_update_kernel(meta, src, blk, col, x, moved, *rest):
@@ -290,7 +322,7 @@
     diag = theta_diag[None, :]
 
     x_near = swap_near(samples)
-    (x_first,) = load(samples, [(0, CHUNKS[0])], 62)
+    x_first = load_first(samples, CHUNKS[0])
     x_own, *x_rest = load(samples, [(0, count_ns), *zip(firsts[1:], CHUNKS[1:], strict=True)], 10)
     x_far = [swap_far(x) for x in (x_first, *x_rest)]
 

time: 99.2 us -> 99.2 us (level)
  Pallas kernels: 32.9 us -> 30.5 us
  starting transfers between devices: 36.5 us -> 38.9 us
    ppermute x5, waiting for transfers between devices: 8.85 us -> 11.9 us  [shards(): swap_far = lambda v: lax.ppermute(v, 'blk', far)]
    ppermute x10, waiting for transfers between devices: 14.3 us -> 11.7 us  [shards(): lax.ppermute(v, 'rep', [(i, (i + n) % reps) for i in range(reps)])]
    pallas_call x2, Pallas kernels: 9.07 us -> 6.53 us  [shards(): call(functools.partial(own_image_kernel, first), 'own_image', like((rows,...]
    ppermute x10, starting transfers between devices: 13.9 us -> 16.4 us  [shards(): lax.ppermute(v, 'rep', [(i, (i + n) % reps) for i in range(reps)])]
    pallas_call x2 -> x1, Pallas kernels: 3.45 us -> 1.2 us  [load(): call(functools.partial(load_kernel, [first for first, _ in ranges]), 'loa...]
    pallas_call x0 -> x1, Pallas kernels: none -> 2.03 us  [load_first(): call(load_first_kernel, 'load', like((rows, src.shape[1]), src.dtype), [H...]
  transfers between devices with their start and end apart: 18 -> 18, of which waited for: 9 -> 9; matrix products, arithmetic and copies ran while one was open for 0% -> 0% of each run, Pallas kernels for 30% -> 26%
where the time goes in v4:
time: 99.2 us
  starting transfers between devices  38.9 us (39%)
  Pallas kernels  30.5 us (31%)
  waiting for transfers between devices  23.6 us (24%)
  local copies, waits for them, and re-layouts  4.51 us (5%)
  between operations  1.69 us (2%)
    ppermute x5, starting transfers between devices, shards(): swap_far = lambda v: lax.ppermute(v, 'blk', far)  21.2 us
    ppermute x10, starting transfers between devices, shards(): lax.ppermute(v, 'rep', [(i, (i + n) % reps) for i in range(reps)])  16.4 us
    ppermute x5, waiting for transfers between devices, shards(): swap_far = lambda v: lax.ppermute(v, 'blk', far)  11.9 us
    ppermute x10, waiting for transfers between devices, shards(): lax.ppermute(v, 'rep', [(i, (i + n) % reps) for i in range(reps)])  11.7 us
    pallas_call x2, Pallas kernels, shards(): call(functools.partial(own_image_kernel, first), 'own_image', like((rows,...  6.53 us
    pallas_call x2, Pallas kernels, shards(): call(far_image_kernel, 'far_image', [like((part, width), F32)] + [like((p...  4.55 us
    pallas_call x1, Pallas kernels, shards(): call(first_update_kernel, 'first_update', [like(theta_tiles.shape, F32),...  4.54 us
    unnamed x16, local copies, waits for them, and re-layouts  4.51 us
  transfers between devices with their start and end apart: 18, of which 9 were waited for; matrix products, arithmetic and copies ran while one was open for 0% of the time, Pallas kernels for 26%

profile of v4, /device:TPU:103, one launch (start us, length us, event | category | flops | bytes accessed | tf_op | source)
XLA Modules:
  0.0 99.2 jit_solution(7834358426201127628)
XLA Ops:
  0.6 0.8 collective-permute-start
  1.4 2.0 %load.3 = bf16[256,2048]{1,0:T(8,128)(2,1)} custom-call(bf16[512,2048]{1,0:T(8,128)(2,1)} %src.3), custom_call_target="tpu_custom_call" | custom-call | bytes 1048576 | tf_op jit(solution)/shard_map/load/pallas_call | solution.py:100
  3.4 0.0 copy-start
  3.4 4.7 %collective-permute-start.1 = (bf16[256,2048]{1,0:T(8,128)(2,1)}, bf16[256,2048]{1,0:T(8,128)(2,1)S(1)}, u32[]{:S(2)}, u32[]{:S(2)}) collective-permute-start(bf16[256,2048]{1,0:T(8,128)(2,1)} %load.3), channel_id=1, source_target_pairs={{4,8},{8,4},{12,16},{16,12},{20,24},{24,20},{28,32},{32,28},{36,40... | collective-permute-start | bytes 3145736 | tf_op jit(solution)/shard_map/ppermute | solution.py:311
  8.2 0.0 copy-start.4
  8.2 1.6 %copy-done.4 = bf16[512,2048]{1,0:T(8,128)(2,1)S(1)} copy-done((bf16[512,2048]{1,0:T(8,128)(2,1)S(1)}, bf16[512,2048]{1,0:T(8,128)(2,1)}, u32[]{:S(2)}) %copy-start.4) | copy-done | bytes 2097176
  9.8 1.2 %load.2 = (bf16[512,2048]{1,0:T(8,128)(2,1)S(1)}, bf16[256,2048]{1,0:T(8,128)(2,1)}) custom-call(bf16[512,2048]{1,0:T(8,128)(2,1)S(1)} %copy-done.4), custom_call_target="tpu_custom_call" | custom-call | flops 2147483648 | bytes 1048576 | tf_op jit(solution)/shard_map/load/pallas_call | solution.py:107
  11.0 0.0 copy-start.1
  11.0 1.3 %copy-done.1 = bf16[512,2048]{1,0:T(8,128)(2,1)} copy-done((bf16[512,2048]{1,0:T(8,128)(2,1)}, bf16[512,2048]{1,0:T(8,128)(2,1)S(1)}, u32[]{:S(2)}) %copy-start.1) | copy-done | bytes 2097176
  12.3 4.3 %collective-permute-start.2 = (bf16[256,2048]{1,0:T(8,128)(2,1)}, bf16[256,2048]{1,0:T(8,128)(2,1)}, u32[]{:S(2)}, u32[]{:S(2)}) collective-permute-start(bf16[256,2048]{1,0:T(8,128)(2,1)} %get-tuple-element.22), channel_id=1, source_target_pairs={{4,8},{8,4},{12,16},{16,12},{20,24},{24,20},{28,32},{32,28},{36,40... | collective-permute-start | bytes 3145736 | tf_op jit(solution)/shard_map/ppermute | solution.py:311
  17.3 0.1 pad_add_fusion.meta
  17.3 0.0 copy-done.7
  17.3 0.0 collective-permute-done.x_near
  17.4 0.0 copy-done
  17.4 0.0 copy-done.6
  17.4 0.0 copy-start.2
  17.4 1.6 %copy-done.2 = bf16[512,2048]{1,0:T(8,128)(2,1)S(1)} copy-done((bf16[512,2048]{1,0:T(8,128)(2,1)S(1)}, bf16[512,2048]{1,0:T(8,128)(2,1)}, u32[]{:S(2)}) %copy-start.2) | copy-done | bytes 2097176
  19.0 3.3 %own_image.3.acc = f32[256,2048]{1,0:T(8,128)S(1)} custom-call(s32[2]{0:T(128)S(1)} %pad_add_fusion.meta, s32[16]{0:T(128)S(1)} %get-tuple-element.41.src, s32[16]{0:T(128)S(1)} %get-tuple-element.40.blk, s32[16]{0:T(128)S(1)} %copy-done.6, bf16[512,2048]{1,0:T(8,128)(2,1)S(1)} %copy-done.2, bf16[512,2048]{1,0:T(8,128)(2,1)} %collective-permute-done.x_near, ...), custom_call_target="tpu_custom_call" | custom-call | flops 1073741824 | bytes 4194304 | tf_op jit(solution)/shard_map/own_image/pallas_call | solution.py:330
  22.2 0.0 copy-start.3
  22.2 1.0 collective-permute-done.1.refs_0_.x_far
  23.2 1.9 %far_image.3 = (f32[64,2048]{1,0:T(8,128)S(1)}, bf16[64,2048]{1,0:T(8,128)(2,1)S(1)}, bf16[64,2048]{1,0:T(8,128)(2,1)S(1)}, bf16[64,2048]{1,0:T(8,128)(2,1)S(1)}) custom-call(s32[2]{0:T(128)S(1)} %pad_add_fusion.meta, s32[16]{0:T(128)S(1)} %get-tuple-element.41.src, s32[16]{0:T(128)S(1)} %get-tuple-element.40.blk, s32[16]{0:T(128)S(1)} %copy-done.6, ...), custom_call_target="tpu_custom_call" | custom-call | flops 268435456 | bytes 1048576 | tf_op jit(solution)/shard_map/far_image/pallas_call | solution.py:344
  25.2 0.5 collective-permute-start.6
  25.7 3.5 %collective-permute-start.7 = (bf16[64,2048]{1,0:T(8,128)(2,1)S(1)}, bf16[64,2048]{1,0:T(8,128)(2,1)S(1)}, u32[]{:S(2)}, u32[]{:S(2)}) collective-permute-start(bf16[64,2048]{1,0:T(8,128)(2,1)S(1)} %get-tuple-element.29), channel_id=1, source_target_pairs={{0,2},{1,3},{2,0},{3,1},{4,6},{5,7},{6,4},{7,5},{8,10},{9,11},{10,... | collective-permute-start | bytes 786440 | tf_op jit(solution)/shard_map/ppermute | solution.py:313
  29.1 1.5 %collective-permute-start.8 = (bf16[64,2048]{1,0:T(8,128)(2,1)S(1)}, bf16[64,2048]{1,0:T(8,128)(2,1)S(1)}, u32[]{:S(2)}, u32[]{:S(2)}) collective-permute-start(bf16[64,2048]{1,0:T(8,128)(2,1)S(1)} %get-tuple-element.30), channel_id=1, source_target_pairs={{0,3},{1,0},{2,1},{3,2},{4,7},{5,4},{6,5},{7,6},{8,11},{9,8},{10,9... | collective-permute-start | bytes 786440 | tf_op jit(solution)/shard_map/ppermute | solution.py:313
  30.6 0.0 copy-done.3
  30.6 3.3 %own_image.2.acc = f32[256,2048]{1,0:T(8,128)S(1)} custom-call(s32[2]{0:T(128)S(1)} %pad_add_fusion.meta, s32[16]{0:T(128)S(1)} %get-tuple-element.41.src, s32[16]{0:T(128)S(1)} %get-tuple-element.40.blk, s32[16]{0:T(128)S(1)} %copy-done.6, bf16[512,2048]{1,0:T(8,128)(2,1)S(1)} %copy-done.3, bf16[512,2048]{1,0:T(8,128)(2,1)} %collective-permute-done.x_near, ...), custom_call_target="tpu_custom_call" | custom-call | flops 1073741824 | bytes 4194304 | tf_op jit(solution)/shard_map/own_image/pallas_call | solution.py:330
  33.9 0.0 copy-start.5
  33.9 0.7 collective-permute-done.2.refs_1_.x_far
  34.6 2.6 %far_image.2 = (f32[64,2048]{1,0:T(8,128)S(1)}, bf16[64,2048]{1,0:T(8,128)(2,1)S(1)}, bf16[64,2048]{1,0:T(8,128)(2,1)S(1)}, bf16[64,2048]{1,0:T(8,128)(2,1)S(1)}) custom-call(s32[2]{0:T(128)S(1)} %pad_add_fusion.meta, s32[16]{0:T(128)S(1)} %get-tuple-element.41.src, s32[16]{0:T(128)S(1)} %get-tuple-element.40.blk, s32[16]{0:T(128)S(1)} %copy-done.6, ...), custom_call_target="tpu_custom_call" | custom-call | flops 268435456 | bytes 1048576 | tf_op jit(solution)/shard_map/far_image/pallas_call | solution.py:344
  37.2 0.5 collective-permute-start.3
  37.7 3.5 %collective-permute-start.4 = (bf16[64,2048]{1,0:T(8,128)(2,1)S(1)}, bf16[64,2048]{1,0:T(8,128)(2,1)S(1)}, u32[]{:S(2)}, u32[]{:S(2)}) collective-permute-start(bf16[64,2048]{1,0:T(8,128)(2,1)S(1)} %get-tuple-element.25), channel_id=1, source_target_pairs={{0,2},{1,3},{2,0},{3,1},{4,6},{5,7},{6,4},{7,5},{8,10},{9,11},{10,... | collective-permute-start | bytes 786440 | tf_op jit(solution)/shard_map/ppermute | solution.py:313
  41.1 0.0 collective-permute-done.6.got_1
  41.1 1.5 %collective-permute-start.5 = (bf16[64,2048]{1,0:T(8,128)(2,1)S(1)}, bf16[64,2048]{1,0:T(8,128)(2,1)S(1)}, u32[]{:S(2)}, u32[]{:S(2)}) collective-permute-start(bf16[64,2048]{1,0:T(8,128)(2,1)S(1)} %get-tuple-element.26), channel_id=1, source_target_pairs={{0,3},{1,0},{2,1},{3,2},{4,7},{5,4},{6,5},{7,6},{8,11},{9,8},{10,9... | collective-permute-start | bytes 786440 | tf_op jit(solution)/shard_map/ppermute | solution.py:313
  42.6 0.0 collective-permute-done.7.got_2
  42.6 0.0 collective-permute-done.8.got_3
  42.6 0.0 copy-done.5
  42.6 0.7 combine.2.refs_0_
  43.4 4.8 %collective-permute-start.9 = (bf16[64,2048]{1,0:T(8,128)(2,1)S(1)}, bf16[64,2048]{1,0:T(8,128)(2,1)S(1)}, u32[]{:S(2)}, u32[]{:S(2)}) collective-permute-start(bf16[64,2048]{1,0:T(8,128)(2,1)S(1)} %combine.2.refs_0_), channel_id=1, source_target_pairs={{4,8},{8,4},{12,16},{16,12},{20,24},{24,20},{28,32},{32,28},{36,40... | collective-permute-start | bytes 786440 | tf_op jit(solution)/shard_map/ppermute | solution.py:311
  48.2 2.3 %reorder.1.refs_2_.x = bf16[3,512,2048]{2,1,0:T(8,128)(2,1)S(1)} custom-call(s32[2]{0:T(128)S(1)} %pad_add_fusion.meta, bf16[512,2048]{1,0:T(8,128)(2,1)S(1)} %copy-done.3, bf16[512,2048]{1,0:T(8,128)(2,1)} %collective-permute-done.x_near, bf16[256,2048]{1,0:T(8,128)(2,1)S(1)} %collective-permute-done.1.refs_0_.x_far, ...), custom_call_target="tpu_custom_call" | custom-call | bytes 2097152 | tf_op jit(solution)/shard_map/reorder/pallas_call | solution.py:336
  50.5 0.0 collective-permute-done.3.got_1
  50.5 0.2 collective-permute-done.4.got_2
  50.7 0.0 collective-permute-done.5.got_3
  50.7 3.6 %collective-permute-done.9.refs_1_.rest_0_ = bf16[64,2048]{1,0:T(8,128)(2,1)S(1)} collective-permute-done((bf16[64,2048]{1,0:T(8,128)(2,1)S(1)}, bf16[64,2048]{1,0:T(8,128)(2,1)S(1)}, u32[]{:S(2)}, u32[]{:S(2)}) %collective-permute-start.9) | collective-permute-done | bytes 262176 | tf_op jit(solution)/shard_map/ppermute | solution.py:311
  54.4 0.7 combine.3.mine
  55.1 0.1 collective-permute-start.10
  55.2 2.7 %collective-permute-start.11 = (bf16[128,2048]{1,0:T(8,128)(2,1)S(1)}, bf16[128,2048]{1,0:T(8,128)(2,1)S(1)}, u32[]{:S(2)}, u32[]{:S(2)}) collective-permute-start(bf16[128,2048]{1,0:T(8,128)(2,1)S(1)} %combine.3.mine), channel_id=1, source_target_pairs={{0,3},{1,0},{2,1},{3,2},{4,7},{5,4},{6,5},{7,6},{8,11},{9,8},{10,9... | collective-permute-start | bytes 1572872 | tf_op jit(solution)/shard_map/ppermute | solution.py:313
  57.9 7.6 %collective-permute-done.10.below = bf16[128,2048]{1,0:T(8,128)(2,1)S(1)} collective-permute-done((bf16[128,2048]{1,0:T(8,128)(2,1)S(1)}, bf16[128,2048]{1,0:T(8,128)(2,1)S(1)}, u32[]{:S(2)}, u32[]{:S(2)}) %collective-permute-start.10) | collective-permute-done | bytes 524320 | tf_op jit(solution)/shard_map/ppermute | solution.py:313
  65.5 2.1 %collective-permute-done.11.above = bf16[128,2048]{1,0:T(8,128)(2,1)S(1)} collective-permute-done((bf16[128,2048]{1,0:T(8,128)(2,1)S(1)}, bf16[128,2048]{1,0:T(8,128)(2,1)S(1)}, u32[]{:S(2)}, u32[]{:S(2)}) %collective-permute-start.11) | collective-permute-done | bytes 524320 | tf_op jit(solution)/shard_map/ppermute | solution.py:313
  67.6 0.2 stack.9
  67.8 0.1 collective-permute-start.14
  67.9 3.2 %collective-permute-start.16 = (bf16[320,2048]{1,0:T(8,128)(2,1)S(1)}, bf16[320,2048]{1,0:T(8,128)(2,1)S(1)}, u32[]{:S(2)}, u32[]{:S(2)}) collective-permute-start(bf16[320,2048]{1,0:T(8,128)(2,1)S(1)} %get-tuple-element.37), channel_id=1, source_target_pairs={{4,8},{8,4},{12,16},{16,12},{20,24},{24,20},{28,32},{32,28},{36,40... | collective-permute-start | bytes 3932168 | tf_op jit(solution)/shard_map/ppermute | solution.py:311
  71.1 0.2 collective-permute-start.12
  71.3 2.6 %collective-permute-start.13 = (bf16[64,2048]{1,0:T(8,128)(2,1)S(1)}, bf16[64,2048]{1,0:T(8,128)(2,1)S(1)}, u32[]{:S(2)}, u32[]{:S(2)}) collective-permute-start(bf16[64,2048]{1,0:T(8,128)(2,1)S(1)} %get-tuple-element.32), channel_id=1, source_target_pairs={{0,3},{1,0},{2,1},{3,2},{4,7},{5,4},{6,5},{7,6},{8,11},{9,8},{10,9... | collective-permute-start | bytes 786440 | tf_op jit(solution)/shard_map/ppermute | solution.py:313
  73.8 0.0 collective-permute-done.14.w_near
  73.8 4.5 %first_update.1 = (f32[16,256,256]{2,1,0:T(8,128)S(1)}, f32[1,2048]{1,0:T(1,128)S(1)}) custom-call(s32[2]{0:T(128)S(1)} %pad_add_fusion.meta, s32[16]{0:T(128)S(1)} %get-tuple-element.41.src, s32[16]{0:T(128)S(1)} %get-tuple-element.40.blk, s32[16]{0:T(128)S(1)} %copy-done.6, bf16[3,512,2048]{2,1,0:T(8,128)(2,1)S(1)} %reorder.1.refs_2_.x, ...), custom_call_target="tpu_custom_call" | custom-call | flops 1073741824 | bytes 4194304 | tf_op jit(solution)/shard_map/first_update/pallas_call | solution.py:371
  78.4 1.7 %collective-permute-done.12.op_a = bf16[64,2048]{1,0:T(8,128)(2,1)S(1)} collective-permute-done((bf16[64,2048]{1,0:T(8,128)(2,1)S(1)}, bf16[64,2048]{1,0:T(8,128)(2,1)S(1)}, u32[]{:S(2)}, u32[]{:S(2)}) %collective-permute-start.12) | collective-permute-done | bytes 262176 | tf_op jit(solution)/shard_map/ppermute | solution.py:313
  80.1 0.0 collective-permute-done.13.op_b
  80.1 0.5 collective-permute-start.15
  80.6 4.2 %collective-permute-start.17 = (bf16[128,2048]{1,0:T(8,128)(2,1)S(1)}, bf16[128,2048]{1,0:T(8,128)(2,1)S(1)}, u32[]{:S(2)}, u32[]{:S(2)}) collective-permute-start(bf16[128,2048]{1,0:T(8,128)(2,1)S(1)} %join.1.w_op), channel_id=1, source_target_pairs={{4,8},{8,4},{12,16},{16,12},{20,24},{24,20},{28,32},{32,28},{36,40... | collective-permute-start | bytes 1572872 | tf_op jit(solution)/shard_map/ppermute | solution.py:311
  84.8 0.0 collective-permute-done.15.near_op
  84.8 4.3 %own_update.1 = (bf16[16,256,256]{2,1,0:T(8,128)(2,1)}, f32[16,256,256]{2,1,0:T(8,128)S(1)}, f32[1,2048]{1,0:T(1,128)}) custom-call(s32[2]{0:T(128)S(1)} %pad_add_fusion.meta, s32[16]{0:T(128)S(1)} %get-tuple-element.41.src, s32[16]{0:T(128)S(1)} %get-tuple-element.40.blk, s32[16]{0:T(128)S(1)} %copy-done.6, bf16[3,512,2048]{2,1,0:T(8,128)(2,1)S(1)} %reorder.1.refs_2_.x, ...), custom_call_target="tpu_custom_call" | custom-call | flops 1073741824 | bytes 4194304 | tf_op jit(solution)/shard_map/own_update/pallas_call | solution.py:382
  89.2 1.0 collective-permute-done.16.rest_1_
  90.2 5.6 %collective-permute-done.17.rest_2_ = bf16[128,2048]{1,0:T(8,128)(2,1)S(1)} collective-permute-done((bf16[128,2048]{1,0:T(8,128)(2,1)S(1)}, bf16[128,2048]{1,0:T(8,128)(2,1)S(1)}, u32[]{:S(2)}, u32[]{:S(2)}) %collective-permute-start.17) | collective-permute-done | bytes 524320 | tf_op jit(solution)/shard_map/ppermute | solution.py:311
  95.8 3.3 %far_update.1 = bf16[16,256,256]{2,1,0:T(8,128)(2,1)} custom-call(s32[2]{0:T(128)S(1)} %pad_add_fusion.meta, s32[16]{0:T(128)S(1)} %get-tuple-element.41.src, s32[16]{0:T(128)S(1)} %get-tuple-element.40.blk, s32[16]{0:T(128)S(1)} %copy-done.6, bf16[3,512,2048]{2,1,0:T(8,128)(2,1)S(1)} %reorder.1.refs_2_.x, ...), custom_call_target="tpu_custom_call", output_to_operand_aliasing={{}: (9, {})} | custom-call | flops 268435456 | bytes 2097152 | tf_op jit(solution)/shard_map/far_update/pallas_call | solution.py:390
  (4 shorter events, 0.1 us)
Async XLA Ops:
  0.6 16.7 %collective-permute-start = (bf16[512,2048]{1,0:T(8,128)(2,1)}, bf16[512,2048]{1,0:T(8,128)(2,1)}, u32[]{:S(2)}, u32[]{:S(2)}) collective-permute-start(bf16[512,2048]{1,0:T(8,128)(2,1)} %src.3), channel_id=1, source_target_pairs={{0,4},{4,0},{8,12},{12,8},{16,20},{20,16},{24,28},{28,24},{32,36},... | collective-permute-start | bytes 6291464 | tf_op jit(solution)/shard_map/ppermute | solution.py:312
  3.4 13.9 %copy-start = (bf16[16,256,256]{2,1,0:T(8,128)(2,1)S(1)}, bf16[16,256,256]{2,1,0:T(8,128)(2,1)}, u32[]{:S(2)}) copy-start(bf16[16,256,256]{2,1,0:T(8,128)(2,1)} %tiles.9) | copy-start | bytes 6291460
  3.4 19.8 %collective-permute-start.1 = (bf16[256,2048]{1,0:T(8,128)(2,1)}, bf16[256,2048]{1,0:T(8,128)(2,1)S(1)}, u32[]{:S(2)}, u32[]{:S(2)}) collective-permute-start(bf16[256,2048]{1,0:T(8,128)(2,1)} %load.3), channel_id=1, source_target_pairs={{4,8},{8,4},{12,16},{16,12},{20,24},{24,20},{28,32},{32,28},{36,40... | collective-permute-start | bytes 3145736 | tf_op jit(solution)/shard_map/ppermute | solution.py:311
  8.2 1.6 %copy-start.4 = (bf16[512,2048]{1,0:T(8,128)(2,1)S(1)}, bf16[512,2048]{1,0:T(8,128)(2,1)}, u32[]{:S(2)}) copy-start(bf16[512,2048]{1,0:T(8,128)(2,1)} %src.3) | copy-start | bytes 6291460
  9.8 7.6 %copy-start.7 = (s32[16]{0:T(128)S(1)}, s32[16]{0:T(128)}, u32[]{:S(2)}) copy-start(s32[16]{0:T(128)} %param.9) | copy-start | bytes 196
  9.8 7.6 %copy-start.6 = (s32[16]{0:T(128)S(1)}, s32[16]{0:T(128)}, u32[]{:S(2)}) copy-start(s32[16]{0:T(128)} %col.13) | copy-start | bytes 196
  11.0 1.3 %copy-start.1 = (bf16[512,2048]{1,0:T(8,128)(2,1)}, bf16[512,2048]{1,0:T(8,128)(2,1)S(1)}, u32[]{:S(2)}) copy-start(bf16[512,2048]{1,0:T(8,128)(2,1)S(1)} %get-tuple-element.21.x_own.samples) | copy-start | bytes 6291460
  12.3 22.3 %collective-permute-start.2 = (bf16[256,2048]{1,0:T(8,128)(2,1)}, bf16[256,2048]{1,0:T(8,128)(2,1)}, u32[]{:S(2)}, u32[]{:S(2)}) collective-permute-start(bf16[256,2048]{1,0:T(8,128)(2,1)} %get-tuple-element.22), channel_id=1, source_target_pairs={{4,8},{8,4},{12,16},{16,12},{20,24},{24,20},{28,32},{32,28},{36,40... | collective-permute-start | bytes 3145736 | tf_op jit(solution)/shard_map/ppermute | solution.py:311
  17.4 1.6 %copy-start.2 = (bf16[512,2048]{1,0:T(8,128)(2,1)S(1)}, bf16[512,2048]{1,0:T(8,128)(2,1)}, u32[]{:S(2)}) copy-start(bf16[512,2048]{1,0:T(8,128)(2,1)} %copy-done.1) | copy-start | bytes 6291460
  22.2 8.4 %copy-start.3 = (bf16[512,2048]{1,0:T(8,128)(2,1)S(1)}, bf16[512,2048]{1,0:T(8,128)(2,1)}, u32[]{:S(2)}) copy-start(bf16[512,2048]{1,0:T(8,128)(2,1)} %copy-done.1) | copy-start | bytes 6291460
  25.2 16.0 %collective-permute-start.6 = (bf16[64,2048]{1,0:T(8,128)(2,1)S(1)}, bf16[64,2048]{1,0:T(8,128)(2,1)S(1)}, u32[]{:S(2)}, u32[]{:S(2)}) collective-permute-start(bf16[64,2048]{1,0:T(8,128)(2,1)S(1)} %get-tuple-element.28), channel_id=1, source_target_pairs={{0,1},{1,2},{2,3},{3,0},{4,5},{5,6},{6,7},{7,4},{8,9},{9,10},{10,1... | collective-permute-start | bytes 786440 | tf_op jit(solution)/shard_map/ppermute | solution.py:313
  25.7 17.0 %collective-permute-start.7 = (bf16[64,2048]{1,0:T(8,128)(2,1)S(1)}, bf16[64,2048]{1,0:T(8,128)(2,1)S(1)}, u32[]{:S(2)}, u32[]{:S(2)}) collective-permute-start(bf16[64,2048]{1,0:T(8,128)(2,1)S(1)} %get-tuple-element.29), channel_id=1, source_target_pairs={{0,2},{1,3},{2,0},{3,1},{4,6},{5,7},{6,4},{7,5},{8,10},{9,11},{10,... | collective-permute-start | bytes 786440 | tf_op jit(solution)/shard_map/ppermute | solution.py:313
  29.1 13.5 %collective-permute-start.8 = (bf16[64,2048]{1,0:T(8,128)(2,1)S(1)}, bf16[64,2048]{1,0:T(8,128)(2,1)S(1)}, u32[]{:S(2)}, u32[]{:S(2)}) collective-permute-start(bf16[64,2048]{1,0:T(8,128)(2,1)S(1)} %get-tuple-element.30), channel_id=1, source_target_pairs={{0,3},{1,0},{2,1},{3,2},{4,7},{5,4},{6,5},{7,6},{8,11},{9,8},{10,9... | collective-permute-start | bytes 786440 | tf_op jit(solution)/shard_map/ppermute | solution.py:313
  33.9 8.8 %copy-start.5 = (f32[2048]{0:T(1024)S(1)}, f32[2048]{0:T(1024)}, u32[]{:S(2)}) copy-start(f32[2048]{0:T(1024)} %param.8) | copy-start | bytes 24580
  37.2 13.3 %collective-permute-start.3 = (bf16[64,2048]{1,0:T(8,128)(2,1)S(1)}, bf16[64,2048]{1,0:T(8,128)(2,1)S(1)}, u32[]{:S(2)}, u32[]{:S(2)}) collective-permute-start(bf16[64,2048]{1,0:T(8,128)(2,1)S(1)} %get-tuple-element.24), channel_id=1, source_target_pairs={{0,1},{1,2},{2,3},{3,0},{4,5},{5,6},{6,7},{7,4},{8,9},{9,10},{10,1... | collective-permute-start | bytes 786440 | tf_op jit(solution)/shard_map/ppermute | solution.py:313
  37.7 13.0 %collective-permute-start.4 = (bf16[64,2048]{1,0:T(8,128)(2,1)S(1)}, bf16[64,2048]{1,0:T(8,128)(2,1)S(1)}, u32[]{:S(2)}, u32[]{:S(2)}) collective-permute-start(bf16[64,2048]{1,0:T(8,128)(2,1)S(1)} %get-tuple-element.25), channel_id=1, source_target_pairs={{0,2},{1,3},{2,0},{3,1},{4,6},{5,7},{6,4},{7,5},{8,10},{9,11},{10,... | collective-permute-start | bytes 786440 | tf_op jit(solution)/shard_map/ppermute | solution.py:313
  41.1 9.6 %collective-permute-start.5 = (bf16[64,2048]{1,0:T(8,128)(2,1)S(1)}, bf16[64,2048]{1,0:T(8,128)(2,1)S(1)}, u32[]{:S(2)}, u32[]{:S(2)}) collective-permute-start(bf16[64,2048]{1,0:T(8,128)(2,1)S(1)} %get-tuple-element.26), channel_id=1, source_target_pairs={{0,3},{1,0},{2,1},{3,2},{4,7},{5,4},{6,5},{7,6},{8,11},{9,8},{10,9... | collective-permute-start | bytes 786440 | tf_op jit(solution)/shard_map/ppermute | solution.py:313
  43.4 11.0 %collective-permute-start.9 = (bf16[64,2048]{1,0:T(8,128)(2,1)S(1)}, bf16[64,2048]{1,0:T(8,128)(2,1)S(1)}, u32[]{:S(2)}, u32[]{:S(2)}) collective-permute-start(bf16[64,2048]{1,0:T(8,128)(2,1)S(1)} %combine.2.refs_0_), channel_id=1, source_target_pairs={{4,8},{8,4},{12,16},{16,12},{20,24},{24,20},{28,32},{32,28},{36,40... | collective-permute-start | bytes 786440 | tf_op jit(solution)/shard_map/ppermute | solution.py:311
  55.1 10.3 %collective-permute-start.10 = (bf16[128,2048]{1,0:T(8,128)(2,1)S(1)}, bf16[128,2048]{1,0:T(8,128)(2,1)S(1)}, u32[]{:S(2)}, u32[]{:S(2)}) collective-permute-start(bf16[128,2048]{1,0:T(8,128)(2,1)S(1)} %combine.3.mine), channel_id=1, source_target_pairs={{0,1},{1,2},{2,3},{3,0},{4,5},{5,6},{6,7},{7,4},{8,9},{9,10},{10,1... | collective-permute-start | bytes 1572872 | tf_op jit(solution)/shard_map/ppermute | solution.py:313
  55.2 12.4 %collective-permute-start.11 = (bf16[128,2048]{1,0:T(8,128)(2,1)S(1)}, bf16[128,2048]{1,0:T(8,128)(2,1)S(1)}, u32[]{:S(2)}, u32[]{:S(2)}) collective-permute-start(bf16[128,2048]{1,0:T(8,128)(2,1)S(1)} %combine.3.mine), channel_id=1, source_target_pairs={{0,3},{1,0},{2,1},{3,2},{4,7},{5,4},{6,5},{7,6},{8,11},{9,8},{10,9... | collective-permute-start | bytes 1572872 | tf_op jit(solution)/shard_map/ppermute | solution.py:313
  67.8 6.0 %collective-permute-start.14 = (bf16[384,2048]{1,0:T(8,128)(2,1)S(1)}, bf16[384,2048]{1,0:T(8,128)(2,1)S(1)}, u32[]{:S(2)}, u32[]{:S(2)}) collective-permute-start(bf16[384,2048]{1,0:T(8,128)(2,1)S(1)} %get-tuple-element.33.w_own), channel_id=1, source_target_pairs={{0,4},{4,0},{8,12},{12,8},{16,20},{20,16},{24,28},{28,24},{32,36},... | collective-permute-start | bytes 4718600 | tf_op jit(solution)/shard_map/ppermute | solution.py:312
  67.9 22.2 %collective-permute-start.16 = (bf16[320,2048]{1,0:T(8,128)(2,1)S(1)}, bf16[320,2048]{1,0:T(8,128)(2,1)S(1)}, u32[]{:S(2)}, u32[]{:S(2)}) collective-permute-start(bf16[320,2048]{1,0:T(8,128)(2,1)S(1)} %get-tuple-element.37), channel_id=1, source_target_pairs={{4,8},{8,4},{12,16},{16,12},{20,24},{24,20},{28,32},{32,28},{36,40... | collective-permute-start | bytes 3932168 | tf_op jit(solution)/shard_map/ppermute | solution.py:311
  71.1 9.0 %collective-permute-start.12 = (bf16[64,2048]{1,0:T(8,128)(2,1)S(1)}, bf16[64,2048]{1,0:T(8,128)(2,1)S(1)}, u32[]{:S(2)}, u32[]{:S(2)}) collective-permute-start(bf16[64,2048]{1,0:T(8,128)(2,1)S(1)} %get-tuple-element.31), channel_id=1, source_target_pairs={{0,1},{1,2},{2,3},{3,0},{4,5},{5,6},{6,7},{7,4},{8,9},{9,10},{10,1... | collective-permute-start | bytes 786440 | tf_op jit(solution)/shard_map/ppermute | solution.py:313
  71.3 8.8 %collective-permute-start.13 = (bf16[64,2048]{1,0:T(8,128)(2,1)S(1)}, bf16[64,2048]{1,0:T(8,128)(2,1)S(1)}, u32[]{:S(2)}, u32[]{:S(2)}) collective-permute-start(bf16[64,2048]{1,0:T(8,128)(2,1)S(1)} %get-tuple-element.32), channel_id=1, source_target_pairs={{0,3},{1,0},{2,1},{3,2},{4,7},{5,4},{6,5},{7,6},{8,11},{9,8},{10,9... | collective-permute-start | bytes 786440 | tf_op jit(solution)/shard_map/ppermute | solution.py:313
  80.1 4.7 %collective-permute-start.15 = (bf16[128,2048]{1,0:T(8,128)(2,1)S(1)}, bf16[128,2048]{1,0:T(8,128)(2,1)S(1)}, u32[]{:S(2)}, u32[]{:S(2)}) collective-permute-start(bf16[128,2048]{1,0:T(8,128)(2,1)S(1)} %join.1.w_op), channel_id=1, source_target_pairs={{0,4},{4,0},{8,12},{12,8},{16,20},{20,16},{24,28},{28,24},{32,36},... | collective-permute-start | bytes 1572872 | tf_op jit(solution)/shard_map/ppermute | solution.py:312
  80.6 15.2 %collective-permute-start.17 = (bf16[128,2048]{1,0:T(8,128)(2,1)S(1)}, bf16[128,2048]{1,0:T(8,128)(2,1)S(1)}, u32[]{:S(2)}, u32[]{:S(2)}) collective-permute-start(bf16[128,2048]{1,0:T(8,128)(2,1)S(1)} %join.1.w_op), channel_id=1, source_target_pairs={{4,8},{8,4},{12,16},{16,12},{20,24},{24,20},{28,32},{32,28},{36,40... | collective-permute-start | bytes 1572872 | tf_op jit(solution)/shard_map/ppermute | solution.py:311

commit v5 on v4

--- a/solution.py
+++ b/solution.py
@@ -52,13 +52,37 @@
     lax.fori_loop(0, count, step, 0)
 
 
-def each_of(source, src, count, body):
-    def one(s):
-        @pl.when(src[s] == source)
+def list_of(source, src, count, found):
+    def clear(n, carry):
+        found[n] = 0
+        return carry
+
+    def one(s, n):
+        here = src[s] == source
+
+        @pl.when(here)
         def _():
-            body(s)
-
-    each_live(count, one)
+            found[n] = s
+
+        return n + here.astype(jnp.int32)
+
+    lax.fori_loop(0, found.shape[0], clear, 0)
+    return lax.fori_loop(0, count, one, 0)
+
+
+UNROLL = 4
+
+
+def whole_steps(count):
+    return (count + UNROLL - 1) // UNROLL
+
+
+def in_steps(count, body):
+    def step(t, carry):
+        body([UNROLL * t + n for n in range(UNROLL)])
+        return carry
+
+    lax.fori_loop(0, whole_steps(count), step, 0)
 
 
 def over_rows(a, b):
@@ -111,15 +135,20 @@
     )(src)
 
 
-def far_image_kernel(meta, src, blk, col, acc, x_far, tiles, own, send_1, send_2, send_3, total):
+def far_image_kernel(meta, src, blk, col, acc, x_far, tiles, own, send_1, send_2, send_3, total, found):
     rows = total.shape[0]
     part = rows // 4
     total[...] = acc[...]
 
-    def add(s):
-        total[:, block(col[s])] += jnp.dot(x_far[:, block(blk[s])], tiles[s], preferred_element_type=F32)
-
-    each_of(FAR, src, meta[0], add)
+    count = list_of(FAR, src, meta[0], found)
+
+    def add(places):
+        slots = [found[n] for n in places]
+        products = [jnp.dot(x_far[:, block(blk[s])], tiles[s], preferred_element_type=F32) for s in slots]
+        for n, s, product in zip(places, slots, products, strict=True):
+            total[:, block(col[s])] += jnp.where(n < count, product, 0.0)
+
+    in_steps(count, add)
     for k, out in enumerate((own, send_1, send_2, send_3)):
         at = pl.ds(pl.multiple_of(lax.rem(meta[1] + k, 4) * part, part), part)
         out[...] = total[at, :].astype(out.dtype)
@@ -141,58 +170,58 @@
     out[joined:, :] = combined(first, meta, own, (got_1, got_2, got_3), samples, diag)
 
 
-def stack_kernel(mine, below, above, most, rest, go_up, go_down):
+def stack_kernel(mine, below, above, sides, rest, go_up, go_down):
     part = below.shape[0]
     half = part // 2
-    for n, piece in enumerate((mine, below, above)):
-        most[n * part : (n + 1) * part, :] = piece[...]
-    rest[...] = most[most.shape[0] - rest.shape[0] :, :]
+    ours = rest.shape[0] - 2 * part
+    rest[:ours, :] = mine[part - ours :, :]
+    for out, at in ((sides, 0), (rest, ours)):
+        out[at : at + part, :] = below[...]
+        out[at + part : at + 2 * part, :] = above[...]
     go_up[...] = below[:half, :]
     go_down[...] = above[half:, :]
 
 
-def join_kernel(op_a, op_b, _, out):
+def join_kernel(op_a, op_b, out):
     half = op_a.shape[0]
     out[:half, :] = op_a[...]
     out[half:, :] = op_b[...]
 
 
 def reorder_kernel(meta, x_own, x_near, *refs):
-    *x_far, out = refs
-    to = 0
-    for rep in REPS:
-        first = 0
-        for far in x_far:
-            rows = far.shape[0]
-            part = rows // 4
-            at = pl.multiple_of(lax.rem(meta[1] + rep, 4) * part, part)
-            out[OWN, to : to + part, :] = x_own[pl.ds(first + at, part), :]
-            out[FAR, to : to + part, :] = far[pl.ds(at, part), :]
-            out[NEAR, to : to + part, :] = x_near[pl.ds(first + at, part), :]
-            to += part
-            first += rows
-
-
-UNROLL = 4
-
-
-def whole_steps(count):
-    return (count + UNROLL - 1) // UNROLL
-
-
-def in_steps(count, body):
-    def step(t, carry):
-        body([UNROLL * t + n for n in range(UNROLL)])
-        return carry
-
-    lax.fori_loop(0, whole_steps(count), step, 0)
-
-
-def gradient(s, rows, src, blk, col, x, w_own, w_near):
+    *x_far, out, turned = refs
+    spans, first = [], 0
+    for far in x_far:
+        spans.append((first, far.shape[0] // 4))
+        first += far.shape[0]
+
+    def places():
+        for rep in REPS:
+            for c, (first, part) in enumerate(spans):
+                yield c, first, pl.multiple_of(lax.rem(meta[1] + rep, 4) * part, part), part
+
+    def turn(n, carry):
+        at = block(n)
+        own, far, near = [], [], []
+        for c, first, row, part in places():
+            own.append(x_own[pl.ds(first + row, part), at])
+            far.append(x_far[c][pl.ds(row, part), at])
+            near.append(x_near[pl.ds(first + row, part), at])
+        own = jnp.concatenate(own, axis=0)
+        out[:, at] = own
+        turned[OWN, at, :] = own.T
+        turned[FAR, at, :] = jnp.concatenate(far, axis=0).T
+        turned[NEAR, at, :] = jnp.concatenate(near, axis=0).T
+        return carry
+
+    lax.fori_loop(0, out.shape[1] // B, turn, 0)
+
+
+def gradient(s, src, blk, col, x, turned, w_own, w_near):
     k = src[s]
     at_i, at_j = block(blk[s]), block(col[s])
-    one = over_rows(x[k, rows, at_i], w_own[:, at_j])
-    two = over_rows(jnp.where(k == NEAR, w_near[:, at_i], w_own[:, at_i]), x[OWN, rows, at_j])
+    one = jnp.dot(turned[k, at_i, :], w_own[:, at_j], preferred_element_type=F32)
+    two = over_rows(jnp.where(k == NEAR, w_near[:, at_i], w_own[:, at_i]), x[:, at_j])
     return one + jnp.where(k == FAR, 0.0, two)
 
 
@@ -200,21 +229,15 @@
     return jnp.sum(x.astype(F32) * w.astype(F32), axis=0, keepdims=True)
 
 
-def first_update_kernel(meta, src, blk, col, x, w_own, w_near, acc, dots):
-    rows = slice(0, w_own.shape[0])
-
-    def add(slots):
-        for s in slots:
-            acc[s] = gradient(s, rows, src, blk, col, x, w_own, w_near)
-
-    in_steps(meta[0], add)
-    dots[...] = column_dots(x[OWN, rows], w_own[...])
-
-
-def own_update_kernel(meta, src, blk, col, x, w_op, near_op, acc, tiles, diag, dots, out, moved, new_diag, out_v, sem):
-    samples = x.shape[1]
+def own_update_kernel(meta, src, blk, col, x, turned, mine, sides, op, near_mine, near_sides, near_op, tiles, diag,
+                      out, moved, new_diag, w_own, w_near, out_v, sem):
+    samples = x.shape[0]
     slots = tiles.shape[0]
-    rows = slice(samples - w_op.shape[0], samples)
+    for w, pieces in ((w_own, (mine, sides, op)), (w_near, (near_mine, near_sides, near_op))):
+        at = 0
+        for piece in pieces:
+            w[at : at + piece.shape[0], :] = piece[...]
+            at += piece.shape[0]
     scale = STEP / (2.0 * samples)
     count = meta[0]
     whole = whole_steps(count) * UNROLL
@@ -231,7 +254,7 @@
         return jnp.logical_or(s >= count, src[s] != FAR)
 
     def finish(s):
-        value = tiles[s].astype(F32) - (acc[s] + gradient(s, rows, src, blk, col, x, w_op, near_op)) * scale
+        value = tiles[s].astype(F32) - gradient(s, src, blk, col, x, turned, w_own, w_near) * scale
         moved[s] = value
         out_v[s] = jnp.where(s < count, soft(value), jnp.zeros((B, B), BF16))
 
@@ -245,7 +268,7 @@
                 save(s).start()
 
     in_steps(count, step)
-    total = dots[...] + column_dots(x[OWN, rows], w_op[...])
+    total = column_dots(x[...], w_own[...])
     d = diag[...]
     new_diag[...] = d - STEP * (total / samples - 1.0 / d)
 
@@ -277,21 +300,28 @@
 
 
 def far_update_kernel(meta, src, blk, col, x, moved, *rest):
-    *pieces, _, out, w, out_v, sem = rest
-    scale = STEP / (2.0 * x.shape[1])
+    *pieces, _, out, w, out_v, sem, found = rest
+    scale = STEP / (2.0 * x.shape[0])
     at = 0
     for piece in pieces:
         w[at : at + piece.shape[0], :] = piece[...]
         at += piece.shape[0]
-    save = lambda s: pltpu.make_async_copy(out_v.at[s], out.at[s], sem.at[s])
-
-    def finish(s):
-        grad = over_rows(w[:, block(blk[s])], x[OWN, :, block(col[s])])
-        out_v[s] = soft(moved[s] - grad * scale)
-        save(s).start()
-
-    each_of(FAR, src, meta[0], finish)
-    each_of(FAR, src, meta[0], lambda s: save(s).wait())
+    count = list_of(FAR, src, meta[0], found)
+    save = lambda n: pltpu.make_async_copy(out_v.at[n], out.at[found[n]], sem.at[n])
+
+    def finish(places):
+        for n in places:
+            s = found[n]
+            grad = over_rows(w[:, block(blk[s])], x[:, block(col[s])])
+            out_v[n] = soft(moved[s] - grad * scale)
+        for n in places:
+
+            @pl.when(n < count)
+            def _():
+                save(n).start()
+
+    in_steps(count, finish)
+    each_live(count, lambda n: save(n).wait())
 
 
 def shards(samples, theta_tiles, theta_diag, tile_row, tile_col, tile_count):
@@ -333,9 +363,9 @@
         )(*index, x_own, x_near, theta_tiles)
         for first, rows in zip(firsts, CHUNKS, strict=True)
     ]
-    x_all = call(
-        reorder_kernel, "reorder", like((3, count_ns, width), BF16), [SMEM] + [VMEM] * (2 + len(CHUNKS)), VMEM,
-        0, 2 << 20,
+    x_rows, x_turned = call(
+        reorder_kernel, "reorder", [like((count_ns, width), BF16), like((3, width, count_ns), BF16)],
+        [SMEM] + [VMEM] * (2 + len(CHUNKS)), [VMEM] * 2, 0, 0,
     )(meta, x_own, x_near, *x_far)
 
     joined, done, before = [], 0, []
@@ -345,12 +375,12 @@
             far_image_kernel, "far_image",
             [like((part, width), F32)] + [like((part, width), BF16)] * 3,
             [SMEM] * 4 + [VMEM] * 3, [VMEM] * 4, slots * dot // 4, 1 << 20,
-            [pltpu.VMEM((rows, width), F32)],
+            [pltpu.VMEM((rows, width), F32), pltpu.SMEM((slots,), jnp.int32)],
         )(*index, accs[c], x_far[c], theta_tiles)
         got = [up(send, k + 1) for k, send in enumerate(sends)]
         if c + 1 == len(CHUNKS):
             far_first = swap_far(joined[0])
-            before = [far_first, x_all]
+            before = [far_first, x_rows]
         joined = [
             call(
                 functools.partial(combine_kernel, first, done), "combine", like((done + part, width), BF16),
@@ -359,40 +389,34 @@
         ]
         done += part
     w_mine = joined[0]
-    w_most, w_rest, go_up, go_down = call(
+    w_sides, w_rest, go_up, go_down = call(
         stack_kernel, "stack",
-        [like((3 * quarter, width), BF16), like((2 * quarter + part, width), BF16)]
+        [like((2 * quarter, width), BF16), like((2 * quarter + part, width), BF16)]
         + [like((quarter // 2, width), BF16)] * 2,
-        [VMEM] * 3, [VMEM] * 4, 0, 1 << 20,
+        [VMEM] * 3, [VMEM] * 4, 0, 0,
     )(w_mine, up(w_mine, 1), up(w_mine, 3))
-    far_rest, near_most = swap_far(w_rest), swap_near(w_most)
-    op_a, op_b = up(go_up, 1), up(go_down, 3)
-
-    acc, dots = call(
-        first_update_kernel, "first_update",
-        [like(theta_tiles.shape, F32), like((1, width), F32)],
-        [SMEM] * 4 + [VMEM] * 3, [VMEM] * 2, slots * dot, 4 << 20,
-    )(*index, x_all, w_most, near_most)
-
+    far_rest = swap_far(w_rest)
     w_op = call(
-        join_kernel, "join", like((quarter, width), BF16), [VMEM] * 2 + [ANY], VMEM, 0, 1 << 20,
-    )(op_a, op_b, acc)
+        join_kernel, "join", like((quarter, width), BF16), [VMEM] * 2, VMEM, 0, 0,
+    )(up(go_up, 1), up(go_down, 3))
     far_op = swap_far(w_op)
+    w_own = (w_mine, w_sides, w_op)
 
     new_tiles, moved, new_diag = call(
         own_update_kernel, "own_update",
         [like(theta_tiles.shape, BF16), like(theta_tiles.shape, F32), like((1, width), F32)],
-        [SMEM] * 4 + [VMEM] * 7, [HBM, VMEM, VMEM], slots * dot, 4 << 20,
-        [pltpu.VMEM(theta_tiles.shape, BF16), DMA((slots,))],
-    )(*index, x_all, w_op, swap_near(w_op), acc, theta_tiles, diag, dots)
+        [SMEM] * 4 + [VMEM] * 10, [HBM, VMEM, VMEM], 0, 0,
+        [pltpu.VMEM((count_ns, width), BF16)] * 2 + [pltpu.VMEM(theta_tiles.shape, BF16), DMA((slots,))], vmem=14,
+    )(*index, x_rows, x_turned, *w_own, *[swap_near(w) for w in w_own], theta_tiles, diag)
 
     far_pieces = [far_first, far_rest, far_op]
     new_tiles = call(
         far_update_kernel, "far_update", like(theta_tiles.shape, BF16),
         [SMEM] * 4 + [VMEM] * (2 + len(far_pieces)) + [HBM], HBM, slots * dot // 4, 2 << 20,
-        [pltpu.VMEM((count_ns, width), BF16), pltpu.VMEM(theta_tiles.shape, BF16), DMA((slots,))],
+        [pltpu.VMEM((count_ns, width), BF16), pltpu.VMEM(theta_tiles.shape, BF16), DMA((slots,)),
+         pltpu.SMEM((slots,), jnp.int32)],
         {6 + len(far_pieces): 0},
-    )(*index, x_all, moved, *far_pieces, new_tiles)
+    )(*index, x_rows, moved, *far_pieces, new_tiles)
     return new_tiles, new_diag.reshape(width)
 
 

time: 99.2 us -> 98.6 us (level)
  Pallas kernels: 30.5 us -> 27.2 us
  starting transfers between devices: 38.9 us -> 41.2 us
    ppermute x10, waiting for transfers between devices: 11.7 us -> 15.4 us  [shards(): lax.ppermute(v, 'rep', [(i, (i + n) % reps) for i in range(reps)])]
    ppermute x5, waiting for transfers between devices: 11.9 us -> 8.3 us  [shards(): swap_far = lambda v: lax.ppermute(v, 'blk', far)]
    pallas_call x4 -> x3, Pallas kernels: 7.08 us -> 4.17 us  [the longest x1 3.95 us: shards(): call(reorder_kernel, 'reorder', [like((count_ns, width), BF16), like((3,...]
    ppermute x5, starting transfers between devices: 21.2 us -> 22.6 us  [shards(): swap_far = lambda v: lax.ppermute(v, 'blk', far)]
    ppermute x3 -> x4, starting transfers between devices: 1.32 us -> 2.49 us  [shards(): swap_near = lambda v: lax.ppermute(v, 'blk', near)]
    pallas_call x1, Pallas kernels: 4.34 us -> 5.34 us  [shards(): call(own_update_kernel, 'own_update', [like(theta_tiles.shape, BF16), lik...]
  transfers between devices with their start and end apart: 18 -> 19, of which waited for: 9 -> 7; matrix products, arithmetic and copies ran while one was open for 0% -> 0% of each run, Pallas kernels for 26% -> 24%
where the time goes in v5:
time: 98.6 us; the launch traced here: 98.4 us
  starting transfers between devices  41.2 us (42%)
  Pallas kernels  27.2 us (28%)
  waiting for transfers between devices  23.7 us (24%)
  local copies, waits for them, and re-layouts  4.51 us (5%)
  between operations  1.72 us (2%)
    ppermute x5, starting transfers between devices, shards(): swap_far = lambda v: lax.ppermute(v, 'blk', far)  22.6 us
    ppermute x10, starting transfers between devices, shards(): lax.ppermute(v, 'rep', [(i, (i + n) % reps) for i in range(reps)])  16.1 us
    ppermute x10, waiting for transfers between devices, shards(): lax.ppermute(v, 'rep', [(i, (i + n) % reps) for i in range(reps)])  15.4 us
    ppermute x5, waiting for transfers between devices, shards(): swap_far = lambda v: lax.ppermute(v, 'blk', far)  8.3 us
    pallas_call x2, Pallas kernels, shards(): call(functools.partial(own_image_kernel, first), 'own_image', like((rows,...  5.78 us
    pallas_call x1, Pallas kernels, shards(): call(own_update_kernel, 'own_update', [like(theta_tiles.shape, BF16), lik...  5.34 us
    unnamed x16, local copies, waits for them, and re-layouts  4.51 us
    pallas_call x2, Pallas kernels, shards(): call(far_image_kernel, 'far_image', [like((part, width), F32)] + [like((p...  4.15 us
  transfers between devices with their start and end apart: 19, of which 7 were waited for; matrix products, arithmetic and copies ran while one was open for 0% of the time, Pallas kernels for 24%

profile of v5, /device:TPU:103, one launch (start us, length us, event | category | flops | bytes accessed | tf_op | source)
XLA Modules:
  0.0 98.4 jit_solution(554052236386667582)
XLA Ops:
  0.6 0.8 collective-permute-start
  1.4 2.0 %load.3 = bf16[256,2048]{1,0:T(8,128)(2,1)} custom-call(bf16[512,2048]{1,0:T(8,128)(2,1)} %src.3), custom_call_target="tpu_custom_call" | custom-call | bytes 1048576 | tf_op jit(solution)/shard_map/load/pallas_call | solution.py:124
  3.4 0.0 copy-start
  3.5 4.7 %collective-permute-start.1 = (bf16[256,2048]{1,0:T(8,128)(2,1)}, bf16[256,2048]{1,0:T(8,128)(2,1)S(1)}, u32[]{:S(2)}, u32[]{:S(2)}) collective-permute-start(bf16[256,2048]{1,0:T(8,128)(2,1)} %load.3), channel_id=1, source_target_pairs={{4,8},{8,4},{12,16},{16,12},{20,24},{24,20},{28,32},{32,28},{36,40... | collective-permute-start | bytes 3145736 | tf_op jit(solution)/shard_map/ppermute | solution.py:341
  8.2 0.0 copy-start.4
  8.2 1.6 %copy-done.4 = bf16[512,2048]{1,0:T(8,128)(2,1)S(1)} copy-done((bf16[512,2048]{1,0:T(8,128)(2,1)S(1)}, bf16[512,2048]{1,0:T(8,128)(2,1)}, u32[]{:S(2)}) %copy-start.4) | copy-done | bytes 2097176
  9.8 1.2 %load.2 = (bf16[512,2048]{1,0:T(8,128)(2,1)S(1)}, bf16[256,2048]{1,0:T(8,128)(2,1)}) custom-call(bf16[512,2048]{1,0:T(8,128)(2,1)S(1)} %copy-done.4), custom_call_target="tpu_custom_call" | custom-call | flops 2147483648 | bytes 1048576 | tf_op jit(solution)/shard_map/load/pallas_call | solution.py:131
  11.0 0.0 copy-start.1
  11.0 1.3 %copy-done.1 = bf16[512,2048]{1,0:T(8,128)(2,1)} copy-done((bf16[512,2048]{1,0:T(8,128)(2,1)}, bf16[512,2048]{1,0:T(8,128)(2,1)S(1)}, u32[]{:S(2)}) %copy-start.1) | copy-done | bytes 2097176
  12.3 4.3 %collective-permute-start.2 = (bf16[256,2048]{1,0:T(8,128)(2,1)}, bf16[256,2048]{1,0:T(8,128)(2,1)}, u32[]{:S(2)}, u32[]{:S(2)}) collective-permute-start(bf16[256,2048]{1,0:T(8,128)(2,1)} %get-tuple-element.22), channel_id=1, source_target_pairs={{4,8},{8,4},{12,16},{16,12},{20,24},{24,20},{28,32},{32,28},{36,40... | collective-permute-start | bytes 3145736 | tf_op jit(solution)/shard_map/ppermute | solution.py:341
  17.3 0.1 pad_add_fusion.meta
  17.3 0.0 copy-done.7
  17.4 0.0 collective-permute-done.x_near
  17.4 0.0 copy-done
  17.4 0.0 copy-done.6
  17.4 0.0 copy-start.2
  17.4 1.6 %copy-done.2 = bf16[512,2048]{1,0:T(8,128)(2,1)S(1)} copy-done((bf16[512,2048]{1,0:T(8,128)(2,1)S(1)}, bf16[512,2048]{1,0:T(8,128)(2,1)}, u32[]{:S(2)}) %copy-start.2) | copy-done | bytes 2097176
  19.0 2.9 %own_image.3.acc = f32[256,2048]{1,0:T(8,128)S(1)} custom-call(s32[2]{0:T(128)S(1)} %pad_add_fusion.meta, s32[16]{0:T(128)S(1)} %get-tuple-element.41.src, s32[16]{0:T(128)S(1)} %get-tuple-element.40.blk, s32[16]{0:T(128)S(1)} %copy-done.6, bf16[512,2048]{1,0:T(8,128)(2,1)S(1)} %copy-done.2, bf16[512,2048]{1,0:T(8,128)(2,1)} %collective-permute-done.x_near, ...), custom_call_target="tpu_custom_call" | custom-call | flops 1073741824 | bytes 4194304 | tf_op jit(solution)/shard_map/own_image/pallas_call | solution.py:360
  21.9 0.0 copy-start.3
  21.9 1.3 %collective-permute-done.1.refs_0_.x_far = bf16[256,2048]{1,0:T(8,128)(2,1)S(1)} collective-permute-done((bf16[256,2048]{1,0:T(8,128)(2,1)}, bf16[256,2048]{1,0:T(8,128)(2,1)S(1)}, u32[]{:S(2)}, u32[]{:S(2)}) %collective-permute-start.1) | collective-permute-done | bytes 1048608 | tf_op jit(solution)/shard_map/ppermute | solution.py:341
  23.2 1.7 %far_image.3 = (f32[64,2048]{1,0:T(8,128)S(1)}, bf16[64,2048]{1,0:T(8,128)(2,1)S(1)}, bf16[64,2048]{1,0:T(8,128)(2,1)S(1)}, bf16[64,2048]{1,0:T(8,128)(2,1)S(1)}) custom-call(s32[2]{0:T(128)S(1)} %pad_add_fusion.meta, s32[16]{0:T(128)S(1)} %get-tuple-element.41.src, s32[16]{0:T(128)S(1)} %get-tuple-element.40.blk, s32[16]{0:T(128)S(1)} %copy-done.6, ...), custom_call_target="tpu_custom_call" | custom-call | flops 268435456 | bytes 1048576 | tf_op jit(solution)/shard_map/far_image/pallas_call | solution.py:374
  25.0 1.0 %collective-permute-start.6 = (bf16[64,2048]{1,0:T(8,128)(2,1)S(1)}, bf16[64,2048]{1,0:T(8,128)(2,1)S(1)}, u32[]{:S(2)}, u32[]{:S(2)}) collective-permute-start(bf16[64,2048]{1,0:T(8,128)(2,1)S(1)} %get-tuple-element.30), channel_id=1, source_target_pairs={{0,1},{1,2},{2,3},{3,0},{4,5},{5,6},{6,7},{7,4},{8,9},{9,10},{10,1... | collective-permute-start | bytes 786440 | tf_op jit(solution)/shard_map/ppermute | solution.py:343
  26.0 2.7 %collective-permute-start.7 = (bf16[64,2048]{1,0:T(8,128)(2,1)S(1)}, bf16[64,2048]{1,0:T(8,128)(2,1)S(1)}, u32[]{:S(2)}, u32[]{:S(2)}) collective-permute-start(bf16[64,2048]{1,0:T(8,128)(2,1)S(1)} %get-tuple-element.31), channel_id=1, source_target_pairs={{0,2},{1,3},{2,0},{3,1},{4,6},{5,7},{6,4},{7,5},{8,10},{9,11},{10,... | collective-permute-start | bytes 786440 | tf_op jit(solution)/shard_map/ppermute | solution.py:343
  28.7 1.4 %collective-permute-start.8 = (bf16[64,2048]{1,0:T(8,128)(2,1)S(1)}, bf16[64,2048]{1,0:T(8,128)(2,1)S(1)}, u32[]{:S(2)}, u32[]{:S(2)}) collective-permute-start(bf16[64,2048]{1,0:T(8,128)(2,1)S(1)} %get-tuple-element.32), channel_id=1, source_target_pairs={{0,3},{1,0},{2,1},{3,2},{4,7},{5,4},{6,5},{7,6},{8,11},{9,8},{10,9... | collective-permute-start | bytes 786440 | tf_op jit(solution)/shard_map/ppermute | solution.py:343
  30.1 0.0 copy-done.3
  30.1 2.9 %own_image.2.acc = f32[256,2048]{1,0:T(8,128)S(1)} custom-call(s32[2]{0:T(128)S(1)} %pad_add_fusion.meta, s32[16]{0:T(128)S(1)} %get-tuple-element.41.src, s32[16]{0:T(128)S(1)} %get-tuple-element.40.blk, s32[16]{0:T(128)S(1)} %copy-done.6, bf16[512,2048]{1,0:T(8,128)(2,1)S(1)} %copy-done.3, bf16[512,2048]{1,0:T(8,128)(2,1)} %collective-permute-done.x_near, ...), custom_call_target="tpu_custom_call" | custom-call | flops 1073741824 | bytes 4194304 | tf_op jit(solution)/shard_map/own_image/pallas_call | solution.py:360
  33.0 0.0 copy-start.5
  33.0 1.6 %collective-permute-done.2.refs_1_.x_far = bf16[256,2048]{1,0:T(8,128)(2,1)} collective-permute-done((bf16[256,2048]{1,0:T(8,128)(2,1)}, bf16[256,2048]{1,0:T(8,128)(2,1)}, u32[]{:S(2)}, u32[]{:S(2)}) %collective-permute-start.2) | collective-permute-done | bytes 1048608 | tf_op jit(solution)/shard_map/ppermute | solution.py:341
  34.6 2.4 %far_image.2 = (f32[64,2048]{1,0:T(8,128)S(1)}, bf16[64,2048]{1,0:T(8,128)(2,1)S(1)}, bf16[64,2048]{1,0:T(8,128)(2,1)S(1)}, bf16[64,2048]{1,0:T(8,128)(2,1)S(1)}) custom-call(s32[2]{0:T(128)S(1)} %pad_add_fusion.meta, s32[16]{0:T(128)S(1)} %get-tuple-element.41.src, s32[16]{0:T(128)S(1)} %get-tuple-element.40.blk, s32[16]{0:T(128)S(1)} %copy-done.6, ...), custom_call_target="tpu_custom_call" | custom-call | flops 268435456 | bytes 1048576 | tf_op jit(solution)/shard_map/far_image/pallas_call | solution.py:374
  37.0 1.0 %collective-permute-start.3 = (bf16[64,2048]{1,0:T(8,128)(2,1)S(1)}, bf16[64,2048]{1,0:T(8,128)(2,1)S(1)}, u32[]{:S(2)}, u32[]{:S(2)}) collective-permute-start(bf16[64,2048]{1,0:T(8,128)(2,1)S(1)} %get-tuple-element.26), channel_id=1, source_target_pairs={{0,1},{1,2},{2,3},{3,0},{4,5},{5,6},{6,7},{7,4},{8,9},{9,10},{10,1... | collective-permute-start | bytes 786440 | tf_op jit(solution)/shard_map/ppermute | solution.py:343
  38.0 2.7 %collective-permute-start.4 = (bf16[64,2048]{1,0:T(8,128)(2,1)S(1)}, bf16[64,2048]{1,0:T(8,128)(2,1)S(1)}, u32[]{:S(2)}, u32[]{:S(2)}) collective-permute-start(bf16[64,2048]{1,0:T(8,128)(2,1)S(1)} %get-tuple-element.27), channel_id=1, source_target_pairs={{0,2},{1,3},{2,0},{3,1},{4,6},{5,7},{6,4},{7,5},{8,10},{9,11},{10,... | collective-permute-start | bytes 786440 | tf_op jit(solution)/shard_map/ppermute | solution.py:343
  40.7 0.0 collective-permute-done.6.got_1
  40.7 1.4 %collective-permute-start.5 = (bf16[64,2048]{1,0:T(8,128)(2,1)S(1)}, bf16[64,2048]{1,0:T(8,128)(2,1)S(1)}, u32[]{:S(2)}, u32[]{:S(2)}) collective-permute-start(bf16[64,2048]{1,0:T(8,128)(2,1)S(1)} %get-tuple-element.28), channel_id=1, source_target_pairs={{0,3},{1,0},{2,1},{3,2},{4,7},{5,4},{6,5},{7,6},{8,11},{9,8},{10,9... | collective-permute-start | bytes 786440 | tf_op jit(solution)/shard_map/ppermute | solution.py:343
  42.1 0.0 collective-permute-done.7.got_2
  42.1 0.0 collective-permute-done.8.got_3
  42.1 0.7 combine.2.refs_0_
  42.9 5.0 %collective-permute-start.9 = (bf16[64,2048]{1,0:T(8,128)(2,1)S(1)}, bf16[64,2048]{1,0:T(8,128)(2,1)S(1)}, u32[]{:S(2)}, u32[]{:S(2)}) collective-permute-start(bf16[64,2048]{1,0:T(8,128)(2,1)S(1)} %combine.2.refs_0_), channel_id=1, source_target_pairs={{4,8},{8,4},{12,16},{16,12},{20,24},{24,20},{28,32},{32,28},{36,40... | collective-permute-start | bytes 786440 | tf_op jit(solution)/shard_map/ppermute | solution.py:341
  47.9 4.0 %reorder.1 = (bf16[512,2048]{1,0:T(8,128)(2,1)S(1)}, bf16[3,2048,512]{2,1,0:T(8,128)(2,1)S(1)}) custom-call(s32[2]{0:T(128)S(1)} %pad_add_fusion.meta, bf16[512,2048]{1,0:T(8,128)(2,1)S(1)} %copy-done.3, bf16[512,2048]{1,0:T(8,128)(2,1)} %collective-permute-done.x_near, bf16[256,2048]{1,0:T(8,128)(2,1)S(1)} %collective-permute-done.1.refs_0_.x_far, ...), custom_call_target="tpu_custom_call" | custom-call | tf_op jit(solution)/shard_map/reorder/pallas_call | solution.py:366
  51.9 0.0 collective-permute-done.3.got_1
  51.9 0.0 collective-permute-done.4.got_2
  51.9 0.0 collective-permute-done.5.got_3
  51.9 2.0 %collective-permute-done.9.refs_1_.rest_0_ = bf16[64,2048]{1,0:T(8,128)(2,1)S(1)} collective-permute-done((bf16[64,2048]{1,0:T(8,128)(2,1)S(1)}, bf16[64,2048]{1,0:T(8,128)(2,1)S(1)}, u32[]{:S(2)}, u32[]{:S(2)}) %collective-permute-start.9) | collective-permute-done | bytes 262176 | tf_op jit(solution)/shard_map/ppermute | solution.py:341
  53.9 0.7 combine.3.mine
  54.6 0.1 collective-permute-start.10
  54.7 2.6 %collective-permute-start.11 = (bf16[128,2048]{1,0:T(8,128)(2,1)S(1)}, bf16[128,2048]{1,0:T(8,128)(2,1)S(1)}, u32[]{:S(2)}, u32[]{:S(2)}) collective-permute-start(bf16[128,2048]{1,0:T(8,128)(2,1)S(1)} %combine.3.mine), channel_id=1, source_target_pairs={{0,3},{1,0},{2,1},{3,2},{4,7},{5,4},{6,5},{7,6},{8,11},{9,8},{10,9... | collective-permute-start | bytes 1572872 | tf_op jit(solution)/shard_map/ppermute | solution.py:343
  57.4 7.8 %collective-permute-done.10.below = bf16[128,2048]{1,0:T(8,128)(2,1)S(1)} collective-permute-done((bf16[128,2048]{1,0:T(8,128)(2,1)S(1)}, bf16[128,2048]{1,0:T(8,128)(2,1)S(1)}, u32[]{:S(2)}, u32[]{:S(2)}) %collective-permute-start.10) | collective-permute-done | bytes 524320 | tf_op jit(solution)/shard_map/ppermute | solution.py:343
  65.2 1.9 %collective-permute-done.11.above = bf16[128,2048]{1,0:T(8,128)(2,1)S(1)} collective-permute-done((bf16[128,2048]{1,0:T(8,128)(2,1)S(1)}, bf16[128,2048]{1,0:T(8,128)(2,1)S(1)}, u32[]{:S(2)}, u32[]{:S(2)}) %collective-permute-start.11) | collective-permute-done | bytes 524320 | tf_op jit(solution)/shard_map/ppermute | solution.py:343
  67.1 0.2 stack.9
  67.3 3.0 %collective-permute-start.17 = (bf16[320,2048]{1,0:T(8,128)(2,1)S(1)}, bf16[320,2048]{1,0:T(8,128)(2,1)S(1)}, u32[]{:S(2)}, u32[]{:S(2)}) collective-permute-start(bf16[320,2048]{1,0:T(8,128)(2,1)S(1)} %get-tuple-element.37), channel_id=1, source_target_pairs={{4,8},{8,4},{12,16},{16,12},{20,24},{24,20},{28,32},{32,28},{36,40... | collective-permute-start | bytes 3932168 | tf_op jit(solution)/shard_map/ppermute | solution.py:341
  70.3 0.1 collective-permute-start.15
  70.4 0.1 collective-permute-start.12
  70.5 3.0 %collective-permute-start.13 = (bf16[64,2048]{1,0:T(8,128)(2,1)S(1)}, bf16[64,2048]{1,0:T(8,128)(2,1)S(1)}, u32[]{:S(2)}, u32[]{:S(2)}) collective-permute-start(bf16[64,2048]{1,0:T(8,128)(2,1)S(1)} %get-tuple-element.35), channel_id=1, source_target_pairs={{0,3},{1,0},{2,1},{3,2},{4,7},{5,4},{6,5},{7,6},{8,11},{9,8},{10,9... | collective-permute-start | bytes 786440 | tf_op jit(solution)/shard_map/ppermute | solution.py:343
  73.5 0.6 collective-permute-start.14
  74.1 5.6 %collective-permute-done.12.op_a = bf16[64,2048]{1,0:T(8,128)(2,1)S(1)} collective-permute-done((bf16[64,2048]{1,0:T(8,128)(2,1)S(1)}, bf16[64,2048]{1,0:T(8,128)(2,1)S(1)}, u32[]{:S(2)}, u32[]{:S(2)}) %collective-permute-start.12) | collective-permute-done | bytes 262176 | tf_op jit(solution)/shard_map/ppermute | solution.py:343
  79.7 0.0 collective-permute-done.13.op_b
  79.8 1.0 %collective-permute-start.16 = (bf16[128,2048]{1,0:T(8,128)(2,1)S(1)}, bf16[128,2048]{1,0:T(8,128)(2,1)S(1)}, u32[]{:S(2)}, u32[]{:S(2)}) collective-permute-start(bf16[128,2048]{1,0:T(8,128)(2,1)S(1)} %join.1.op), channel_id=1, source_target_pairs={{0,4},{4,0},{8,12},{12,8},{16,20},{20,16},{24,28},{28,24},{32,36},... | collective-permute-start | bytes 1572872 | tf_op jit(solution)/shard_map/ppermute | solution.py:342
  80.8 5.5 %collective-permute-start.18 = (bf16[128,2048]{1,0:T(8,128)(2,1)S(1)}, bf16[128,2048]{1,0:T(8,128)(2,1)S(1)}, u32[]{:S(2)}, u32[]{:S(2)}) collective-permute-start(bf16[128,2048]{1,0:T(8,128)(2,1)S(1)} %join.1.op), channel_id=1, source_target_pairs={{4,8},{8,4},{12,16},{16,12},{20,24},{24,20},{28,32},{32,28},{36,40... | collective-permute-start | bytes 1572872 | tf_op jit(solution)/shard_map/ppermute | solution.py:341
  86.4 0.0 collective-permute-done.14.near_mine
  86.4 0.0 collective-permute-done.16.near_op
  86.4 0.0 collective-permute-done.15.near_sides
  86.4 5.3 %own_update.1 = (bf16[16,256,256]{2,1,0:T(8,128)(2,1)}, f32[16,256,256]{2,1,0:T(8,128)S(1)}, f32[1,2048]{1,0:T(1,128)}) custom-call(s32[2]{0:T(128)S(1)} %pad_add_fusion.meta, s32[16]{0:T(128)S(1)} %get-tuple-element.41.src, s32[16]{0:T(128)S(1)} %get-tuple-element.40.blk, s32[16]{0:T(128)S(1)} %copy-done.6, ...), custom_call_target="tpu_custom_call" | custom-call | tf_op jit(solution)/shard_map/own_update/pallas_call | solution.py:405
  91.7 3.4 %collective-permute-done.18.rest_2_ = bf16[128,2048]{1,0:T(8,128)(2,1)S(1)} collective-permute-done((bf16[128,2048]{1,0:T(8,128)(2,1)S(1)}, bf16[128,2048]{1,0:T(8,128)(2,1)S(1)}, u32[]{:S(2)}, u32[]{:S(2)}) %collective-permute-start.18) | collective-permute-done | bytes 524320 | tf_op jit(solution)/shard_map/ppermute | solution.py:341
  95.2 0.0 collective-permute-done.17.rest_1_
  95.2 3.1 %far_update.1 = bf16[16,256,256]{2,1,0:T(8,128)(2,1)} custom-call(s32[2]{0:T(128)S(1)} %pad_add_fusion.meta, s32[16]{0:T(128)S(1)} %get-tuple-element.41.src, s32[16]{0:T(128)S(1)} %get-tuple-element.40.blk, s32[16]{0:T(128)S(1)} %copy-done.6, bf16[512,2048]{1,0:T(8,128)(2,1)S(1)} %get-tuple-element.23.refs_2_.x, ...), custom_call_target="tpu_custom_call", output_to_operand_aliasing={{}: (9, {})} | custom-call | flops 268435456 | bytes 2097152 | tf_op jit(solution)/shard_map/far_update/pallas_call | solution.py:413
  (5 shorter events, 0.1 us)
Async XLA Ops:
  0.6 16.7 %collective-permute-start = (bf16[512,2048]{1,0:T(8,128)(2,1)}, bf16[512,2048]{1,0:T(8,128)(2,1)}, u32[]{:S(2)}, u32[]{:S(2)}) collective-permute-start(bf16[512,2048]{1,0:T(8,128)(2,1)} %src.3), channel_id=1, source_target_pairs={{0,4},{4,0},{8,12},{12,8},{16,20},{20,16},{24,28},{28,24},{32,36},... | collective-permute-start | bytes 6291464 | tf_op jit(solution)/shard_map/ppermute | solution.py:342
  3.4 13.9 %copy-start = (bf16[16,256,256]{2,1,0:T(8,128)(2,1)S(1)}, bf16[16,256,256]{2,1,0:T(8,128)(2,1)}, u32[]{:S(2)}) copy-start(bf16[16,256,256]{2,1,0:T(8,128)(2,1)} %tiles.9) | copy-start | bytes 6291460
  3.5 19.8 %collective-permute-start.1 = (bf16[256,2048]{1,0:T(8,128)(2,1)}, bf16[256,2048]{1,0:T(8,128)(2,1)S(1)}, u32[]{:S(2)}, u32[]{:S(2)}) collective-permute-start(bf16[256,2048]{1,0:T(8,128)(2,1)} %load.3), channel_id=1, source_target_pairs={{4,8},{8,4},{12,16},{16,12},{20,24},{24,20},{28,32},{32,28},{36,40... | collective-permute-start | bytes 3145736 | tf_op jit(solution)/shard_map/ppermute | solution.py:341
  8.2 1.6 %copy-start.4 = (bf16[512,2048]{1,0:T(8,128)(2,1)S(1)}, bf16[512,2048]{1,0:T(8,128)(2,1)}, u32[]{:S(2)}) copy-start(bf16[512,2048]{1,0:T(8,128)(2,1)} %src.3) | copy-start | bytes 6291460
  9.8 7.6 %copy-start.7 = (s32[16]{0:T(128)S(1)}, s32[16]{0:T(128)}, u32[]{:S(2)}) copy-start(s32[16]{0:T(128)} %param.9) | copy-start | bytes 196
  9.8 7.6 %copy-start.6 = (s32[16]{0:T(128)S(1)}, s32[16]{0:T(128)}, u32[]{:S(2)}) copy-start(s32[16]{0:T(128)} %col.11) | copy-start | bytes 196
  11.0 1.3 %copy-start.1 = (bf16[512,2048]{1,0:T(8,128)(2,1)}, bf16[512,2048]{1,0:T(8,128)(2,1)S(1)}, u32[]{:S(2)}) copy-start(bf16[512,2048]{1,0:T(8,128)(2,1)S(1)} %get-tuple-element.21.x_own.samples) | copy-start | bytes 6291460
  12.3 22.3 %collective-permute-start.2 = (bf16[256,2048]{1,0:T(8,128)(2,1)}, bf16[256,2048]{1,0:T(8,128)(2,1)}, u32[]{:S(2)}, u32[]{:S(2)}) collective-permute-start(bf16[256,2048]{1,0:T(8,128)(2,1)} %get-tuple-element.22), channel_id=1, source_target_pairs={{4,8},{8,4},{12,16},{16,12},{20,24},{24,20},{28,32},{32,28},{36,40... | collective-permute-start | bytes 3145736 | tf_op jit(solution)/shard_map/ppermute | solution.py:341
  17.4 1.6 %copy-start.2 = (bf16[512,2048]{1,0:T(8,128)(2,1)S(1)}, bf16[512,2048]{1,0:T(8,128)(2,1)}, u32[]{:S(2)}) copy-start(bf16[512,2048]{1,0:T(8,128)(2,1)} %copy-done.1) | copy-start | bytes 6291460
  21.9 8.2 %copy-start.3 = (bf16[512,2048]{1,0:T(8,128)(2,1)S(1)}, bf16[512,2048]{1,0:T(8,128)(2,1)}, u32[]{:S(2)}) copy-start(bf16[512,2048]{1,0:T(8,128)(2,1)} %copy-done.1) | copy-start | bytes 6291460
  25.0 15.7 %collective-permute-start.6 = (bf16[64,2048]{1,0:T(8,128)(2,1)S(1)}, bf16[64,2048]{1,0:T(8,128)(2,1)S(1)}, u32[]{:S(2)}, u32[]{:S(2)}) collective-permute-start(bf16[64,2048]{1,0:T(8,128)(2,1)S(1)} %get-tuple-element.30), channel_id=1, source_target_pairs={{0,1},{1,2},{2,3},{3,0},{4,5},{5,6},{6,7},{7,4},{8,9},{9,10},{10,1... | collective-permute-start | bytes 786440 | tf_op jit(solution)/shard_map/ppermute | solution.py:343
  26.0 16.2 %collective-permute-start.7 = (bf16[64,2048]{1,0:T(8,128)(2,1)S(1)}, bf16[64,2048]{1,0:T(8,128)(2,1)S(1)}, u32[]{:S(2)}, u32[]{:S(2)}) collective-permute-start(bf16[64,2048]{1,0:T(8,128)(2,1)S(1)} %get-tuple-element.31), channel_id=1, source_target_pairs={{0,2},{1,3},{2,0},{3,1},{4,6},{5,7},{6,4},{7,5},{8,10},{9,11},{10,... | collective-permute-start | bytes 786440 | tf_op jit(solution)/shard_map/ppermute | solution.py:343
  28.7 13.5 %collective-permute-start.8 = (bf16[64,2048]{1,0:T(8,128)(2,1)S(1)}, bf16[64,2048]{1,0:T(8,128)(2,1)S(1)}, u32[]{:S(2)}, u32[]{:S(2)}) collective-permute-start(bf16[64,2048]{1,0:T(8,128)(2,1)S(1)} %get-tuple-element.32), channel_id=1, source_target_pairs={{0,3},{1,0},{2,1},{3,2},{4,7},{5,4},{6,5},{7,6},{8,11},{9,8},{10,9... | collective-permute-start | bytes 786440 | tf_op jit(solution)/shard_map/ppermute | solution.py:343
  33.0 9.1 %copy-start.5 = (f32[2048]{0:T(1024)S(1)}, f32[2048]{0:T(1024)}, u32[]{:S(2)}) copy-start(f32[2048]{0:T(1024)} %param.8) | copy-start | bytes 24580
  37.0 14.9 %collective-permute-start.3 = (bf16[64,2048]{1,0:T(8,128)(2,1)S(1)}, bf16[64,2048]{1,0:T(8,128)(2,1)S(1)}, u32[]{:S(2)}, u32[]{:S(2)}) collective-permute-start(bf16[64,2048]{1,0:T(8,128)(2,1)S(1)} %get-tuple-element.26), channel_id=1, source_target_pairs={{0,1},{1,2},{2,3},{3,0},{4,5},{5,6},{6,7},{7,4},{8,9},{9,10},{10,1... | collective-permute-start | bytes 786440 | tf_op jit(solution)/shard_map/ppermute | solution.py:343
  38.0 13.9 %collective-permute-start.4 = (bf16[64,2048]{1,0:T(8,128)(2,1)S(1)}, bf16[64,2048]{1,0:T(8,128)(2,1)S(1)}, u32[]{:S(2)}, u32[]{:S(2)}) collective-permute-start(bf16[64,2048]{1,0:T(8,128)(2,1)S(1)} %get-tuple-element.27), channel_id=1, source_target_pairs={{0,2},{1,3},{2,0},{3,1},{4,6},{5,7},{6,4},{7,5},{8,10},{9,11},{10,... | collective-permute-start | bytes 786440 | tf_op jit(solution)/shard_map/ppermute | solution.py:343
  40.7 11.2 %collective-permute-start.5 = (bf16[64,2048]{1,0:T(8,128)(2,1)S(1)}, bf16[64,2048]{1,0:T(8,128)(2,1)S(1)}, u32[]{:S(2)}, u32[]{:S(2)}) collective-permute-start(bf16[64,2048]{1,0:T(8,128)(2,1)S(1)} %get-tuple-element.28), channel_id=1, source_target_pairs={{0,3},{1,0},{2,1},{3,2},{4,7},{5,4},{6,5},{7,6},{8,11},{9,8},{10,9... | collective-permute-start | bytes 786440 | tf_op jit(solution)/shard_map/ppermute | solution.py:343
  42.9 11.0 %collective-permute-start.9 = (bf16[64,2048]{1,0:T(8,128)(2,1)S(1)}, bf16[64,2048]{1,0:T(8,128)(2,1)S(1)}, u32[]{:S(2)}, u32[]{:S(2)}) collective-permute-start(bf16[64,2048]{1,0:T(8,128)(2,1)S(1)} %combine.2.refs_0_), channel_id=1, source_target_pairs={{4,8},{8,4},{12,16},{16,12},{20,24},{24,20},{28,32},{32,28},{36,40... | collective-permute-start | bytes 786440 | tf_op jit(solution)/shard_map/ppermute | solution.py:341
  54.6 10.6 %collective-permute-start.10 = (bf16[128,2048]{1,0:T(8,128)(2,1)S(1)}, bf16[128,2048]{1,0:T(8,128)(2,1)S(1)}, u32[]{:S(2)}, u32[]{:S(2)}) collective-permute-start(bf16[128,2048]{1,0:T(8,128)(2,1)S(1)} %combine.3.mine), channel_id=1, source_target_pairs={{0,1},{1,2},{2,3},{3,0},{4,5},{5,6},{6,7},{7,4},{8,9},{9,10},{10,1... | collective-permute-start | bytes 1572872 | tf_op jit(solution)/shard_map/ppermute | solution.py:343
  54.7 12.4 %collective-permute-start.11 = (bf16[128,2048]{1,0:T(8,128)(2,1)S(1)}, bf16[128,2048]{1,0:T(8,128)(2,1)S(1)}, u32[]{:S(2)}, u32[]{:S(2)}) collective-permute-start(bf16[128,2048]{1,0:T(8,128)(2,1)S(1)} %combine.3.mine), channel_id=1, source_target_pairs={{0,3},{1,0},{2,1},{3,2},{4,7},{5,4},{6,5},{7,6},{8,11},{9,8},{10,9... | collective-permute-start | bytes 1572872 | tf_op jit(solution)/shard_map/ppermute | solution.py:343
  67.3 27.9 %collective-permute-start.17 = (bf16[320,2048]{1,0:T(8,128)(2,1)S(1)}, bf16[320,2048]{1,0:T(8,128)(2,1)S(1)}, u32[]{:S(2)}, u32[]{:S(2)}) collective-permute-start(bf16[320,2048]{1,0:T(8,128)(2,1)S(1)} %get-tuple-element.37), channel_id=1, source_target_pairs={{4,8},{8,4},{12,16},{16,12},{20,24},{24,20},{28,32},{32,28},{36,40... | collective-permute-start | bytes 3932168 | tf_op jit(solution)/shard_map/ppermute | solution.py:341
  70.3 16.1 %collective-permute-start.15 = (bf16[256,2048]{1,0:T(8,128)(2,1)S(1)}, bf16[256,2048]{1,0:T(8,128)(2,1)S(1)}, u32[]{:S(2)}, u32[]{:S(2)}) collective-permute-start(bf16[256,2048]{1,0:T(8,128)(2,1)S(1)} %get-tuple-element.33.sides), channel_id=1, source_target_pairs={{0,4},{4,0},{8,12},{12,8},{16,20},{20,16},{24,28},{28,24},{32,36},... | collective-permute-start | bytes 3145736 | tf_op jit(solution)/shard_map/ppermute | solution.py:342
  70.4 9.4 %collective-permute-start.12 = (bf16[64,2048]{1,0:T(8,128)(2,1)S(1)}, bf16[64,2048]{1,0:T(8,128)(2,1)S(1)}, u32[]{:S(2)}, u32[]{:S(2)}) collective-permute-start(bf16[64,2048]{1,0:T(8,128)(2,1)S(1)} %get-tuple-element.34), channel_id=1, source_target_pairs={{0,1},{1,2},{2,3},{3,0},{4,5},{5,6},{6,7},{7,4},{8,9},{9,10},{10,1... | collective-permute-start | bytes 786440 | tf_op jit(solution)/shard_map/ppermute | solution.py:343
  70.5 9.3 %collective-permute-start.13 = (bf16[64,2048]{1,0:T(8,128)(2,1)S(1)}, bf16[64,2048]{1,0:T(8,128)(2,1)S(1)}, u32[]{:S(2)}, u32[]{:S(2)}) collective-permute-start(bf16[64,2048]{1,0:T(8,128)(2,1)S(1)} %get-tuple-element.35), channel_id=1, source_target_pairs={{0,3},{1,0},{2,1},{3,2},{4,7},{5,4},{6,5},{7,6},{8,11},{9,8},{10,9... | collective-permute-start | bytes 786440 | tf_op jit(solution)/shard_map/ppermute | solution.py:343
  73.5 12.9 %collective-permute-start.14 = (bf16[128,2048]{1,0:T(8,128)(2,1)S(1)}, bf16[128,2048]{1,0:T(8,128)(2,1)S(1)}, u32[]{:S(2)}, u32[]{:S(2)}) collective-permute-start(bf16[128,2048]{1,0:T(8,128)(2,1)S(1)} %combine.3.mine), channel_id=1, source_target_pairs={{0,4},{4,0},{8,12},{12,8},{16,20},{20,16},{24,28},{28,24},{32,36},... | collective-permute-start | bytes 1572872 | tf_op jit(solution)/shard_map/ppermute | solution.py:342
  79.8 6.6 %collective-permute-start.16 = (bf16[128,2048]{1,0:T(8,128)(2,1)S(1)}, bf16[128,2048]{1,0:T(8,128)(2,1)S(1)}, u32[]{:S(2)}, u32[]{:S(2)}) collective-permute-start(bf16[128,2048]{1,0:T(8,128)(2,1)S(1)} %join.1.op), channel_id=1, source_target_pairs={{0,4},{4,0},{8,12},{12,8},{16,20},{20,16},{24,28},{28,24},{32,36},... | collective-permute-start | bytes 1572872 | tf_op jit(solution)/shard_map/ppermute | solution.py:342
  80.8 14.3 %collective-permute-start.18 = (bf16[128,2048]{1,0:T(8,128)(2,1)S(1)}, bf16[128,2048]{1,0:T(8,128)(2,1)S(1)}, u32[]{:S(2)}, u32[]{:S(2)}) collective-permute-start(bf16[128,2048]{1,0:T(8,128)(2,1)S(1)} %join.1.op), channel_id=1, source_target_pairs={{4,8},{8,4},{12,16},{16,12},{20,24},{24,20},{28,32},{32,28},{36,40... | collective-permute-start | bytes 1572872 | tf_op jit(solution)/shard_map/ppermute | solution.py:341

commit v6 on v5

--- a/solution.py
+++ b/solution.py
@@ -299,20 +299,32 @@
     in_steps(meta[0], add)
 
 
-def far_update_kernel(meta, src, blk, col, x, moved, *rest):
-    *pieces, _, out, w, out_v, sem, found = rest
+def far_first_kernel(meta, src, blk, col, x, moved, first, rest, out, w, found):
+    rows, cut = w.shape[0], first.shape[0]
     scale = STEP / (2.0 * x.shape[0])
-    at = 0
-    for piece in pieces:
-        w[at : at + piece.shape[0], :] = piece[...]
-        at += piece.shape[0]
+    w[:cut, :] = first[...]
+    w[cut:, :] = rest[...]
+    count = list_of(FAR, src, meta[0], found)
+
+    def add(places):
+        for n in places:
+            s = found[n]
+            out[s] = moved[s] - over_rows(w[:, block(blk[s])], x[:rows, block(col[s])]) * scale
+
+    in_steps(count, add)
+
+
+def far_update_kernel(meta, src, blk, col, x, moved, w, _, out, out_v, sem, found):
+    samples = x.shape[0]
+    rows = slice(samples - w.shape[0], samples)
+    scale = STEP / (2.0 * samples)
     count = list_of(FAR, src, meta[0], found)
     save = lambda n: pltpu.make_async_copy(out_v.at[n], out.at[found[n]], sem.at[n])
 
     def finish(places):
         for n in places:
             s = found[n]
-            grad = over_rows(w[:, block(blk[s])], x[:, block(col[s])])
+            grad = over_rows(w[:, block(blk[s])], x[rows, block(col[s])])
             out_v[n] = soft(moved[s] - grad * scale)
         for n in places:
 
@@ -409,14 +421,15 @@
         [pltpu.VMEM((count_ns, width), BF16)] * 2 + [pltpu.VMEM(theta_tiles.shape, BF16), DMA((slots,))], vmem=14,
     )(*index, x_rows, x_turned, *w_own, *[swap_near(w) for w in w_own], theta_tiles, diag)
 
-    far_pieces = [far_first, far_rest, far_op]
+    moved = call(
+        far_first_kernel, "far_first", like(theta_tiles.shape, F32), [SMEM] * 4 + [VMEM] * 4, VMEM, 0, 0,
+        [pltpu.VMEM((3 * quarter, width), BF16), pltpu.SMEM((slots,), jnp.int32)],
+    )(*index, x_rows, moved, far_first, far_rest)
     new_tiles = call(
         far_update_kernel, "far_update", like(theta_tiles.shape, BF16),
-        [SMEM] * 4 + [VMEM] * (2 + len(far_pieces)) + [HBM], HBM, slots * dot // 4, 2 << 20,
-        [pltpu.VMEM((count_ns, width), BF16), pltpu.VMEM(theta_tiles.shape, BF16), DMA((slots,)),
-         pltpu.SMEM((slots,), jnp.int32)],
-        {6 + len(far_pieces): 0},
-    )(*index, x_rows, moved, *far_pieces, new_tiles)
+        [SMEM] * 4 + [VMEM] * 3 + [HBM], HBM, 0, 0,
+        [pltpu.VMEM(theta_tiles.shape, BF16), DMA((slots,)), pltpu.SMEM((slots,), jnp.int32)], {7: 0},
+    )(*index, x_rows, moved, far_op, new_tiles)
     return new_tiles, new_diag.reshape(width)
 
 

time: 98.6 us -> 97.4 us (0.988)
  Pallas kernels: 27.2 us -> 23.1 us
  waiting for transfers between devices: 23.7 us -> 25.7 us
    ppermute x5, waiting for transfers between devices: 8.3 us -> 10.5 us  [shards(): swap_far = lambda v: lax.ppermute(v, 'blk', far)]
    pallas_call x1, Pallas kernels: 5.34 us -> 3.47 us  [shards(): call(own_update_kernel, 'own_update', [like(theta_tiles.shape, BF16), lik...]
    pallas_call x2, Pallas kernels: 5.78 us -> 4.24 us  [shards(): call(functools.partial(own_image_kernel, first), 'own_image', like((rows,...]
    pallas_call x0 -> x1, Pallas kernels: none -> 1.33 us  [shards(): call(far_first_kernel, 'far_first', like(theta_tiles.shape, F32), [SMEM]...]
    pallas_call x1, Pallas kernels: 3.07 us -> 1.88 us  [shards(): call(far_update_kernel, 'far_update', like(theta_tiles.shape, BF16), [SME...]
  transfers between devices with their start and end apart: 19 -> 19, of which waited for: 7 -> 7; matrix products, arithmetic and copies ran while one was open for 0% -> 0% of each run, Pallas kernels for 24% -> 21%
where the time goes in v6:
time: 97.4 us; the launch traced here: 96.7 us
  starting transfers between devices  41.6 us (43%)
  waiting for transfers between devices  25.7 us (26%)
  Pallas kernels  23.1 us (24%)
  local copies, waits for them, and re-layouts  4.51 us (5%)
  between operations  1.74 us (2%)
    ppermute x5, starting transfers between devices, shards(): swap_far = lambda v: lax.ppermute(v, 'blk', far)  23 us
    ppermute x10, starting transfers between devices, shards(): lax.ppermute(v, 'rep', [(i, (i + n) % reps) for i in range(reps)])  16.1 us
    ppermute x10, waiting for transfers between devices, shards(): lax.ppermute(v, 'rep', [(i, (i + n) % reps) for i in range(reps)])  15.2 us
    ppermute x5, waiting for transfers between devices, shards(): swap_far = lambda v: lax.ppermute(v, 'blk', far)  10.5 us
    unnamed x16, local copies, waits for them, and re-layouts  4.51 us
    pallas_call x2, Pallas kernels, shards(): call(functools.partial(own_image_kernel, first), 'own_image', like((rows,...  4.24 us
    pallas_call x1, Pallas kernels, shards(): call(reorder_kernel, 'reorder', [like((count_ns, width), BF16), like((3,...  3.95 us
    pallas_call x1, Pallas kernels, shards(): call(own_update_kernel, 'own_update', [like(theta_tiles.shape, BF16), lik...  3.47 us
  transfers between devices with their start and end apart: 19, of which 7 were waited for; matrix products, arithmetic and copies ran while one was open for 0% of the time, Pallas kernels for 21%

profile of v6, /device:TPU:103, one launch (start us, length us, event | category | flops | bytes accessed | tf_op | source)
XLA Modules:
  0.0 96.7 jit_solution(15974408836100661712)
XLA Ops:
  0.6 0.8 collective-permute-start
  1.4 2.0 %load.3 = bf16[256,2048]{1,0:T(8,128)(2,1)} custom-call(bf16[512,2048]{1,0:T(8,128)(2,1)} %src.3), custom_call_target="tpu_custom_call" | custom-call | bytes 1048576 | tf_op jit(solution)/shard_map/load/pallas_call | solution.py:124
  3.4 0.0 copy-start
  3.5 4.7 %collective-permute-start.1 = (bf16[256,2048]{1,0:T(8,128)(2,1)}, bf16[256,2048]{1,0:T(8,128)(2,1)S(1)}, u32[]{:S(2)}, u32[]{:S(2)}) collective-permute-start(bf16[256,2048]{1,0:T(8,128)(2,1)} %load.3), channel_id=1, source_target_pairs={{4,8},{8,4},{12,16},{16,12},{20,24},{24,20},{28,32},{32,28},{36,40... | collective-permute-start | bytes 3145736 | tf_op jit(solution)/shard_map/ppermute | solution.py:353
  8.2 0.0 copy-start.4
  8.2 1.6 %copy-done.4 = bf16[512,2048]{1,0:T(8,128)(2,1)S(1)} copy-done((bf16[512,2048]{1,0:T(8,128)(2,1)S(1)}, bf16[512,2048]{1,0:T(8,128)(2,1)}, u32[]{:S(2)}) %copy-start.4) | copy-done | bytes 2097176
  9.8 1.2 %load.2 = (bf16[512,2048]{1,0:T(8,128)(2,1)S(1)}, bf16[256,2048]{1,0:T(8,128)(2,1)}) custom-call(bf16[512,2048]{1,0:T(8,128)(2,1)S(1)} %copy-done.4), custom_call_target="tpu_custom_call" | custom-call | flops 2147483648 | bytes 1048576 | tf_op jit(solution)/shard_map/load/pallas_call | solution.py:131
  11.0 0.0 copy-start.1
  11.0 1.3 %copy-done.1 = bf16[512,2048]{1,0:T(8,128)(2,1)} copy-done((bf16[512,2048]{1,0:T(8,128)(2,1)}, bf16[512,2048]{1,0:T(8,128)(2,1)S(1)}, u32[]{:S(2)}) %copy-start.1) | copy-done | bytes 2097176
  12.3 4.3 %collective-permute-start.2 = (bf16[256,2048]{1,0:T(8,128)(2,1)}, bf16[256,2048]{1,0:T(8,128)(2,1)}, u32[]{:S(2)}, u32[]{:S(2)}) collective-permute-start(bf16[256,2048]{1,0:T(8,128)(2,1)} %get-tuple-element.22), channel_id=1, source_target_pairs={{4,8},{8,4},{12,16},{16,12},{20,24},{24,20},{28,32},{32,28},{36,40... | collective-permute-start | bytes 3145736 | tf_op jit(solution)/shard_map/ppermute | solution.py:353
  17.3 0.1 pad_add_fusion.meta
  17.3 0.0 copy-done.7
  17.4 0.0 collective-permute-done.x_near
  17.4 0.0 copy-done
  17.4 0.0 copy-start.2
  17.4 1.6 %copy-done.2 = bf16[512,2048]{1,0:T(8,128)(2,1)S(1)} copy-done((bf16[512,2048]{1,0:T(8,128)(2,1)S(1)}, bf16[512,2048]{1,0:T(8,128)(2,1)}, u32[]{:S(2)}) %copy-start.2) | copy-done | bytes 2097176
  19.0 2.1 %own_image.3.acc = f32[256,2048]{1,0:T(8,128)S(1)} custom-call(s32[2]{0:T(128)S(1)} %pad_add_fusion.meta, s32[16]{0:T(128)S(1)} %get-tuple-element.41.src, s32[16]{0:T(128)S(1)} %get-tuple-element.40.blk, s32[16]{0:T(128)S(1)} %copy-done.6, bf16[512,2048]{1,0:T(8,128)(2,1)S(1)} %copy-done.2, bf16[512,2048]{1,0:T(8,128)(2,1)} %collective-permute-done.x_near, ...), custom_call_target="tpu_custom_call" | custom-call | flops 1073741824 | bytes 4194304 | tf_op jit(solution)/shard_map/own_image/pallas_call | solution.py:372
  21.1 0.0 copy-start.3
  21.1 2.1 %collective-permute-done.1.refs_0_.x_far = bf16[256,2048]{1,0:T(8,128)(2,1)S(1)} collective-permute-done((bf16[256,2048]{1,0:T(8,128)(2,1)}, bf16[256,2048]{1,0:T(8,128)(2,1)S(1)}, u32[]{:S(2)}, u32[]{:S(2)}) %collective-permute-start.1) | collective-permute-done | bytes 1048608 | tf_op jit(solution)/shard_map/ppermute | solution.py:353
  23.2 1.3 %far_image.3 = (f32[64,2048]{1,0:T(8,128)S(1)}, bf16[64,2048]{1,0:T(8,128)(2,1)S(1)}, bf16[64,2048]{1,0:T(8,128)(2,1)S(1)}, bf16[64,2048]{1,0:T(8,128)(2,1)S(1)}) custom-call(s32[2]{0:T(128)S(1)} %pad_add_fusion.meta, s32[16]{0:T(128)S(1)} %get-tuple-element.41.src, s32[16]{0:T(128)S(1)} %get-tuple-element.40.blk, s32[16]{0:T(128)S(1)} %copy-done.6, ...), custom_call_target="tpu_custom_call" | custom-call | flops 268435456 | bytes 1048576 | tf_op jit(solution)/shard_map/far_image/pallas_call | solution.py:386
  24.5 1.5 %collective-permute-start.6 = (bf16[64,2048]{1,0:T(8,128)(2,1)S(1)}, bf16[64,2048]{1,0:T(8,128)(2,1)S(1)}, u32[]{:S(2)}, u32[]{:S(2)}) collective-permute-start(bf16[64,2048]{1,0:T(8,128)(2,1)S(1)} %get-tuple-element.30), channel_id=1, source_target_pairs={{0,1},{1,2},{2,3},{3,0},{4,5},{5,6},{6,7},{7,4},{8,9},{9,10},{10,1... | collective-permute-start | bytes 786440 | tf_op jit(solution)/shard_map/ppermute | solution.py:355
  26.0 2.5 %collective-permute-start.7 = (bf16[64,2048]{1,0:T(8,128)(2,1)S(1)}, bf16[64,2048]{1,0:T(8,128)(2,1)S(1)}, u32[]{:S(2)}, u32[]{:S(2)}) collective-permute-start(bf16[64,2048]{1,0:T(8,128)(2,1)S(1)} %get-tuple-element.31), channel_id=1, source_target_pairs={{0,2},{1,3},{2,0},{3,1},{4,6},{5,7},{6,4},{7,5},{8,10},{9,11},{10,... | collective-permute-start | bytes 786440 | tf_op jit(solution)/shard_map/ppermute | solution.py:355
  28.5 1.1 %collective-permute-start.8 = (bf16[64,2048]{1,0:T(8,128)(2,1)S(1)}, bf16[64,2048]{1,0:T(8,128)(2,1)S(1)}, u32[]{:S(2)}, u32[]{:S(2)}) collective-permute-start(bf16[64,2048]{1,0:T(8,128)(2,1)S(1)} %get-tuple-element.32), channel_id=1, source_target_pairs={{0,3},{1,0},{2,1},{3,2},{4,7},{5,4},{6,5},{7,6},{8,11},{9,8},{10,9... | collective-permute-start | bytes 786440 | tf_op jit(solution)/shard_map/ppermute | solution.py:355
  29.7 0.0 copy-done.3
  29.7 2.1 %own_image.2.acc = f32[256,2048]{1,0:T(8,128)S(1)} custom-call(s32[2]{0:T(128)S(1)} %pad_add_fusion.meta, s32[16]{0:T(128)S(1)} %get-tuple-element.41.src, s32[16]{0:T(128)S(1)} %get-tuple-element.40.blk, s32[16]{0:T(128)S(1)} %copy-done.6, bf16[512,2048]{1,0:T(8,128)(2,1)S(1)} %copy-done.3, bf16[512,2048]{1,0:T(8,128)(2,1)} %collective-permute-done.x_near, ...), custom_call_target="tpu_custom_call" | custom-call | flops 1073741824 | bytes 4194304 | tf_op jit(solution)/shard_map/own_image/pallas_call | solution.py:372
  31.8 0.0 copy-start.5
  31.8 2.8 %collective-permute-done.2.refs_1_.x_far = bf16[256,2048]{1,0:T(8,128)(2,1)} collective-permute-done((bf16[256,2048]{1,0:T(8,128)(2,1)}, bf16[256,2048]{1,0:T(8,128)(2,1)}, u32[]{:S(2)}, u32[]{:S(2)}) %collective-permute-start.2) | collective-permute-done | bytes 1048608 | tf_op jit(solution)/shard_map/ppermute | solution.py:353
  34.6 2.0 %far_image.2 = (f32[64,2048]{1,0:T(8,128)S(1)}, bf16[64,2048]{1,0:T(8,128)(2,1)S(1)}, bf16[64,2048]{1,0:T(8,128)(2,1)S(1)}, bf16[64,2048]{1,0:T(8,128)(2,1)S(1)}) custom-call(s32[2]{0:T(128)S(1)} %pad_add_fusion.meta, s32[16]{0:T(128)S(1)} %get-tuple-element.41.src, s32[16]{0:T(128)S(1)} %get-tuple-element.40.blk, s32[16]{0:T(128)S(1)} %copy-done.6, ...), custom_call_target="tpu_custom_call" | custom-call | flops 268435456 | bytes 1048576 | tf_op jit(solution)/shard_map/far_image/pallas_call | solution.py:386
  36.6 1.5 %collective-permute-start.3 = (bf16[64,2048]{1,0:T(8,128)(2,1)S(1)}, bf16[64,2048]{1,0:T(8,128)(2,1)S(1)}, u32[]{:S(2)}, u32[]{:S(2)}) collective-permute-start(bf16[64,2048]{1,0:T(8,128)(2,1)S(1)} %get-tuple-element.26), channel_id=1, source_target_pairs={{0,1},{1,2},{2,3},{3,0},{4,5},{5,6},{6,7},{7,4},{8,9},{9,10},{10,1... | collective-permute-start | bytes 786440 | tf_op jit(solution)/shard_map/ppermute | solution.py:355
  38.1 2.5 %collective-permute-start.4 = (bf16[64,2048]{1,0:T(8,128)(2,1)S(1)}, bf16[64,2048]{1,0:T(8,128)(2,1)S(1)}, u32[]{:S(2)}, u32[]{:S(2)}) collective-permute-start(bf16[64,2048]{1,0:T(8,128)(2,1)S(1)} %get-tuple-element.27), channel_id=1, source_target_pairs={{0,2},{1,3},{2,0},{3,1},{4,6},{5,7},{6,4},{7,5},{8,10},{9,11},{10,... | collective-permute-start | bytes 786440 | tf_op jit(solution)/shard_map/ppermute | solution.py:355
  40.6 0.0 collective-permute-done.6.got_1
  40.6 1.1 %collective-permute-start.5 = (bf16[64,2048]{1,0:T(8,128)(2,1)S(1)}, bf16[64,2048]{1,0:T(8,128)(2,1)S(1)}, u32[]{:S(2)}, u32[]{:S(2)}) collective-permute-start(bf16[64,2048]{1,0:T(8,128)(2,1)S(1)} %get-tuple-element.28), channel_id=1, source_target_pairs={{0,3},{1,0},{2,1},{3,2},{4,7},{5,4},{6,5},{7,6},{8,11},{9,8},{10,9... | collective-permute-start | bytes 786440 | tf_op jit(solution)/shard_map/ppermute | solution.py:355
  41.7 0.0 collective-permute-done.7.got_2
  41.7 0.0 collective-permute-done.8.got_3
  41.7 0.7 combine.2.refs_0_
  42.4 5.5 %collective-permute-start.9 = (bf16[64,2048]{1,0:T(8,128)(2,1)S(1)}, bf16[64,2048]{1,0:T(8,128)(2,1)S(1)}, u32[]{:S(2)}, u32[]{:S(2)}) collective-permute-start(bf16[64,2048]{1,0:T(8,128)(2,1)S(1)} %combine.2.refs_0_), channel_id=1, source_target_pairs={{4,8},{8,4},{12,16},{16,12},{20,24},{24,20},{28,32},{32,28},{36,40... | collective-permute-start | bytes 786440 | tf_op jit(solution)/shard_map/ppermute | solution.py:353
  47.9 4.0 %reorder.1 = (bf16[512,2048]{1,0:T(8,128)(2,1)S(1)}, bf16[3,2048,512]{2,1,0:T(8,128)(2,1)S(1)}) custom-call(s32[2]{0:T(128)S(1)} %pad_add_fusion.meta, bf16[512,2048]{1,0:T(8,128)(2,1)S(1)} %copy-done.3, bf16[512,2048]{1,0:T(8,128)(2,1)} %collective-permute-done.x_near, bf16[256,2048]{1,0:T(8,128)(2,1)S(1)} %collective-permute-done.1.refs_0_.x_far, ...), custom_call_target="tpu_custom_call" | custom-call | tf_op jit(solution)/shard_map/reorder/pallas_call | solution.py:378
  51.9 0.0 collective-permute-done.3.got_1
  51.9 0.0 collective-permute-done.4.got_2
  51.9 0.0 collective-permute-done.5.got_3
  51.9 1.5 %collective-permute-done.9.refs_1_.first = bf16[64,2048]{1,0:T(8,128)(2,1)S(1)} collective-permute-done((bf16[64,2048]{1,0:T(8,128)(2,1)S(1)}, bf16[64,2048]{1,0:T(8,128)(2,1)S(1)}, u32[]{:S(2)}, u32[]{:S(2)}) %collective-permute-start.9) | collective-permute-done | bytes 262176 | tf_op jit(solution)/shard_map/ppermute | solution.py:353
  53.4 0.7 combine.3.mine
  54.2 0.4 collective-permute-start.10
  54.6 2.3 %collective-permute-start.11 = (bf16[128,2048]{1,0:T(8,128)(2,1)S(1)}, bf16[128,2048]{1,0:T(8,128)(2,1)S(1)}, u32[]{:S(2)}, u32[]{:S(2)}) collective-permute-start(bf16[128,2048]{1,0:T(8,128)(2,1)S(1)} %combine.3.mine), channel_id=1, source_target_pairs={{0,3},{1,0},{2,1},{3,2},{4,7},{5,4},{6,5},{7,6},{8,11},{9,8},{10,9... | collective-permute-start | bytes 1572872 | tf_op jit(solution)/shard_map/ppermute | solution.py:355
  56.9 8.1 %collective-permute-done.10.below = bf16[128,2048]{1,0:T(8,128)(2,1)S(1)} collective-permute-done((bf16[128,2048]{1,0:T(8,128)(2,1)S(1)}, bf16[128,2048]{1,0:T(8,128)(2,1)S(1)}, u32[]{:S(2)}, u32[]{:S(2)}) %collective-permute-start.10) | collective-permute-done | bytes 524320 | tf_op jit(solution)/shard_map/ppermute | solution.py:355
  65.0 1.5 %collective-permute-done.11.above = bf16[128,2048]{1,0:T(8,128)(2,1)S(1)} collective-permute-done((bf16[128,2048]{1,0:T(8,128)(2,1)S(1)}, bf16[128,2048]{1,0:T(8,128)(2,1)S(1)}, u32[]{:S(2)}, u32[]{:S(2)}) %collective-permute-start.11) | collective-permute-done | bytes 524320 | tf_op jit(solution)/shard_map/ppermute | solution.py:355
  66.5 0.2 stack.9
  66.7 3.6 %collective-permute-start.17 = (bf16[320,2048]{1,0:T(8,128)(2,1)S(1)}, bf16[320,2048]{1,0:T(8,128)(2,1)S(1)}, u32[]{:S(2)}, u32[]{:S(2)}) collective-permute-start(bf16[320,2048]{1,0:T(8,128)(2,1)S(1)} %get-tuple-element.37), channel_id=1, source_target_pairs={{4,8},{8,4},{12,16},{16,12},{20,24},{24,20},{28,32},{32,28},{36,40... | collective-permute-start | bytes 3932168 | tf_op jit(solution)/shard_map/ppermute | solution.py:353
  70.3 0.1 collective-permute-start.15
  70.4 0.1 collective-permute-start.12
  70.5 3.0 %collective-permute-start.13 = (bf16[64,2048]{1,0:T(8,128)(2,1)S(1)}, bf16[64,2048]{1,0:T(8,128)(2,1)S(1)}, u32[]{:S(2)}, u32[]{:S(2)}) collective-permute-start(bf16[64,2048]{1,0:T(8,128)(2,1)S(1)} %get-tuple-element.35), channel_id=1, source_target_pairs={{0,3},{1,0},{2,1},{3,2},{4,7},{5,4},{6,5},{7,6},{8,11},{9,8},{10,9... | collective-permute-start | bytes 786440 | tf_op jit(solution)/shard_map/ppermute | solution.py:355
  73.5 0.6 collective-permute-start.14
  74.2 5.6 %collective-permute-done.12.op_a = bf16[64,2048]{1,0:T(8,128)(2,1)S(1)} collective-permute-done((bf16[64,2048]{1,0:T(8,128)(2,1)S(1)}, bf16[64,2048]{1,0:T(8,128)(2,1)S(1)}, u32[]{:S(2)}, u32[]{:S(2)}) %collective-permute-start.12) | collective-permute-done | bytes 262176 | tf_op jit(solution)/shard_map/ppermute | solution.py:355
  79.8 0.0 collective-permute-done.13.op_b
  79.8 1.0 %collective-permute-start.16 = (bf16[128,2048]{1,0:T(8,128)(2,1)S(1)}, bf16[128,2048]{1,0:T(8,128)(2,1)S(1)}, u32[]{:S(2)}, u32[]{:S(2)}) collective-permute-start(bf16[128,2048]{1,0:T(8,128)(2,1)S(1)} %join.1.op), channel_id=1, source_target_pairs={{0,4},{4,0},{8,12},{12,8},{16,20},{20,16},{24,28},{28,24},{32,36},... | collective-permute-start | bytes 1572872 | tf_op jit(solution)/shard_map/ppermute | solution.py:354
  80.8 4.9 %collective-permute-start.18 = (bf16[128,2048]{1,0:T(8,128)(2,1)S(1)}, bf16[128,2048]{1,0:T(8,128)(2,1)S(1)}, u32[]{:S(2)}, u32[]{:S(2)}) collective-permute-start(bf16[128,2048]{1,0:T(8,128)(2,1)S(1)} %join.1.op), channel_id=1, source_target_pairs={{4,8},{8,4},{12,16},{16,12},{20,24},{24,20},{28,32},{32,28},{36,40... | collective-permute-start | bytes 1572872 | tf_op jit(solution)/shard_map/ppermute | solution.py:353
  85.8 0.0 collective-permute-done.14.near_mine
  85.8 0.0 collective-permute-done.16.near_op
  85.8 0.0 collective-permute-done.15.near_sides
  85.8 3.5 %own_update.1 = (bf16[16,256,256]{2,1,0:T(8,128)(2,1)}, f32[16,256,256]{2,1,0:T(8,128)S(1)}, f32[1,2048]{1,0:T(1,128)}) custom-call(s32[2]{0:T(128)S(1)} %pad_add_fusion.meta, s32[16]{0:T(128)S(1)} %get-tuple-element.41.src, s32[16]{0:T(128)S(1)} %get-tuple-element.40.blk, s32[16]{0:T(128)S(1)} %copy-done.6, ...), custom_call_target="tpu_custom_call" | custom-call | tf_op jit(solution)/shard_map/own_update/pallas_call | solution.py:417
  89.3 0.0 collective-permute-done.17.rest
  89.3 1.3 %far_first.1.moved = f32[16,256,256]{2,1,0:T(8,128)S(1)} custom-call(s32[2]{0:T(128)S(1)} %pad_add_fusion.meta, s32[16]{0:T(128)S(1)} %get-tuple-element.41.src, s32[16]{0:T(128)S(1)} %get-tuple-element.40.blk, s32[16]{0:T(128)S(1)} %copy-done.6, bf16[512,2048]{1,0:T(8,128)(2,1)S(1)} %get-tuple-element.23.refs_2_.x, ...), custom_call_target="tpu_custom_call" | custom-call | tf_op jit(solution)/shard_map/far_first/pallas_call | solution.py:424
  90.6 4.0 %collective-permute-done.18.w = bf16[128,2048]{1,0:T(8,128)(2,1)S(1)} collective-permute-done((bf16[128,2048]{1,0:T(8,128)(2,1)S(1)}, bf16[128,2048]{1,0:T(8,128)(2,1)S(1)}, u32[]{:S(2)}, u32[]{:S(2)}) %collective-permute-start.18) | collective-permute-done | bytes 524320 | tf_op jit(solution)/shard_map/ppermute | solution.py:353
  94.7 1.9 %far_update.1 = bf16[16,256,256]{2,1,0:T(8,128)(2,1)} custom-call(s32[2]{0:T(128)S(1)} %pad_add_fusion.meta, s32[16]{0:T(128)S(1)} %get-tuple-element.41.src, s32[16]{0:T(128)S(1)} %get-tuple-element.40.blk, s32[16]{0:T(128)S(1)} %copy-done.6, bf16[512,2048]{1,0:T(8,128)(2,1)S(1)} %get-tuple-element.23.refs_2_.x, ...), custom_call_target="tpu_custom_call", output_to_operand_aliasing={{}: (7, {})} | custom-call | tf_op jit(solution)/shard_map/far_update/pallas_call | solution.py:428
  (6 shorter events, 0.1 us)
Async XLA Ops:
  0.6 16.7 %collective-permute-start = (bf16[512,2048]{1,0:T(8,128)(2,1)}, bf16[512,2048]{1,0:T(8,128)(2,1)}, u32[]{:S(2)}, u32[]{:S(2)}) collective-permute-start(bf16[512,2048]{1,0:T(8,128)(2,1)} %src.3), channel_id=1, source_target_pairs={{0,4},{4,0},{8,12},{12,8},{16,20},{20,16},{24,28},{28,24},{32,36},... | collective-permute-start | bytes 6291464 | tf_op jit(solution)/shard_map/ppermute | solution.py:354
  3.4 13.9 %copy-start = (bf16[16,256,256]{2,1,0:T(8,128)(2,1)S(1)}, bf16[16,256,256]{2,1,0:T(8,128)(2,1)}, u32[]{:S(2)}) copy-start(bf16[16,256,256]{2,1,0:T(8,128)(2,1)} %tiles.9) | copy-start | bytes 6291460
  3.5 19.8 %collective-permute-start.1 = (bf16[256,2048]{1,0:T(8,128)(2,1)}, bf16[256,2048]{1,0:T(8,128)(2,1)S(1)}, u32[]{:S(2)}, u32[]{:S(2)}) collective-permute-start(bf16[256,2048]{1,0:T(8,128)(2,1)} %load.3), channel_id=1, source_target_pairs={{4,8},{8,4},{12,16},{16,12},{20,24},{24,20},{28,32},{32,28},{36,40... | collective-permute-start | bytes 3145736 | tf_op jit(solution)/shard_map/ppermute | solution.py:353
  8.2 1.6 %copy-start.4 = (bf16[512,2048]{1,0:T(8,128)(2,1)S(1)}, bf16[512,2048]{1,0:T(8,128)(2,1)}, u32[]{:S(2)}) copy-start(bf16[512,2048]{1,0:T(8,128)(2,1)} %src.3) | copy-start | bytes 6291460
  9.8 7.6 %copy-start.7 = (s32[16]{0:T(128)S(1)}, s32[16]{0:T(128)}, u32[]{:S(2)}) copy-start(s32[16]{0:T(128)} %param.9) | copy-start | bytes 196
  9.8 7.6 %copy-start.6 = (s32[16]{0:T(128)S(1)}, s32[16]{0:T(128)}, u32[]{:S(2)}) copy-start(s32[16]{0:T(128)} %col.13) | copy-start | bytes 196
  11.0 1.3 %copy-start.1 = (bf16[512,2048]{1,0:T(8,128)(2,1)}, bf16[512,2048]{1,0:T(8,128)(2,1)S(1)}, u32[]{:S(2)}) copy-start(bf16[512,2048]{1,0:T(8,128)(2,1)S(1)} %get-tuple-element.21.x_own.samples) | copy-start | bytes 6291460
  12.3 22.3 %collective-permute-start.2 = (bf16[256,2048]{1,0:T(8,128)(2,1)}, bf16[256,2048]{1,0:T(8,128)(2,1)}, u32[]{:S(2)}, u32[]{:S(2)}) collective-permute-start(bf16[256,2048]{1,0:T(8,128)(2,1)} %get-tuple-element.22), channel_id=1, source_target_pairs={{4,8},{8,4},{12,16},{16,12},{20,24},{24,20},{28,32},{32,28},{36,40... | collective-permute-start | bytes 3145736 | tf_op jit(solution)/shard_map/ppermute | solution.py:353
  17.4 1.6 %copy-start.2 = (bf16[512,2048]{1,0:T(8,128)(2,1)S(1)}, bf16[512,2048]{1,0:T(8,128)(2,1)}, u32[]{:S(2)}) copy-start(bf16[512,2048]{1,0:T(8,128)(2,1)} %copy-done.1) | copy-start | bytes 6291460
  21.1 8.6 %copy-start.3 = (bf16[512,2048]{1,0:T(8,128)(2,1)S(1)}, bf16[512,2048]{1,0:T(8,128)(2,1)}, u32[]{:S(2)}) copy-start(bf16[512,2048]{1,0:T(8,128)(2,1)} %copy-done.1) | copy-start | bytes 6291460
  24.5 16.0 %collective-permute-start.6 = (bf16[64,2048]{1,0:T(8,128)(2,1)S(1)}, bf16[64,2048]{1,0:T(8,128)(2,1)S(1)}, u32[]{:S(2)}, u32[]{:S(2)}) collective-permute-start(bf16[64,2048]{1,0:T(8,128)(2,1)S(1)} %get-tuple-element.30), channel_id=1, source_target_pairs={{0,1},{1,2},{2,3},{3,0},{4,5},{5,6},{6,7},{7,4},{8,9},{9,10},{10,1... | collective-permute-start | bytes 786440 | tf_op jit(solution)/shard_map/ppermute | solution.py:355
  26.0 15.6 %collective-permute-start.7 = (bf16[64,2048]{1,0:T(8,128)(2,1)S(1)}, bf16[64,2048]{1,0:T(8,128)(2,1)S(1)}, u32[]{:S(2)}, u32[]{:S(2)}) collective-permute-start(bf16[64,2048]{1,0:T(8,128)(2,1)S(1)} %get-tuple-element.31), channel_id=1, source_target_pairs={{0,2},{1,3},{2,0},{3,1},{4,6},{5,7},{6,4},{7,5},{8,10},{9,11},{10,... | collective-permute-start | bytes 786440 | tf_op jit(solution)/shard_map/ppermute | solution.py:355
  28.5 13.1 %collective-permute-start.8 = (bf16[64,2048]{1,0:T(8,128)(2,1)S(1)}, bf16[64,2048]{1,0:T(8,128)(2,1)S(1)}, u32[]{:S(2)}, u32[]{:S(2)}) collective-permute-start(bf16[64,2048]{1,0:T(8,128)(2,1)S(1)} %get-tuple-element.32), channel_id=1, source_target_pairs={{0,3},{1,0},{2,1},{3,2},{4,7},{5,4},{6,5},{7,6},{8,11},{9,8},{10,9... | collective-permute-start | bytes 786440 | tf_op jit(solution)/shard_map/ppermute | solution.py:355
  31.8 9.9 %copy-start.5 = (f32[2048]{0:T(1024)S(1)}, f32[2048]{0:T(1024)}, u32[]{:S(2)}) copy-start(f32[2048]{0:T(1024)} %param.8) | copy-start | bytes 24580
  36.6 15.3 %collective-permute-start.3 = (bf16[64,2048]{1,0:T(8,128)(2,1)S(1)}, bf16[64,2048]{1,0:T(8,128)(2,1)S(1)}, u32[]{:S(2)}, u32[]{:S(2)}) collective-permute-start(bf16[64,2048]{1,0:T(8,128)(2,1)S(1)} %get-tuple-element.26), channel_id=1, source_target_pairs={{0,1},{1,2},{2,3},{3,0},{4,5},{5,6},{6,7},{7,4},{8,9},{9,10},{10,1... | collective-permute-start | bytes 786440 | tf_op jit(solution)/shard_map/ppermute | solution.py:355
  38.1 13.8 %collective-permute-start.4 = (bf16[64,2048]{1,0:T(8,128)(2,1)S(1)}, bf16[64,2048]{1,0:T(8,128)(2,1)S(1)}, u32[]{:S(2)}, u32[]{:S(2)}) collective-permute-start(bf16[64,2048]{1,0:T(8,128)(2,1)S(1)} %get-tuple-element.27), channel_id=1, source_target_pairs={{0,2},{1,3},{2,0},{3,1},{4,6},{5,7},{6,4},{7,5},{8,10},{9,11},{10,... | collective-permute-start | bytes 786440 | tf_op jit(solution)/shard_map/ppermute | solution.py:355
  40.6 11.3 %collective-permute-start.5 = (bf16[64,2048]{1,0:T(8,128)(2,1)S(1)}, bf16[64,2048]{1,0:T(8,128)(2,1)S(1)}, u32[]{:S(2)}, u32[]{:S(2)}) collective-permute-start(bf16[64,2048]{1,0:T(8,128)(2,1)S(1)} %get-tuple-element.28), channel_id=1, source_target_pairs={{0,3},{1,0},{2,1},{3,2},{4,7},{5,4},{6,5},{7,6},{8,11},{9,8},{10,9... | collective-permute-start | bytes 786440 | tf_op jit(solution)/shard_map/ppermute | solution.py:355
  42.4 11.0 %collective-permute-start.9 = (bf16[64,2048]{1,0:T(8,128)(2,1)S(1)}, bf16[64,2048]{1,0:T(8,128)(2,1)S(1)}, u32[]{:S(2)}, u32[]{:S(2)}) collective-permute-start(bf16[64,2048]{1,0:T(8,128)(2,1)S(1)} %combine.2.refs_0_), channel_id=1, source_target_pairs={{4,8},{8,4},{12,16},{16,12},{20,24},{24,20},{28,32},{32,28},{36,40... | collective-permute-start | bytes 786440 | tf_op jit(solution)/shard_map/ppermute | solution.py:353
  54.2 10.8 %collective-permute-start.10 = (bf16[128,2048]{1,0:T(8,128)(2,1)S(1)}, bf16[128,2048]{1,0:T(8,128)(2,1)S(1)}, u32[]{:S(2)}, u32[]{:S(2)}) collective-permute-start(bf16[128,2048]{1,0:T(8,128)(2,1)S(1)} %combine.3.mine), channel_id=1, source_target_pairs={{0,1},{1,2},{2,3},{3,0},{4,5},{5,6},{6,7},{7,4},{8,9},{9,10},{10,1... | collective-permute-start | bytes 1572872 | tf_op jit(solution)/shard_map/ppermute | solution.py:355
  54.6 11.9 %collective-permute-start.11 = (bf16[128,2048]{1,0:T(8,128)(2,1)S(1)}, bf16[128,2048]{1,0:T(8,128)(2,1)S(1)}, u32[]{:S(2)}, u32[]{:S(2)}) collective-permute-start(bf16[128,2048]{1,0:T(8,128)(2,1)S(1)} %combine.3.mine), channel_id=1, source_target_pairs={{0,3},{1,0},{2,1},{3,2},{4,7},{5,4},{6,5},{7,6},{8,11},{9,8},{10,9... | collective-permute-start | bytes 1572872 | tf_op jit(solution)/shard_map/ppermute | solution.py:355
  66.7 22.6 %collective-permute-start.17 = (bf16[320,2048]{1,0:T(8,128)(2,1)S(1)}, bf16[320,2048]{1,0:T(8,128)(2,1)S(1)}, u32[]{:S(2)}, u32[]{:S(2)}) collective-permute-start(bf16[320,2048]{1,0:T(8,128)(2,1)S(1)} %get-tuple-element.37), channel_id=1, source_target_pairs={{4,8},{8,4},{12,16},{16,12},{20,24},{24,20},{28,32},{32,28},{36,40... | collective-permute-start | bytes 3932168 | tf_op jit(solution)/shard_map/ppermute | solution.py:353
  70.3 15.5 %collective-permute-start.15 = (bf16[256,2048]{1,0:T(8,128)(2,1)S(1)}, bf16[256,2048]{1,0:T(8,128)(2,1)S(1)}, u32[]{:S(2)}, u32[]{:S(2)}) collective-permute-start(bf16[256,2048]{1,0:T(8,128)(2,1)S(1)} %get-tuple-element.33.sides), channel_id=1, source_target_pairs={{0,4},{4,0},{8,12},{12,8},{16,20},{20,16},{24,28},{28,24},{32,36},... | collective-permute-start | bytes 3145736 | tf_op jit(solution)/shard_map/ppermute | solution.py:354
  70.4 9.4 %collective-permute-start.12 = (bf16[64,2048]{1,0:T(8,128)(2,1)S(1)}, bf16[64,2048]{1,0:T(8,128)(2,1)S(1)}, u32[]{:S(2)}, u32[]{:S(2)}) collective-permute-start(bf16[64,2048]{1,0:T(8,128)(2,1)S(1)} %get-tuple-element.34), channel_id=1, source_target_pairs={{0,1},{1,2},{2,3},{3,0},{4,5},{5,6},{6,7},{7,4},{8,9},{9,10},{10,1... | collective-permute-start | bytes 786440 | tf_op jit(solution)/shard_map/ppermute | solution.py:355
  70.5 9.3 %collective-permute-start.13 = (bf16[64,2048]{1,0:T(8,128)(2,1)S(1)}, bf16[64,2048]{1,0:T(8,128)(2,1)S(1)}, u32[]{:S(2)}, u32[]{:S(2)}) collective-permute-start(bf16[64,2048]{1,0:T(8,128)(2,1)S(1)} %get-tuple-element.35), channel_id=1, source_target_pairs={{0,3},{1,0},{2,1},{3,2},{4,7},{5,4},{6,5},{7,6},{8,11},{9,8},{10,9... | collective-permute-start | bytes 786440 | tf_op jit(solution)/shard_map/ppermute | solution.py:355
  73.5 12.2 %collective-permute-start.14 = (bf16[128,2048]{1,0:T(8,128)(2,1)S(1)}, bf16[128,2048]{1,0:T(8,128)(2,1)S(1)}, u32[]{:S(2)}, u32[]{:S(2)}) collective-permute-start(bf16[128,2048]{1,0:T(8,128)(2,1)S(1)} %combine.3.mine), channel_id=1, source_target_pairs={{0,4},{4,0},{8,12},{12,8},{16,20},{20,16},{24,28},{28,24},{32,36},... | collective-permute-start | bytes 1572872 | tf_op jit(solution)/shard_map/ppermute | solution.py:354
  79.8 6.0 %collective-permute-start.16 = (bf16[128,2048]{1,0:T(8,128)(2,1)S(1)}, bf16[128,2048]{1,0:T(8,128)(2,1)S(1)}, u32[]{:S(2)}, u32[]{:S(2)}) collective-permute-start(bf16[128,2048]{1,0:T(8,128)(2,1)S(1)} %join.1.op), channel_id=1, source_target_pairs={{0,4},{4,0},{8,12},{12,8},{16,20},{20,16},{24,28},{28,24},{32,36},... | collective-permute-start | bytes 1572872 | tf_op jit(solution)/shard_map/ppermute | solution.py:354
  80.8 13.8 %collective-permute-start.18 = (bf16[128,2048]{1,0:T(8,128)(2,1)S(1)}, bf16[128,2048]{1,0:T(8,128)(2,1)S(1)}, u32[]{:S(2)}, u32[]{:S(2)}) collective-permute-start(bf16[128,2048]{1,0:T(8,128)(2,1)S(1)} %join.1.op), channel_id=1, source_target_pairs={{4,8},{8,4},{12,16},{16,12},{20,24},{24,20},{28,32},{32,28},{36,40... | collective-permute-start | bytes 1572872 | tf_op jit(solution)/shard_map/ppermute | solution.py:353
